TPU v7x, 512 devices: a whole 4x4x16 slice. The times are simulated.
512 devices in a mesh: seq: 64 (over y, z), head: 8 (over x, core).
Axes of the slice: x: 4, y: 4, z: 16, core: 2. Of those that a mesh axis runs over, the one named last changes fastest.
Arguments:
- queries: bfloat16 [65536, 2048], P(('seq', 'head')), may hold values from -6 to 6
- keys: bfloat16 [65536, 2048], P(('seq', 'head')), may hold values from -6 to 6
- values: bfloat16 [65536, 2048], P(('seq', 'head')), may hold values from -6 to 6
- cotangent: bfloat16 [65536, 2048], P(('seq', 'head')), may hold values from -6 to 6
- gain: float32 [2048], replicated, may hold values from 0.1 to 1.9
- lengths: int32 [32], replicated, may hold values from 1 to 16384, 65536 in all
Outputs:
- normed: bfloat16 [65536, 2048], P(('seq', 'head'))
- grad_queries: bfloat16 [65536, 2048], P('seq', 'head')
- grad_keys: bfloat16 [65536, 2048], P('seq', 'head')
- grad_values: bfloat16 [65536, 2048], P('seq', 'head')
Inputs may be any that keep to these rules, and one draw needn't show every extreme that they name: The lengths sum to 65536, and the longest is exactly 16384.
All inputs are finite; a program needn't handle non-finite values.
Results may differ from a plain program's by a relative error of at most 0.012.
The roundings to bfloat16 on the way count: a program that leaves them out, or rounds other values in their place, can miss the bound.
Values may be sent and summed in bfloat16 or wider, within the bound.
No kernel may reach another device: no remote copies, remote signals or barrier semaphores. Data moves between devices by JAX's collectives and lax.ppermute only.
A program may use at most 64 MiB of HBM per device.

v0:
```python
import jax
import jax.numpy as jnp
from jax import lax
from jax.sharding import PartitionSpec as P

HEAD_DIM = 128


epsilon = 1e-05


def entering(shard, axis, combine, identity, reverse):
    count, position = (lax.axis_size(axis), lax.axis_index(axis))
    everything = jax.tree.map(lambda part: lax.all_gather(part, axis), shard)
    start = jax.tree.map(
        lambda part, zero: jnp.broadcast_to(jnp.asarray(zero, part.dtype), part.shape),
        shard,
        identity,
    )

    def step(k, before):
        at = count - 1 - k if reverse else k
        reached = at > position if reverse else at < position
        new = combine(before, jax.tree.map(lambda part: part[at], everything))
        return jax.tree.map(lambda a, b: jnp.where(reached, a, b), new, before)

    return lax.fori_loop(0, count, step, start)


def doc_index(positions, starts):
    hits = (positions[:, None] >= starts[None, :]).astype(jnp.int32)
    return jnp.sum(hits, axis=1) - 1


def normalize(field, gain_heads):
    mean_square = jnp.mean(field * field, axis=-1, keepdims=True)
    return field * lax.rsqrt(mean_square + epsilon) * gain_heads


def carry_combine(earlier, later):
    flag = jnp.maximum(earlier[0], later[0])
    state = jnp.where(later[0][0] > 0, later[1], earlier[1] + later[1])
    return (flag, state)


def head_major(field, rows, heads_here):
    return field.reshape(rows, heads_here, HEAD_DIM).transpose(1, 0, 2)


def token_major(field, rows, width):
    return field.transpose(1, 0, 2).reshape(rows, width)


def on_device(queries, keys, values, cotangent, gain, lengths):
    q_part, k_part, v_part = (
        lax.all_to_all(queries, "head", split_axis=1, concat_axis=0, tiled=True),
        lax.all_to_all(keys, "head", split_axis=1, concat_axis=0, tiled=True),
        lax.all_to_all(values, "head", split_axis=1, concat_axis=0, tiled=True),
    )
    rows, width = q_part.shape
    heads_here = width // HEAD_DIM
    q_heads = head_major(q_part, rows, heads_here)
    k_heads = head_major(k_part, rows, heads_here)
    v_heads = head_major(v_part, rows, heads_here)
    gain_heads = lax.dynamic_slice_in_dim(gain, lax.axis_index("head") * width, width).reshape(
        heads_here, 1, HEAD_DIM
    )
    starts = jnp.cumsum(lengths) - lengths
    mine = lax.axis_index("seq")
    first_pos = mine * rows
    places = jnp.arange(rows, dtype=jnp.int32)
    docs = doc_index(first_pos + places, starts)
    edges = doc_index(jnp.stack([first_pos - 1, first_pos + rows]), starts)
    prev_doc = edges[0]
    next_doc = edges[1]
    first_doc = docs[0]
    last_doc = docs[-1]
    mask = (places[:, None] >= places[None, :]) & (docs[:, None] == docs[None, :])
    carried = (docs == prev_doc)[None, :, None]
    later = (docs == next_doc)[None, :, None]
    tail_keys = jnp.where((docs == last_doc)[None, :, None], k_heads, jnp.zeros_like(k_heads))
    tail = jnp.einsum("htd,hte->hde", tail_keys, v_heads, preferred_element_type=jnp.float32)
    forward_flag = (last_doc != prev_doc).astype(jnp.float32).reshape(1)
    identity = (jnp.zeros((1,), jnp.float32), jnp.zeros_like(tail))
    carried_state = entering((forward_flag, tail), "seq", carry_combine, identity, False)[1]
    state_low = carried_state.astype(jnp.bfloat16)
    scores = jnp.einsum("htd,hsd->hts", q_heads, k_heads, preferred_element_type=jnp.float32)
    attn = jnp.where(mask[None], scores, 0.0).astype(jnp.bfloat16)
    intra = jnp.einsum("hts,hse->hte", attn, v_heads, preferred_element_type=jnp.float32)
    inter = jnp.einsum("htd,hde->hte", q_heads, state_low, preferred_element_type=jnp.float32)
    attended = intra + jnp.where(carried, inter, 0.0)
    normed_heads = token_major(normalize(attended, gain_heads).astype(jnp.bfloat16), rows, width)
    normed = lax.all_to_all(normed_heads, "head", split_axis=0, concat_axis=1, tiled=True)
    g_part = lax.all_to_all(cotangent, "head", split_axis=1, concat_axis=0, tiled=True)
    g_heads = head_major(g_part, rows, heads_here).astype(jnp.float32)
    _, pullback = jax.vjp(lambda field: normalize(field, gain_heads), attended)
    grad_att = pullback(g_heads)[0].astype(jnp.bfloat16)
    head_queries = jnp.where((docs == first_doc)[None, :, None], q_heads, jnp.zeros_like(q_heads))
    head_part = jnp.einsum(
        "htd,hte->hde", head_queries, grad_att, preferred_element_type=jnp.float32
    )
    backward_flag = (first_doc != next_doc).astype(jnp.float32).reshape(1)
    back_in = entering((backward_flag, head_part), "seq", carry_combine, identity, True)
    back_low = back_in[1].astype(jnp.bfloat16)
    grad_scores = jnp.einsum("hte,hse->hts", grad_att, v_heads, preferred_element_type=jnp.float32)
    grad_attn = jnp.where(mask[None], grad_scores, 0.0).astype(jnp.bfloat16)
    grad_q = jnp.einsum("hts,hsd->htd", grad_attn, k_heads, preferred_element_type=jnp.float32)
    grad_q = grad_q + jnp.where(
        carried,
        jnp.einsum("hte,hde->htd", grad_att, state_low, preferred_element_type=jnp.float32),
        0.0,
    )
    grad_k = jnp.einsum("hts,htd->hsd", grad_attn, q_heads, preferred_element_type=jnp.float32)
    grad_k = grad_k + jnp.where(
        later,
        jnp.einsum("hse,hde->hsd", v_heads, back_low, preferred_element_type=jnp.float32),
        0.0,
    )
    grad_v = jnp.einsum("hts,hte->hse", attn, grad_att, preferred_element_type=jnp.float32)
    grad_v = grad_v + jnp.where(
        later,
        jnp.einsum("hsd,hde->hse", k_heads, back_low, preferred_element_type=jnp.float32),
        0.0,
    )
    return (
        normed,
        token_major(grad_q.astype(jnp.bfloat16), rows, width),
        token_major(grad_k.astype(jnp.bfloat16), rows, width),
        token_major(grad_v.astype(jnp.bfloat16), rows, width),
    )


def solution(mesh):
    placed = (
        P(("seq", "head"), None),
        P(("seq", "head"), None),
        P(("seq", "head"), None),
        P(("seq", "head"), None),
        P(),
        P(),
    )
    return jax.shard_map(
        on_device,
        mesh=mesh,
        in_specs=placed,
        out_specs=(P(("seq", "head"), None), P("seq", "head"), P("seq", "head"), P("seq", "head")),
        check_vma=False,
    )
```

profile of v0, /device:TPU:1, one launch (start us, length us, event | category | flops | bytes accessed | tf_op | source)
XLA Modules:
  0.0 668.1 jit_solution(10264480717424580470)
XLA Ops:
  7.2 2.0 copy.84
  9.2 10.3 %all-to-all-start.1 = ((bf16[128,8,256]{0,2,1:T(8,128)(2,1)}), bf16[128,8,256]{0,2,1:T(8,128)(2,1)S(1)}, u32[]{:S(2)}, u32[]{:S(2)}) async-start(bf16[128,8,256]{0,2,1:T(8,128)(2,1)} %bitcast.4), calls=%async_computation.1 | async-start | bytes 1048576 | tf_op jit(solution)/shard_map/all_to_all | solution.py:57
  21.2 2.1 copy.87
  23.5 5.5 all-to-all-done.1
  29.0 4.3 all-to-all-start.2
  34.5 2.5 broadcast_compare_fusion
  37.9 4.8 all-to-all-done.2
  45.5 4.3 all-to-all-start
  50.8 8.5 %all-to-all-done = bf16[128,8,256]{0,2,1:T(8,128)(2,1)S(1)} async-done(((bf16[128,8,256]{0,2,1:T(8,128)(2,1)}), bf16[128,8,256]{0,2,1:T(8,128)(2,1)S(1)}, u32[]{:S(2)}, u32[]{:S(2)}) %all-to-all-start) | async-done | bytes 524320 | tf_op jit(solution)/shard_map/all_to_all | solution.py:56
  59.3 4.3 all-to-all-start.4
  68.9 118.6 %all-reduce.2 = (f32[64]{0:T(128)S(1)}, f32[64]{0:T(128)S(1)}) all-reduce(f32[64]{0:T(128)S(1)} %dynamic-update-slice, f32[64]{0:T(128)S(1)} %dynamic-update-slice.1), channel_id=1, replica_groups=mesh['seq'=64,'head'=8] {'seq'}, use_global_device_ids=true, to_apply=%add | all-reduce | flops 128 | bytes 1024
  187.6 1.6 fusion.2
  191.4 4.7 select_convert_fusion.1
  196.1 142.1 %while.30 = (s32[]{:T(128)}, f32[2,128,128]{2,1,0:T(8,128)S(1)}, s32[]{:T(128)}, f32[64,1]{0,1:T(1,128)S(1)}, f32[64,2,128,128]{3,2,1,0:T(8,128)}, /*index=5*/s32[]{:T(128)}, s32[]{:T(128)}) while((s32[]{:T(128)}, f32[2,128,128]{2,1,0:T(8,128)S(1)}, s32[]{:T(128)}, f32[64,1]{0,1:T(1,128)S(1)}, f32[64,2,128,128]{3,2,1,0:T(8,128)}, ...), condition=%wide.region_4.5_spmd.clone, body=%wide.region_3.4_spmd.clone.sunk | while | flops 131077 | bytes 393335 | solution.py:27
  338.5 4.0 fusion.12
  346.0 32.4 %all-to-all-start.3 = ((bf16[8,128,256]{1,2,0:T(8,128)(2,1)}), bf16[8,128,256]{1,2,0:T(8,128)(2,1)S(1)}, u32[]{:S(2)}, u32[]{:S(2)}) async-start(bf16[8,128,256]{1,2,0:T(8,128)(2,1)} %copy.92), calls=%async_computation.3 | async-start | bytes 1048576 | tf_op jit(solution)/shard_map/all_to_all | solution.py:93
  378.4 3.0 select_convert_fusion
  381.4 1.9 copy-done.1
  386.2 1.7 all-to-all-done.3
  388.9 121.2 %all-gather.7.cloned.1.call-done = f32[128,128,128]{2,1,0:T(8,128)} async-done(((f32[2,128,128]{2,1,0:T(8,128)}), f32[128,128,128]{2,1,0:T(8,128)}) %all-gather.7.cloned.1.call-update) | async-done | bytes 8388624 | tf_op jit(solution)/shard_map/all_gather | solution.py:14
  510.1 142.4 %while.31 = (s32[]{:T(128)}, f32[2,128,128]{2,1,0:T(8,128)S(1)}, s32[]{:T(128)}, f32[64,1]{0,1:T(1,128)S(1)}, f32[64,2,128,128]{3,2,1,0:T(8,128)}, /*index=5*/s32[]{:T(128)}, s32[]{:T(128)}, s32[]{:T(128)}, s32[]{:T(128)}) while((s32[]{:T(128)}, f32[2,128,128]{2,1,0:T(8,128)S(1)}, s32[]{:T(128)}, f32[64,1]{0,1:T(1,128)S(1)}, ...), condition=%wide.region_8.9_spmd.clone, body=%wide.region_7.8_spmd.clone.sunk | while | flops 131081 | bytes 393397 | solution.py:27
  519.6 1.6 fusion.62
  653.2 3.0 fusion.9
  657.2 3.0 fusion.10
  (341 shorter events, 302.4 us)
Async XLA Ops:
  7.2 180.3 %copy-start = (f32[2048]{0:T(1024)S(1)}, f32[2048]{0:T(1024)}, u32[]{:S(2)}) copy-start(f32[2048]{0:T(1024)} %param.14) | copy-start | bytes 24580
  9.2 19.8 %all-to-all-start.1 = ((bf16[128,8,256]{0,2,1:T(8,128)(2,1)}), bf16[128,8,256]{0,2,1:T(8,128)(2,1)S(1)}, u32[]{:S(2)}, u32[]{:S(2)}) async-start(bf16[128,8,256]{0,2,1:T(8,128)(2,1)} %bitcast.4), calls=%async_computation.1 | async-start | bytes 1048576 | tf_op jit(solution)/shard_map/all_to_all | solution.py:57
  21.1 23.4 %copy-start.14 = (bf16[128,2048]{1,0:T(8,128)(2,1)S(1)}, bf16[128,2048]{1,0:T(8,128)(2,1)}, u32[]{:S(2)}) copy-start(bf16[128,2048]{1,0:T(8,128)(2,1)} %param.10) | copy-start | bytes 1572868
  29.0 13.8 %all-to-all-start.2 = ((bf16[128,8,256]{0,2,1:T(8,128)(2,1)}), bf16[128,8,256]{0,2,1:T(8,128)(2,1)S(1)}, u32[]{:S(2)}, u32[]{:S(2)}) async-start(bf16[128,8,256]{0,2,1:T(8,128)(2,1)} %bitcast.7), calls=%async_computation.2 | async-start | bytes 1048576 | tf_op jit(solution)/shard_map/all_to_all | solution.py:58
  33.3 162.8 %all-gather.5.cloned.1.call-start = ((), (), s32[]{:S(2)}) async-start(), calls=%async_computation.5 | async-start | bytes 8519680 | tf_op jit(solution)/shard_map/all_gather | solution.py:14
  37.0 12.8 %copy-start.15 = (bf16[128,2048]{1,0:T(8,128)(2,1)S(1)}, bf16[128,2048]{1,0:T(8,128)(2,1)}, u32[]{:S(2)}) copy-start(bf16[128,2048]{1,0:T(8,128)(2,1)} %param.13) | copy-start | bytes 1572868
  37.6 5.2 copy-start.8
  37.9 153.5 %copy-start.10 = (bf16[1024,2,128]{2,0,1:T(8,128)(2,1)}, bf16[1024,2,128]{2,0,1:T(8,128)(2,1)S(1)}, u32[]{:S(2)}) copy-start(bf16[1024,2,128]{2,0,1:T(8,128)(2,1)S(1)} %copy.86) | copy-start | bytes 1572868
  43.4 21.4 %copy-start.2 = (bf16[1024,2,128]{0,2,1:T(8,128)(2,1)}, bf16[1024,2,128]{0,2,1:T(8,128)(2,1)S(1)}, u32[]{:S(2)}) copy-start(bf16[1024,2,128]{0,2,1:T(8,128)(2,1)S(1)} %reshape.167) | copy-start | bytes 1572868
  45.5 13.8 %all-to-all-start = ((bf16[128,8,256]{0,2,1:T(8,128)(2,1)}), bf16[128,8,256]{0,2,1:T(8,128)(2,1)S(1)}, u32[]{:S(2)}, u32[]{:S(2)}) async-start(bf16[128,8,256]{0,2,1:T(8,128)(2,1)} %bitcast.1), calls=%async_computation | async-start | bytes 1048576 | tf_op jit(solution)/shard_map/all_to_all | solution.py:56
  59.3 130.8 %all-to-all-start.4 = ((bf16[128,8,256]{0,2,1:T(8,128)(2,1)}), bf16[128,8,256]{0,2,1:T(8,128)(2,1)S(1)}, u32[]{:S(2)}, u32[]{:S(2)}) async-start(bf16[128,8,256]{0,2,1:T(8,128)(2,1)} %bitcast.25), calls=%async_computation.4 | async-start | bytes 1048576 | tf_op jit(solution)/shard_map/all_to_all | solution.py:94
  63.6 446.6 %all-gather.7.cloned.1.call-start = ((), (), s32[]{:S(2)}) async-start(), calls=%async_computation.6 | async-start | bytes 8519680 | tf_op jit(solution)/shard_map/all_gather | solution.py:14
  189.8 0.8 copy-start.4
  190.1 148.0 %copy-start.12 = (bf16[1024,2,128]{2,0,1:T(8,128)(2,1)}, bf16[1024,2,128]{2,0,1:T(8,128)(2,1)S(1)}, u32[]{:S(2)}) copy-start(bf16[1024,2,128]{2,0,1:T(8,128)(2,1)S(1)} %copy.83) | copy-start | bytes 1572868
  338.5 5.2 copy-start.13
  342.9 0.8 copy-start.6
  342.9 35.5 %copy-start.3 = (bf16[1024,2,128]{0,2,1:T(8,128)(2,1)S(1)}, bf16[1024,2,128]{0,2,1:T(8,128)(2,1)}, u32[]{:S(2)}) copy-start(bf16[1024,2,128]{0,2,1:T(8,128)(2,1)} %copy-done.2) | copy-start | bytes 1572868
  346.0 37.3 %copy-start.9 = (bf16[1024,2,128]{0,2,1:T(8,128)(2,1)S(1)}, bf16[1024,2,128]{0,2,1:T(8,128)(2,1)}, u32[]{:S(2)}) copy-start(bf16[1024,2,128]{0,2,1:T(8,128)(2,1)} %copy-done.8) | copy-start | bytes 1572868
  346.0 41.9 %all-to-all-start.3 = ((bf16[8,128,256]{1,2,0:T(8,128)(2,1)}), bf16[8,128,256]{1,2,0:T(8,128)(2,1)S(1)}, u32[]{:S(2)}, u32[]{:S(2)}) async-start(bf16[8,128,256]{1,2,0:T(8,128)(2,1)} %copy.92), calls=%async_computation.3 | async-start | bytes 1048576 | tf_op jit(solution)/shard_map/all_to_all | solution.py:93
  381.4 1.9 copy-start.1
  383.3 1.6 copy-start.7
  384.9 267.7 %copy-start.11 = (bf16[1024,2,128]{2,0,1:T(8,128)(2,1)S(1)}, bf16[1024,2,128]{2,0,1:T(8,128)(2,1)}, u32[]{:S(2)}) copy-start(bf16[1024,2,128]{2,0,1:T(8,128)(2,1)} %copy-done.10) | copy-start | bytes 1572868
  652.9 4.3 copy-start.5
Sparse Core Ops, SparseCore 0:
  44.6 148.3 all-gather.4
  344.9 165.1 all-gather.6
where the time goes:
time: 679 us; the launch traced here: 668 us
  other arithmetic  287 us (42%)
  waiting for transfers between devices  142 us (21%)
  blocking collectives  119 us (18%)
  starting transfers between devices  55.5 us (8%)
  matrix products  22.7 us (3%)
  local copies, waits for them, and re-layouts  22.2 us (3%)
  between operations  16.9 us (2%)
    select_n x128, other arithmetic, step(): return jax.tree.map(lambda a, b: jnp.where(reached, a, b), new, before)  206 us
    all_gather x2, waiting for transfers between devices, entering(): everything = jax.tree.map(lambda part: lax.all_gather(part, axis), shard)  121 us
    unnamed x1, blocking collectives  119 us
    gt x128, other arithmetic, carry_combine(): state = jnp.where(later[0][0] > 0, later[1], earlier[1] + later[1])  75.3 us
    all_to_all x1, starting transfers between devices, on_device(): lax.all_to_all(normed_heads, 'head', split_axis=0, concat_axis=1, tiled=T...  32.4 us
    unnamed x46, local copies, waits for them, and re-layouts  16.2 us
  transfers between devices with their start and end apart: 7, of which 5 were waited for; matrix products, arithmetic and copies ran while one was open for 4% of the time, Pallas kernels for 0%

commit v1 on v0

v1 whole, which is shorter than its diff:
```python
import functools

import jax
import jax.numpy as jnp
from jax import lax
from jax.experimental import pallas as pl
from jax.experimental.pallas import tpu as pltpu
from jax.sharding import PartitionSpec as P

HEAD_DIM = 128
TILE = 256
SPAN = 4
SPANS = 4
epsilon = 1e-05

F32 = jnp.float32
BF16 = jnp.bfloat16

ROWS = (((0,), (0,)), ((), ()))
FEATURES = (((1,), (1,)), ((), ()))
PLAIN = (((1,), (0,)), ((), ()))


def dot(a, b, dims):
    return lax.dot_general(a, b, dims, preferred_element_type=F32)


def unpacked(packed_ref, at):
    groups, stacked, width = packed_ref.shape
    tokens = stacked // 4
    return packed_ref[:, at * tokens : (at + 1) * tokens, :].reshape(groups * tokens, width)


def head_cols(head):
    return slice(head * HEAD_DIM, (head + 1) * HEAD_DIM)


def meta_kernel(blocks, rows, lengths_ref, where_ref, marks_ref):
    first = where_ref[0] * rows
    last = first + rows - 1

    def clear(i, carry):
        marks_ref[i] = 0
        return carry

    lax.fori_loop(0, 2 * blocks, clear, 0)
    marks_ref[2 * blocks - 1] = 1
    marks_ref[2 * blocks + 1] = 0
    marks_ref[2 * blocks + 3] = rows

    def step(i, begin):
        after = begin + lengths_ref[i]
        marks_ref[begin // rows] = 1
        marks_ref[blocks + jnp.maximum(begin - 1, 0) // rows] = 1

        @pl.when((begin <= first) & (first < after))
        def _():
            marks_ref[2 * blocks] = after - first
            marks_ref[2 * blocks + 1] = jnp.where(begin < first, after - first, 0)

        @pl.when((begin <= last) & (last < after))
        def _():
            marks_ref[2 * blocks + 2] = begin - first
            marks_ref[2 * blocks + 3] = jnp.where(after > last + 1, begin - first, rows)

        return after

    lax.fori_loop(0, lengths_ref.shape[0], step, jnp.int32(0))


def docs_kernel(lengths_ref, where_ref, span_ref):
    rows = span_ref.shape[1]
    first = where_ref[0] * rows
    place = first + lax.broadcasted_iota(jnp.int32, (1, rows), 1)

    def step(i, carry):
        begin, start, end = carry
        after = begin + lengths_ref[i]
        inside = (place >= begin) & (place < after)
        return (after, jnp.where(inside, begin, start), jnp.where(inside, after, end))

    zero = jnp.zeros((1, rows), jnp.int32)
    _, start, end = lax.fori_loop(0, lengths_ref.shape[0], step, (jnp.int32(0), zero, zero))
    span_ref[0:1, :] = start - first
    span_ref[1:2, :] = end - first


def pack_kernel(*refs):
    *arrays, ended_ref, out_ref, held, in_sems, out_sems = refs
    ended_ref[...] = jnp.zeros_like(ended_ref)
    groups, _, width = out_ref.shape
    tokens = arrays[0].shape[0]
    inward = [
        pltpu.make_async_copy(ref, held.at[k], in_sems.at[k]) for k, ref in enumerate(arrays)
    ]
    outward = [
        [
            pltpu.make_async_copy(
                held.at[k, :, pl.ds(at * width, width)],
                out_ref.at[at, pl.ds(k * tokens, tokens), :],
                out_sems.at[k, at],
            )
            for at in range(groups)
        ]
        for k in range(len(arrays))
    ]
    for copy in inward:
        copy.start()
    for copy, parts in zip(inward, outward):
        copy.wait()
        for part in parts:
            part.start()
    for parts in outward:
        for part in parts:
            part.wait()


def parts_kernel(lengths_ref, where_ref, keys_ref, values_ref, ended_ref, out_ref, held, sems):
    copies = [
        pltpu.make_async_copy(ref, held.at[k], sems.at[k])
        for k, ref in enumerate((keys_ref, values_ref))
    ]
    for copy in copies:
        copy.start()
    ended_ref[...] = jnp.zeros_like(ended_ref)
    groups, width, _ = out_ref.shape
    tokens, cols = keys_ref.shape
    last = (where_ref[0] + 1) * (tokens * groups) - 1
    begin, bound = jnp.int32(0), jnp.int32(0)
    for i in range(lengths_ref.shape[0]):
        bound = jnp.where(begin <= last, begin, bound)
        begin = begin + lengths_ref[i]
    mine = last + 1 - (groups - where_ref[1]) * tokens
    for copy in copies:
        copy.wait()
    place = mine + lax.broadcasted_iota(jnp.int32, (tokens, cols), 0)
    keys = held[0]
    keys = jnp.where(place >= bound, keys, jnp.zeros_like(keys))
    for head in range(cols // HEAD_DIM):
        part = dot(keys[:, head_cols(head)], held[1, :, head_cols(head)], ROWS)
        group, at = divmod(head * HEAD_DIM, width)
        out_ref[group, at : at + HEAD_DIM, :] = part.astype(out_ref.dtype)


def tail_kernel(marks_ref, parts_ref, tail_ref):
    total = parts_ref[0].astype(F32)
    for k in range(1, parts_ref.shape[0]):
        total = total + parts_ref[k].astype(F32)
    tail_ref[...] = total.astype(tail_ref.dtype)


def scan_kernel(reverse, marks_ref, parts_ref, low_ref):
    blocks = parts_ref.shape[0]
    total = jnp.zeros(parts_ref.shape[1:], F32)
    for k in range(blocks):
        at = blocks - 1 - k if reverse else k
        low_ref[at] = total.astype(low_ref.dtype)
        part = parts_ref[at].astype(F32)
        mark = marks_ref[at + (blocks if reverse else 0)]
        total = jnp.where(mark > 0, part, total + part)


def block_mark(marks_ref, blocks, at, reverse):
    return marks_ref[lax.rem(at + blocks, blocks) + (blocks if reverse else 0)]


def span_kernel(reverse, blocks, where_ref, marks_ref, *refs):
    span_ref = refs[-1]
    mine, sign = where_ref[0], -1 if reverse else 1
    total = refs[0][...].astype(F32)
    for k, ref in enumerate(refs[1:-1]):
        mark = block_mark(marks_ref, blocks, mine + sign * (k - 1), reverse)
        total = jnp.where(mark > 0, 0.0, total) + ref[...].astype(F32)
    span_ref[...] = total.astype(span_ref.dtype)


def entering(reverse, blocks, where_ref, marks_ref, span_refs):
    mine, sign = where_ref[0], -1 if reverse else 1
    total = span_refs[0][...].astype(F32)
    for k, ref in enumerate(span_refs[1:]):
        first = SPAN * (SPANS - 1 - k)
        mark = jnp.int32(0)
        for back in range(first - SPAN + 1, first + 1):
            mark = jnp.maximum(mark, block_mark(marks_ref, blocks, mine - sign * back, reverse))
        total = jnp.where(mark > 0, 0.0, total) + ref[...].astype(F32)
    return total.astype(BF16)


def intra_kernel(span_ref, packed_ref, intra_ref):
    keys, values, queries = (unpacked(packed_ref, at) for at in range(3))
    rows, width = keys.shape
    for low in range(0, rows, TILE):
        high = low + TILE
        row = low + lax.broadcasted_iota(jnp.int32, (TILE, high), 0)
        column = lax.broadcasted_iota(jnp.int32, (TILE, high), 1)
        mask = (column <= row) & (row < span_ref[1:2, :high])
        for head in range(width // HEAD_DIM):
            cols = head_cols(head)
            scores = dot(queries[low:high, cols], keys[:high, cols], FEATURES)
            attn = jnp.where(mask, scores, 0.0).astype(BF16)
            intra_ref[low:high, cols] = dot(attn, values[:high, cols], PLAIN)


def norm_kernel(blocks, where_ref, marks_ref, packed_ref, intra_ref, gain_ref, *refs):
    span_refs, (normed_ref, grad_ref, part_ref, state_ref) = refs[:SPANS], refs[SPANS:]
    queries, cotangent = unpacked(packed_ref, 2), unpacked(packed_ref, 3)
    state = entering(False, blocks, where_ref, marks_ref, span_refs)
    state_ref[...] = state
    rows, width = intra_ref.shape
    place = lax.broadcasted_iota(jnp.int32, (rows, HEAD_DIM), 0)
    in_first = place < marks_ref[2 * blocks]
    carried = place < marks_ref[2 * blocks + 1]
    for head in range(width // HEAD_DIM):
        cols = head_cols(head)
        q = queries[:, cols]
        inter = dot(q, state[cols, :], PLAIN)
        attended = intra_ref[:, cols] + jnp.where(carried, inter, 0.0)
        at = pl.multiple_of(where_ref[1] * width + head * HEAD_DIM, HEAD_DIM)
        gain = gain_ref[:, pl.ds(at, HEAD_DIM)]
        scale = lax.rsqrt(jnp.mean(attended * attended, axis=-1, keepdims=True) + epsilon)
        unit = attended * scale
        normed_ref[:, cols] = (unit * gain).astype(BF16)
        pulled = cotangent[:, cols].astype(F32) * gain
        along = jnp.mean(pulled * unit, axis=-1, keepdims=True)
        grad = (scale * (pulled - unit * along)).astype(BF16)
        grad_ref[:, cols] = grad
        kept = jnp.where(in_first, q, jnp.zeros_like(q))
        part_ref[cols, :] = dot(kept, grad, ROWS).astype(part_ref.dtype)


def grad_q_kernel(blocks, marks_ref, span_ref, packed_ref, grad_ref, state_ref, ended_ref, grad_q_ref):
    ended_ref[...] = jnp.zeros_like(ended_ref)
    keys, values = unpacked(packed_ref, 0), unpacked(packed_ref, 1)
    rows, width = keys.shape
    for low in range(0, rows, TILE):
        high = low + TILE
        row = low + lax.broadcasted_iota(jnp.int32, (TILE, high), 0)
        column = lax.broadcasted_iota(jnp.int32, (TILE, high), 1)
        mask = (column <= row) & (row < span_ref[1:2, :high])
        place = low + lax.broadcasted_iota(jnp.int32, (TILE, HEAD_DIM), 0)
        carried = place < marks_ref[2 * blocks + 1]
        for head in range(width // HEAD_DIM):
            cols = head_cols(head)
            grad = grad_ref[low:high, cols]
            scores = dot(grad, values[:high, cols], FEATURES)
            grad_attn = jnp.where(mask, scores, 0.0).astype(BF16)
            inter = dot(grad, state_ref[cols, :], FEATURES)
            grad_q = dot(grad_attn, keys[:high, cols], PLAIN) + jnp.where(carried, inter, 0.0)
            grad_q_ref[low:high, cols] = grad_q.astype(BF16)


def grad_kv_kernel(span_ref, packed_ref, grad_ref, part_k_ref, part_v_ref):
    keys, values, queries = (unpacked(packed_ref, at) for at in range(3))
    rows, width = keys.shape
    for low in range(0, rows, TILE):
        high = low + TILE
        row = low + lax.broadcasted_iota(jnp.int32, (TILE, rows - low), 0)
        column = low + lax.broadcasted_iota(jnp.int32, (TILE, rows - low), 1)
        mask = (row <= column) & (row >= span_ref[0:1, low:])
        for head in range(width // HEAD_DIM):
            cols = head_cols(head)
            q, k, v = (field[:, cols] for field in (queries, keys, values))
            grad = grad_ref[:, cols]
            turned = dot(v[low:high], grad[low:], FEATURES)
            turned = jnp.where(mask, turned, 0.0).astype(BF16)
            part_k_ref[low:high, cols] = dot(turned, q[low:], PLAIN)
            turned = dot(k[low:high], q[low:], FEATURES)
            turned = jnp.where(mask, turned, 0.0).astype(BF16)
            part_v_ref[low:high, cols] = dot(turned, grad[low:], PLAIN)


def last_kernel(blocks, marks_ref, packed_ref, part_k_ref, part_v_ref, back_ref, grad_k_ref, grad_v_ref):
    keys, values = unpacked(packed_ref, 0), unpacked(packed_ref, 1)
    rows, width = keys.shape
    place = lax.broadcasted_iota(jnp.int32, (rows, HEAD_DIM), 0)
    later = place >= marks_ref[2 * blocks + 3]
    for head in range(width // HEAD_DIM):
        cols = head_cols(head)
        inter = dot(values[:, cols], back_ref[cols, :], FEATURES)
        grad_k_ref[:, cols] = (part_k_ref[:, cols] + jnp.where(later, inter, 0.0)).astype(BF16)
        inter = dot(keys[:, cols], back_ref[cols, :], PLAIN)
        grad_v_ref[:, cols] = (part_v_ref[:, cols] + jnp.where(later, inter, 0.0)).astype(BF16)


SMEM = pl.BlockSpec(memory_space=pltpu.SMEM)
VMEM = pl.BlockSpec(memory_space=pltpu.VMEM)
ANYWHERE = pl.BlockSpec(memory_space=pl.ANY)
ENDED = jax.ShapeDtypeStruct((8, HEAD_DIM), F32)


def call(
    kernel, name, outs, scalars, arrays, flops, scratch=(), after=(), in_specs=None, out_specs=None, limit=40, aliases=None
):
    moved = sum(a.size * a.dtype.itemsize for a in (*arrays, *outs))
    given = len(scalars) + len(arrays)

    def body(*refs):
        kernel(*refs[:given], *refs[given + len(after) :])

    return pl.pallas_call(
        body,
        name=name,
        out_shape=outs,
        in_specs=[SMEM] * len(scalars) + (in_specs or [VMEM] * len(arrays)) + [ANYWHERE] * len(after),
        out_specs=out_specs or [VMEM] * len(outs),
        scratch_shapes=list(scratch),
        input_output_aliases=aliases or {},
        compiler_params=pltpu.CompilerParams(vmem_limit_bytes=limit * 1024 * 1024),
        cost_estimate=pl.CostEstimate(flops=flops, bytes_accessed=moved, transcendentals=0),
    )(*scalars, *arrays, *after)


def across_head(parts):
    return lax.all_to_all(parts, "head", split_axis=0, concat_axis=0, tiled=True)


def to_heads(arrays, after):
    groups, count = lax.axis_size("head"), len(arrays)
    tokens, cols = arrays[0].shape
    ended, packed = call(
        pack_kernel,
        "pack",
        [ENDED, jax.ShapeDtypeStruct((groups, count * tokens, cols // groups), BF16)],
        [],
        arrays,
        0,
        [
            pltpu.VMEM((count, tokens, cols), BF16),
            pltpu.SemaphoreType.DMA((count,)),
            pltpu.SemaphoreType.DMA((count, groups)),
        ],
        after,
        [ANYWHERE] * count,
        [VMEM, ANYWHERE],
        60,
    )
    return ended, across_head(packed)


def from_block(field, step):
    blocks = lax.axis_size("seq")
    return lax.ppermute(field, "seq", [(at, (at + step) % blocks) for at in range(blocks)])


def spans_before(part, where, marks, reverse):
    sign = -1 if reverse else 1
    parts = [from_block(part, sign * 2), from_block(part, sign), part, from_block(part, -sign)]
    (span,) = call(
        functools.partial(span_kernel, reverse, lax.axis_size("seq")),
        "span_back" if reverse else "span_forward",
        [jax.ShapeDtypeStruct(part.shape, BF16)],
        [where, marks],
        parts,
        SPAN * part.size,
    )
    spans = {k: from_block(span, sign * (2 + SPAN * k)) for k in (2, 1, 3, 0)}
    return [spans[k] for k in reversed(range(SPANS))], parts[0]


def carried_over(part, marks, reverse, beside):
    blocks = lax.axis_size("seq")
    height, width = part.shape
    first = beside[0]([part])
    sent = part.reshape(blocks, height // blocks, width)
    got = lax.all_to_all(sent, "seq", split_axis=0, concat_axis=0, tiled=True)
    (low,) = call(
        functools.partial(scan_kernel, reverse),
        "scan_back" if reverse else "scan_forward",
        [jax.ShapeDtypeStruct(got.shape, BF16)],
        [marks],
        [got],
        got.size,
        after=first[:1],
    )
    second = beside[1]([low], first)
    mine = lax.all_to_all(low, "seq", split_axis=0, concat_axis=0, tiled=True)
    return mine.reshape(height, width), first, second


def on_device(queries, keys, values, cotangent, gain, lengths):
    groups, blocks = lax.axis_size("head"), lax.axis_size("seq")
    tokens, cols = queries.shape
    rows, width = tokens * groups, cols // groups
    square = rows * rows * width
    here = lax.axis_index("head").astype(jnp.int32)
    where = jnp.stack([lax.axis_index("seq").astype(jnp.int32), here])
    f32 = functools.partial(jax.ShapeDtypeStruct, dtype=F32)
    bf16 = functools.partial(jax.ShapeDtypeStruct, dtype=BF16)
    int32 = functools.partial(jax.ShapeDtypeStruct, dtype=jnp.int32)
    started, parts = call(
        parts_kernel,
        "parts",
        [ENDED, bf16((groups, width, HEAD_DIM))],
        [lengths, where],
        [keys, values],
        2 * tokens * cols * HEAD_DIM,
        [pltpu.VMEM((2, tokens, cols), BF16), pltpu.SemaphoreType.DMA((2,))],
        in_specs=[ANYWHERE] * 2,
        limit=60,
    )
    (marks,) = call(
        functools.partial(meta_kernel, blocks, rows),
        "meta",
        [int32((2 * blocks + 4,))],
        [lengths, where],
        [],
        rows,
        after=[started],
        out_specs=[SMEM],
    )
    (span,) = call(docs_kernel, "docs", [int32((2, rows))], [lengths, where], [], rows, after=[started])
    gathered = across_head(parts)
    ended, packed = to_heads([keys, values, queries, cotangent], [started])
    (tail,) = call(
        tail_kernel,
        "tail",
        [bf16((width, HEAD_DIM))],
        [marks],
        [gathered],
        gathered.size,
        after=[ended, span],
    )
    before, _ = spans_before(tail, where, marks, False)
    (inside,) = call(intra_kernel, "intra", [f32((rows, width))], [], [span, packed], 2 * square)
    normed, grad, part, state = call(
        functools.partial(norm_kernel, blocks),
        "norm",
        [bf16((rows, width)), bf16((rows, width)), bf16((width, HEAD_DIM)), bf16((width, HEAD_DIM))],
        [where, marks],
        [packed, inside, gain.reshape(1, cols), *before],
        4 * rows * width * HEAD_DIM,
    )

    def grads_q(after):
        return call(
            functools.partial(grad_q_kernel, blocks),
            "grads_q",
            [ENDED, bf16((rows, width))],
            [marks],
            [span, packed, grad, state],
            2 * square,
            after=after,
        )

    def grads_kv(after, _):
        return call(
            grad_kv_kernel,
            "grads_kv",
            [f32((rows, width)), f32((rows, width))],
            [],
            [span, packed, grad],
            4 * square,
            after=after,
        )

    back, (_, grad_q), (part_k, part_v) = carried_over(part, marks, True, (grads_q, grads_kv))
    (normed,) = call(
        lambda *refs: None,
        "normed",
        [bf16((rows, width))],
        [],
        [normed],
        0,
        after=[back],
        in_specs=[ANYWHERE],
        out_specs=[ANYWHERE],
        aliases={0: 0},
    )
    normed = across_head(normed.reshape(groups, tokens, width))
    grad_k, grad_v = call(
        functools.partial(last_kernel, blocks),
        "last",
        [bf16((rows, width)), bf16((rows, width))],
        [marks],
        [packed, part_k, part_v, back],
        4 * rows * width * HEAD_DIM,
    )
    return normed.transpose(1, 0, 2).reshape(tokens, cols), grad_q, grad_k, grad_v


def solution(mesh):
    placed = P(("seq", "head"), None)
    return jax.shard_map(
        on_device,
        mesh=mesh,
        in_specs=(placed, placed, placed, placed, P(), P()),
        out_specs=(placed, P("seq", "head"), P("seq", "head"), P("seq", "head")),
        check_vma=False,
    )
```

time: 679 us -> 144 us (0.21); the launches traced: 668 us -> 143 us
  other arithmetic: 287 us -> 0.59 us
  waiting for transfers between devices: 142 us -> 32.9 us
  blocking collectives: 119 us -> 17.8 us
  Pallas kernels: 0 us -> 24.6 us
  matrix products: 22.7 us -> 0 us
  local copies, waits for them, and re-layouts: 22.2 us -> 0.87 us
  between operations: 16.9 us -> 0.83 us
  starting transfers between devices: 55.5 us -> 65.5 us
    select_n x128 -> x0, other arithmetic: 206 us -> none  [step(): return jax.tree.map(lambda a, b: jnp.where(reached, a, b), new, before)]
    all_gather x2 -> x0, waiting for transfers between devices: 121 us -> none  [entering(): everything = jax.tree.map(lambda part: lax.all_gather(part, axis), shard)]
    unnamed x1 -> x0, blocking collectives: 119 us -> none
    gt x128 -> x0, other arithmetic: 75.3 us -> none  [carry_combine(): state = jnp.where(later[0][0] > 0, later[1], earlier[1] + later[1])]
    ppermute x0 -> x7, starting transfers between devices: none -> 29.6 us  [from_block(): lax.ppermute(field, 'seq', [(at, (at + step) % blocks) for at in range(bl...]
    pallas_call x0 -> x13, Pallas kernels: none -> 24.6 us  [call(): pl.pallas_call(body, name=name, out_shape=outs, in_specs=[SMEM] * len(sca...]
    dot_general x12 -> x0, matrix products: 22.7 us -> none  [the longest x1 4.68 us: on_device(): jnp.einsum('htd,hsd->hts', q_heads, k_heads, preferred_element_type=jnp.f...]
    all_to_all x5 -> x4, starting transfers between devices: 55.5 us -> 35.9 us  [the longest x3 23.8 us: across_head(): lax.all_to_all(parts, 'head', split_axis=0, concat_axis=0, tiled=True)]
  transfers between devices with their start and end apart: 7 -> 11, of which waited for: 5 -> 7; matrix products, arithmetic and copies ran while one was open for 4% -> 0% of each run, Pallas kernels for 0% -> 13%
where the time goes in v1:
time: 144 us; the launch traced here: 143 us
  starting transfers between devices  65.5 us (45%)
  waiting for transfers between devices  32.9 us (23%)
  Pallas kernels  24.6 us (17%)
  blocking collectives  17.8 us (12%)
    ppermute x7, starting transfers between devices, from_block(): lax.ppermute(field, 'seq', [(at, (at + step) % blocks) for at in range(bl...  29.6 us
    pallas_call x13, Pallas kernels, call(): pl.pallas_call(body, name=name, out_shape=outs, in_specs=[SMEM] * len(sca...  24.6 us
    all_to_all x3, starting transfers between devices, across_head(): lax.all_to_all(parts, 'head', split_axis=0, concat_axis=0, tiled=True)  23.8 us
    all_to_all x1, blocking collectives, carried_over(): mine = lax.all_to_all(low, 'seq', split_axis=0, concat_axis=0, tiled=True)  17.8 us
    ppermute x7, waiting for transfers between devices, from_block(): lax.ppermute(field, 'seq', [(at, (at + step) % blocks) for at in range(bl...  12.2 us
    all_to_all x1, starting transfers between devices, carried_over(): got = lax.all_to_all(sent, 'seq', split_axis=0, concat_axis=0, tiled=True)  12.1 us
    all_to_all x3, waiting for transfers between devices, across_head(): lax.all_to_all(parts, 'head', split_axis=0, concat_axis=0, tiled=True)  10.3 us
    all_to_all x1, waiting for transfers between devices, carried_over(): got = lax.all_to_all(sent, 'seq', split_axis=0, concat_axis=0, tiled=True)  10.3 us
  transfers between devices with their start and end apart: 11, of which 7 were waited for; matrix products, arithmetic and copies ran while one was open for 0% of the time, Pallas kernels for 13%

profile of v1, /device:TPU:1, one launch (start us, length us, event | category | flops | bytes accessed | tf_op | source)
XLA Modules:
  0.0 143.0 jit_solution(8654265251564204103)
XLA Ops:
  1.2 3.0 %parts.1 = (f32[8,128]{1,0:T(8,128)}, bf16[8,256,128]{2,1,0:T(8,128)(2,1)}) custom-call(s32[32]{0:T(128)} %refs_0_.7, s32[2]{0:T(128)} %pad_add_fusion.refs_1_.refs_0_, bf16[128,2048]{1,0:T(8,128)(2,1)} %refs_0_.6, bf16[128,2048]{1,0:T(8,128)(2,1)} %refs_1_.1), custom_call_target="tpu_custom_call" | custom-call | flops 67108864 | bytes 1576960 | tf_op jit(solution)/shard_map/parts/pallas_call | solution.py:300
  4.3 10.3 %all-to-all-start.1 = ((bf16[8,256,128]{2,1,0:T(8,128)(2,1)}), bf16[8,256,128]{2,1,0:T(8,128)(2,1)S(1)}, u32[]{:S(2)}, u32[]{:S(2)}) async-start(bf16[8,256,128]{2,1,0:T(8,128)(2,1)} %get-tuple-element.20), calls=%async_computation.1 | async-start | bytes 1048576 | tf_op jit(solution)/shard_map/all_to_all | solution.py:314
  14.5 3.3 %pack.1 = (f32[8,128]{1,0:T(8,128)}, bf16[8,512,256]{2,1,0:T(8,128)(2,1)}) custom-call(bf16[128,2048]{1,0:T(8,128)(2,1)} %refs_0_.6, bf16[128,2048]{1,0:T(8,128)(2,1)} %refs_1_.1, bf16[128,2048]{1,0:T(8,128)(2,1)} %refs_2_.3, bf16[128,2048]{1,0:T(8,128)(2,1)} %refs_3_.3, f32[8,128]{1,0:T(8,128)} %get-tuple-element.18.refs_2_.refs_4_), custom_call_target="tpu_custom_call" | custom-call | bytes 4198400 | tf_op jit(solution)/shard_map/pack/pallas_call | solution.py:300
  17.8 6.2 %all-to-all-done.1.refs_1_ = bf16[8,256,128]{2,1,0:T(8,128)(2,1)S(1)} async-done(((bf16[8,256,128]{2,1,0:T(8,128)(2,1)}), bf16[8,256,128]{2,1,0:T(8,128)(2,1)S(1)}, u32[]{:S(2)}, u32[]{:S(2)}) %all-to-all-start.1) | async-done | bytes 524320 | tf_op jit(solution)/shard_map/all_to_all | solution.py:314
  24.1 4.5 %all-to-all-start = ((bf16[8,512,256]{2,1,0:T(8,128)(2,1)}), bf16[8,512,256]{2,1,0:T(8,128)(2,1)S(1)}, u32[]{:S(2)}, u32[]{:S(2)}) async-start(bf16[8,512,256]{2,1,0:T(8,128)(2,1)} %get-tuple-element.19), calls=%async_computation | async-start | bytes 4194304 | tf_op jit(solution)/shard_map/all_to_all | solution.py:314
  28.6 2.5 %meta.1.refs_0_.refs_1_ = s32[132]{0:T(256)S(1)} custom-call(s32[32]{0:T(128)S(1)} %copy-done.3, s32[2]{0:T(128)S(1)} %copy-done.1, f32[8,128]{1,0:T(8,128)S(1)} %copy-done), custom_call_target="tpu_custom_call" | custom-call | flops 1024 | bytes 528 | tf_op jit(solution)/shard_map/meta/pallas_call | solution.py:300
  32.7 9.1 %collective-permute-start.2 = (bf16[256,128]{1,0:T(8,128)(2,1)S(1)}, bf16[256,128]{1,0:T(8,128)(2,1)S(1)}, u32[]{:S(2)}, u32[]{:S(2)}) collective-permute-start(bf16[256,128]{1,0:T(8,128)(2,1)S(1)} %tail.1.refs_4_), channel_id=1, source_target_pairs={{0,504},{8,0},{16,8},{24,16},{32,24},{40,32},{48,40},{56,48},{64,5... | collective-permute-start | bytes 196616 | tf_op jit(solution)/shard_map/ppermute | solution.py:342
  41.8 1.9 %collective-permute-start.1 = (bf16[256,128]{1,0:T(8,128)(2,1)S(1)}, bf16[256,128]{1,0:T(8,128)(2,1)S(1)}, u32[]{:S(2)}, u32[]{:S(2)}) collective-permute-start(bf16[256,128]{1,0:T(8,128)(2,1)S(1)} %tail.1.refs_4_), channel_id=1, source_target_pairs={{0,8},{8,16},{16,24},{24,32},{32,40},{40,48},{48,56},{56,64},{64,7... | collective-permute-start | bytes 196616 | tf_op jit(solution)/shard_map/ppermute | solution.py:342
  45.7 4.5 %collective-permute-done.1.refs_3_ = bf16[256,128]{1,0:T(8,128)(2,1)S(1)} collective-permute-done((bf16[256,128]{1,0:T(8,128)(2,1)S(1)}, bf16[256,128]{1,0:T(8,128)(2,1)S(1)}, u32[]{:S(2)}, u32[]{:S(2)}) %collective-permute-start.1) | collective-permute-done | bytes 65568 | tf_op jit(solution)/shard_map/ppermute | solution.py:342
  50.1 2.9 %collective-permute-done.refs_2_ = bf16[256,128]{1,0:T(8,128)(2,1)S(1)} collective-permute-done((bf16[256,128]{1,0:T(8,128)(2,1)S(1)}, bf16[256,128]{1,0:T(8,128)(2,1)S(1)}, u32[]{:S(2)}, u32[]{:S(2)}) %collective-permute-start) | collective-permute-done | bytes 65568 | tf_op jit(solution)/shard_map/ppermute | solution.py:342
  55.6 5.2 %collective-permute-start.5 = (bf16[256,128]{1,0:T(8,128)(2,1)S(1)}, bf16[256,128]{1,0:T(8,128)(2,1)S(1)}, u32[]{:S(2)}, u32[]{:S(2)}) collective-permute-start(bf16[256,128]{1,0:T(8,128)(2,1)S(1)} %span_forward.1), channel_id=1, source_target_pairs={{0,48},{8,56},{16,64},{24,72},{32,80},{40,88},{48,96},{56,104},{64... | collective-permute-start | bytes 196616 | tf_op jit(solution)/shard_map/ppermute | solution.py:342
  60.8 4.2 %collective-permute-start.4 = (bf16[256,128]{1,0:T(8,128)(2,1)S(1)}, bf16[256,128]{1,0:T(8,128)(2,1)S(1)}, u32[]{:S(2)}, u32[]{:S(2)}) collective-permute-start(bf16[256,128]{1,0:T(8,128)(2,1)S(1)} %span_forward.1), channel_id=1, source_target_pairs={{0,80},{8,88},{16,96},{24,104},{32,112},{40,120},{48,128},{56,136}... | collective-permute-start | bytes 196616 | tf_op jit(solution)/shard_map/ppermute | solution.py:342
  65.0 5.3 %collective-permute-start.3 = (bf16[256,128]{1,0:T(8,128)(2,1)S(1)}, bf16[256,128]{1,0:T(8,128)(2,1)S(1)}, u32[]{:S(2)}, u32[]{:S(2)}) collective-permute-start(bf16[256,128]{1,0:T(8,128)(2,1)S(1)} %span_forward.1), channel_id=1, source_target_pairs={{0,112},{8,120},{16,128},{24,136},{32,144},{40,152},{48,160},{56,1... | collective-permute-start | bytes 196616 | tf_op jit(solution)/shard_map/ppermute | solution.py:342
  72.2 2.7 %collective-permute-done.4.refs_6_ = bf16[256,128]{1,0:T(8,128)(2,1)S(1)} collective-permute-done((bf16[256,128]{1,0:T(8,128)(2,1)S(1)}, bf16[256,128]{1,0:T(8,128)(2,1)S(1)}, u32[]{:S(2)}, u32[]{:S(2)}) %collective-permute-start.4) | collective-permute-done | bytes 65568 | tf_op jit(solution)/shard_map/ppermute | solution.py:342
  75.0 2.1 %collective-permute-done.3.refs_5_ = bf16[256,128]{1,0:T(8,128)(2,1)S(1)} collective-permute-done((bf16[256,128]{1,0:T(8,128)(2,1)S(1)}, bf16[256,128]{1,0:T(8,128)(2,1)S(1)}, u32[]{:S(2)}, u32[]{:S(2)}) %collective-permute-start.3) | collective-permute-done | bytes 65568 | tf_op jit(solution)/shard_map/ppermute | solution.py:342
  77.1 2.5 %norm.1 = (bf16[1024,256]{1,0:T(8,128)(2,1)}, bf16[1024,256]{1,0:T(8,128)(2,1)S(1)}, bf16[256,128]{1,0:T(8,128)(2,1)}, bf16[256,128]{1,0:T(8,128)(2,1)S(1)}) custom-call(s32[2]{0:T(128)S(1)} %copy-done.1, s32[132]{0:T(256)S(1)} %meta.1.refs_0_.refs_1_, bf16[8,512,256]{2,1,0:T(8,128)(2,1)S(1)} %all-to-all-done.refs_1_.refs_2_, f32[1024,256]{1,0:T(8,128)S(1)} %intra.1.refs_3_, ...), custom_call_target="tpu_custom_call" | custom-call | flops 134217728 | bytes 4595712 | tf_op jit(solution)/shard_map/norm/pallas_call | solution.py:300
  79.6 12.1 %all-to-all-start.2 = ((bf16[64,4,128]{2,1,0:T(4,128)(2,1)}), bf16[64,4,128]{2,1,0:T(4,128)(2,1)S(1)}, u32[]{:S(2)}, u32[]{:S(2)}) async-start(bf16[64,4,128]{2,1,0:T(4,128)(2,1)} %bitcast.3), calls=%async_computation.2 | async-start | bytes 131072 | tf_op jit(solution)/shard_map/all_to_all | solution.py:365
  91.7 3.2 %grads_q.1 = (f32[8,128]{1,0:T(8,128)S(1)}, bf16[1024,256]{1,0:T(8,128)(2,1)}) custom-call(s32[132]{0:T(256)S(1)} %meta.1.refs_0_.refs_1_, s32[2,1024]{1,0:T(2,128)S(1)} %docs.1.refs_0_.refs_3_.refs_1_, bf16[8,512,256]{2,1,0:T(8,128)(2,1)S(1)} %all-to-all-done.refs_1_.refs_2_, bf16[1024,256]{1,0:T(8,128)(2,1)S(1)} %get-tuple-element.24.refs_3_.refs_2_, ...), custom_call_target="tpu_custom_call" | custom-call | flops 536870912 | bytes 3223552 | tf_op jit(solution)/shard_map/grads_q/pallas_call | solution.py:300
  94.9 10.3 %all-to-all-done.2.refs_1_ = bf16[64,4,128]{2,1,0:T(4,128)(2,1)S(1)} async-done(((bf16[64,4,128]{2,1,0:T(4,128)(2,1)}), bf16[64,4,128]{2,1,0:T(4,128)(2,1)S(1)}, u32[]{:S(2)}, u32[]{:S(2)}) %all-to-all-start.2) | async-done | bytes 65568 | tf_op jit(solution)/shard_map/all_to_all | solution.py:365
  105.9 17.8 %all_to_all.25 = bf16[64,4,128]{2,1,0:T(4,128)(2,1)S(1)} all-to-all(bf16[64,4,128]{2,1,0:T(4,128)(2,1)S(1)} %scan_back.1.refs_3_), channel_id=1, replica_groups=mesh['seq'=64,'head'=8] {'seq'}, dimensions={0} | all-to-all | bytes 131072 | tf_op jit(solution)/shard_map/all_to_all | solution.py:376
  123.7 9.0 %all-to-all-start.4 = ((bf16[8,128,256]{2,1,0:T(8,128)(2,1)}), bf16[8,128,256]{2,1,0:T(8,128)(2,1)S(1)}, u32[]{:S(2)}, u32[]{:S(2)}) async-start(bf16[8,128,256]{2,1,0:T(8,128)(2,1)} %bitcast.5), calls=%async_computation.4 | async-start | bytes 1048576 | tf_op jit(solution)/shard_map/all_to_all | solution.py:314
  132.7 3.3 %grads_kv.1 = (f32[1024,256]{1,0:T(8,128)S(1)}, f32[1024,256]{1,0:T(8,128)S(1)}) custom-call(s32[2,1024]{1,0:T(2,128)S(1)} %docs.1.refs_0_.refs_3_.refs_1_, bf16[8,512,256]{2,1,0:T(8,128)(2,1)S(1)} %all-to-all-done.refs_1_.refs_2_, bf16[1024,256]{1,0:T(8,128)(2,1)S(1)} %get-tuple-element.24.refs_3_.refs_2_, bf16[64,4,128]{2,1,0:T(4,128)(2,1)S(1)} %scan_back.1.refs_3_), custom_call_target="tpu_custom_call" | custom-call | flops 1073741824 | bytes 4726784 | tf_op jit(solution)/shard_map/grads_kv/pallas_call | solution.py:300
  136.0 2.0 %last.1 = (bf16[1024,256]{1,0:T(8,128)(2,1)}, bf16[1024,256]{1,0:T(8,128)(2,1)}) custom-call(s32[132]{0:T(256)S(1)} %meta.1.refs_0_.refs_1_, bf16[8,512,256]{2,1,0:T(8,128)(2,1)S(1)} %all-to-all-done.refs_1_.refs_2_, f32[1024,256]{1,0:T(8,128)S(1)} %get-tuple-element.28.refs_2_, f32[1024,256]{1,0:T(8,128)S(1)} %get-tuple-element.29.refs_3_, ...), custom_call_target="tpu_custom_call" | custom-call | flops 134217728 | bytes 5308416 | tf_op jit(solution)/shard_map/last/pallas_call | solution.py:300
  138.0 4.1 %all-to-all-done.4 = bf16[8,128,256]{2,1,0:T(8,128)(2,1)S(1)} async-done(((bf16[8,128,256]{2,1,0:T(8,128)(2,1)}), bf16[8,128,256]{2,1,0:T(8,128)(2,1)S(1)}, u32[]{:S(2)}, u32[]{:S(2)}) %all-to-all-start.4) | async-done | bytes 524320 | tf_op jit(solution)/shard_map/all_to_all | solution.py:314
  (24 shorter events, 10.0 us)
Async XLA Ops:
  4.3 19.8 %all-to-all-start.1 = ((bf16[8,256,128]{2,1,0:T(8,128)(2,1)}), bf16[8,256,128]{2,1,0:T(8,128)(2,1)S(1)}, u32[]{:S(2)}, u32[]{:S(2)}) async-start(bf16[8,256,128]{2,1,0:T(8,128)(2,1)} %get-tuple-element.20), calls=%async_computation.1 | async-start | bytes 1048576 | tf_op jit(solution)/shard_map/all_to_all | solution.py:314
  24.1 4.5 %copy-start = (f32[8,128]{1,0:T(8,128)S(1)}, f32[8,128]{1,0:T(8,128)}, u32[]{:S(2)}) copy-start(f32[8,128]{1,0:T(8,128)} %get-tuple-element.18.refs_2_.refs_4_) | copy-start | bytes 12292
  24.1 4.5 %copy-start.1 = (s32[2]{0:T(128)S(1)}, s32[2]{0:T(128)}, u32[]{:S(2)}) copy-start(s32[2]{0:T(128)} %pad_add_fusion.refs_1_.refs_0_) | copy-start | bytes 28
  24.1 4.5 %copy-start.3 = (s32[32]{0:T(128)S(1)}, s32[32]{0:T(128)}, u32[]{:S(2)}) copy-start(s32[32]{0:T(128)} %refs_0_.7) | copy-start | bytes 388
  24.1 8.0 %copy-start.4 = (f32[8,128]{1,0:T(8,128)S(1)}, f32[8,128]{1,0:T(8,128)}, u32[]{:S(2)}) copy-start(f32[8,128]{1,0:T(8,128)} %get-tuple-element.21.refs_2_) | copy-start | bytes 12292
  24.1 46.3 %all-to-all-start = ((bf16[8,512,256]{2,1,0:T(8,128)(2,1)}), bf16[8,512,256]{2,1,0:T(8,128)(2,1)S(1)}, u32[]{:S(2)}, u32[]{:S(2)}) async-start(bf16[8,512,256]{2,1,0:T(8,128)(2,1)} %get-tuple-element.19), calls=%async_computation | async-start | bytes 4194304 | tf_op jit(solution)/shard_map/all_to_all | solution.py:314
  28.6 48.5 %copy-start.2 = (f32[2048]{0:T(1024)S(1)}, f32[2048]{0:T(1024)}, u32[]{:S(2)}) copy-start(f32[2048]{0:T(1024)} %param.10) | copy-start | bytes 24580
  32.7 12.9 %collective-permute-start.2 = (bf16[256,128]{1,0:T(8,128)(2,1)S(1)}, bf16[256,128]{1,0:T(8,128)(2,1)S(1)}, u32[]{:S(2)}, u32[]{:S(2)}) collective-permute-start(bf16[256,128]{1,0:T(8,128)(2,1)S(1)} %tail.1.refs_4_), channel_id=1, source_target_pairs={{0,504},{8,0},{16,8},{24,16},{32,24},{40,32},{48,40},{56,48},{64,5... | collective-permute-start | bytes 196616 | tf_op jit(solution)/shard_map/ppermute | solution.py:342
  41.8 8.3 %collective-permute-start.1 = (bf16[256,128]{1,0:T(8,128)(2,1)S(1)}, bf16[256,128]{1,0:T(8,128)(2,1)S(1)}, u32[]{:S(2)}, u32[]{:S(2)}) collective-permute-start(bf16[256,128]{1,0:T(8,128)(2,1)S(1)} %tail.1.refs_4_), channel_id=1, source_target_pairs={{0,8},{8,16},{16,24},{24,32},{32,40},{40,48},{48,56},{56,64},{64,7... | collective-permute-start | bytes 196616 | tf_op jit(solution)/shard_map/ppermute | solution.py:342
  43.7 9.3 %collective-permute-start = (bf16[256,128]{1,0:T(8,128)(2,1)S(1)}, bf16[256,128]{1,0:T(8,128)(2,1)S(1)}, u32[]{:S(2)}, u32[]{:S(2)}) collective-permute-start(bf16[256,128]{1,0:T(8,128)(2,1)S(1)} %tail.1.refs_4_), channel_id=1, source_target_pairs={{0,16},{8,24},{16,32},{24,40},{32,48},{40,56},{48,64},{56,72},{64,... | collective-permute-start | bytes 196616 | tf_op jit(solution)/shard_map/ppermute | solution.py:342
  53.7 18.6 %collective-permute-start.6 = (bf16[256,128]{1,0:T(8,128)(2,1)S(1)}, bf16[256,128]{1,0:T(8,128)(2,1)S(1)}, u32[]{:S(2)}, u32[]{:S(2)}) collective-permute-start(bf16[256,128]{1,0:T(8,128)(2,1)S(1)} %span_forward.1), channel_id=1, source_target_pairs={{0,16},{8,24},{16,32},{24,40},{32,48},{40,56},{48,64},{56,72},{64,... | collective-permute-start | bytes 196616 | tf_op jit(solution)/shard_map/ppermute | solution.py:342
  55.6 16.6 %collective-permute-start.5 = (bf16[256,128]{1,0:T(8,128)(2,1)S(1)}, bf16[256,128]{1,0:T(8,128)(2,1)S(1)}, u32[]{:S(2)}, u32[]{:S(2)}) collective-permute-start(bf16[256,128]{1,0:T(8,128)(2,1)S(1)} %span_forward.1), channel_id=1, source_target_pairs={{0,48},{8,56},{16,64},{24,72},{32,80},{40,88},{48,96},{56,104},{64... | collective-permute-start | bytes 196616 | tf_op jit(solution)/shard_map/ppermute | solution.py:342
  60.8 14.2 %collective-permute-start.4 = (bf16[256,128]{1,0:T(8,128)(2,1)S(1)}, bf16[256,128]{1,0:T(8,128)(2,1)S(1)}, u32[]{:S(2)}, u32[]{:S(2)}) collective-permute-start(bf16[256,128]{1,0:T(8,128)(2,1)S(1)} %span_forward.1), channel_id=1, source_target_pairs={{0,80},{8,88},{16,96},{24,104},{32,112},{40,120},{48,128},{56,136}... | collective-permute-start | bytes 196616 | tf_op jit(solution)/shard_map/ppermute | solution.py:342
  65.0 12.0 %collective-permute-start.3 = (bf16[256,128]{1,0:T(8,128)(2,1)S(1)}, bf16[256,128]{1,0:T(8,128)(2,1)S(1)}, u32[]{:S(2)}, u32[]{:S(2)}) collective-permute-start(bf16[256,128]{1,0:T(8,128)(2,1)S(1)} %span_forward.1), channel_id=1, source_target_pairs={{0,112},{8,120},{16,128},{24,136},{32,144},{40,152},{48,160},{56,1... | collective-permute-start | bytes 196616 | tf_op jit(solution)/shard_map/ppermute | solution.py:342
  79.6 25.7 %all-to-all-start.2 = ((bf16[64,4,128]{2,1,0:T(4,128)(2,1)}), bf16[64,4,128]{2,1,0:T(4,128)(2,1)S(1)}, u32[]{:S(2)}, u32[]{:S(2)}) async-start(bf16[64,4,128]{2,1,0:T(4,128)(2,1)} %bitcast.3), calls=%async_computation.2 | async-start | bytes 131072 | tf_op jit(solution)/shard_map/all_to_all | solution.py:365
  123.7 18.4 %all-to-all-start.4 = ((bf16[8,128,256]{2,1,0:T(8,128)(2,1)}), bf16[8,128,256]{2,1,0:T(8,128)(2,1)S(1)}, u32[]{:S(2)}, u32[]{:S(2)}) async-start(bf16[8,128,256]{2,1,0:T(8,128)(2,1)} %bitcast.5), calls=%async_computation.4 | async-start | bytes 1048576 | tf_op jit(solution)/shard_map/all_to_all | solution.py:314

commit v2 on v1

--- a/solution.py
+++ b/solution.py
@@ -9,8 +9,8 @@
 
 HEAD_DIM = 128
 TILE = 256
-SPAN = 4
-SPANS = 4
+
+
 epsilon = 1e-05
 
 F32 = jnp.float32
@@ -68,7 +68,7 @@
     lax.fori_loop(0, lengths_ref.shape[0], step, jnp.int32(0))
 
 
-def docs_kernel(lengths_ref, where_ref, span_ref):
+def docs_kernel(lengths_ref, where_ref, marks_ref, span_ref):
     rows = span_ref.shape[1]
     first = where_ref[0] * rows
     place = first + lax.broadcasted_iota(jnp.int32, (1, rows), 1)
@@ -115,31 +115,40 @@
             part.wait()
 
 
-def parts_kernel(lengths_ref, where_ref, keys_ref, values_ref, ended_ref, out_ref, held, sems):
-    copies = [
-        pltpu.make_async_copy(ref, held.at[k], sems.at[k])
+def parts_kernel(
+    lengths_ref, seq_ref, head_ref, keys_ref, values_ref, ended_ref, out_ref, held, sums, in_sems, out_sems
+):
+    inward = [
+        pltpu.make_async_copy(ref, held.at[k], in_sems.at[k])
         for k, ref in enumerate((keys_ref, values_ref))
     ]
-    for copy in copies:
+    for copy in inward:
         copy.start()
     ended_ref[...] = jnp.zeros_like(ended_ref)
     groups, width, _ = out_ref.shape
     tokens, cols = keys_ref.shape
-    last = (where_ref[0] + 1) * (tokens * groups) - 1
+    last = (seq_ref[0] + 1) * (tokens * groups) - 1
     begin, bound = jnp.int32(0), jnp.int32(0)
     for i in range(lengths_ref.shape[0]):
         bound = jnp.where(begin <= last, begin, bound)
         begin = begin + lengths_ref[i]
-    mine = last + 1 - (groups - where_ref[1]) * tokens
-    for copy in copies:
+    mine = last + 1 - (groups - head_ref[0]) * tokens
+    place = mine + lax.broadcasted_iota(jnp.int32, (tokens, HEAD_DIM), 0)
+    for copy in inward:
         copy.wait()
-    place = mine + lax.broadcasted_iota(jnp.int32, (tokens, cols), 0)
-    keys = held[0]
-    keys = jnp.where(place >= bound, keys, jnp.zeros_like(keys))
-    for head in range(cols // HEAD_DIM):
-        part = dot(keys[:, head_cols(head)], held[1, :, head_cols(head)], ROWS)
-        group, at = divmod(head * HEAD_DIM, width)
-        out_ref[group, at : at + HEAD_DIM, :] = part.astype(out_ref.dtype)
+    outward = []
+    for group in range(groups):
+        for head in range(width // HEAD_DIM):
+            at = slice(group * width + head * HEAD_DIM, group * width + (head + 1) * HEAD_DIM)
+            keys = held[0, :, at]
+            keys = jnp.where(place >= bound, keys, jnp.zeros_like(keys))
+            part = dot(keys, held[1, :, at], ROWS)
+            sums[group, head_cols(head), :] = part.astype(sums.dtype)
+        copy = pltpu.make_async_copy(sums.at[group], out_ref.at[group], out_sems.at[group])
+        copy.start()
+        outward.append(copy)
+    for copy in outward:
+        copy.wait()
 
 
 def tail_kernel(marks_ref, parts_ref, tail_ref):
@@ -149,41 +158,35 @@
     tail_ref[...] = total.astype(tail_ref.dtype)
 
 
-def scan_kernel(reverse, marks_ref, parts_ref, low_ref):
-    blocks = parts_ref.shape[0]
-    total = jnp.zeros(parts_ref.shape[1:], F32)
-    for k in range(blocks):
-        at = blocks - 1 - k if reverse else k
-        low_ref[at] = total.astype(low_ref.dtype)
-        part = parts_ref[at].astype(F32)
-        mark = marks_ref[at + (blocks if reverse else 0)]
-        total = jnp.where(mark > 0, part, total + part)
-
-
 def block_mark(marks_ref, blocks, at, reverse):
     return marks_ref[lax.rem(at + blocks, blocks) + (blocks if reverse else 0)]
 
 
-def span_kernel(reverse, blocks, where_ref, marks_ref, *refs):
-    span_ref = refs[-1]
+def chained(reverse, blocks, where_ref, marks_ref, refs, covers):
     mine, sign = where_ref[0], -1 if reverse else 1
     total = refs[0][...].astype(F32)
-    for k, ref in enumerate(refs[1:-1]):
-        mark = block_mark(marks_ref, blocks, mine + sign * (k - 1), reverse)
-        total = jnp.where(mark > 0, 0.0, total) + ref[...].astype(F32)
-    span_ref[...] = total.astype(span_ref.dtype)
-
-
-def entering(reverse, blocks, where_ref, marks_ref, span_refs):
-    mine, sign = where_ref[0], -1 if reverse else 1
-    total = span_refs[0][...].astype(F32)
-    for k, ref in enumerate(span_refs[1:]):
-        first = SPAN * (SPANS - 1 - k)
+    for ref, (low, high) in zip(refs[1:], covers[1:]):
         mark = jnp.int32(0)
-        for back in range(first - SPAN + 1, first + 1):
-            mark = jnp.maximum(mark, block_mark(marks_ref, blocks, mine - sign * back, reverse))
+        for at in range(low, high + 1):
+            mark = jnp.maximum(mark, block_mark(marks_ref, blocks, mine + sign * at, reverse))
         total = jnp.where(mark > 0, 0.0, total) + ref[...].astype(F32)
     return total.astype(BF16)
+
+
+def three_kernel(reverse, blocks, where_ref, marks_ref, *refs):
+    *parts, span_ref = refs
+    covers = ((-1, -1), (0, 0), (1, 1))
+    span_ref[...] = chained(reverse, blocks, where_ref, marks_ref, parts, covers)
+
+
+def nine_kernel(reverse, blocks, where_ref, marks_ref, *refs):
+    *parts, span_ref = refs
+    covers = ((-4, -2), (-1, 1), (2, 4))
+    span_ref[...] = chained(reverse, blocks, where_ref, marks_ref, parts, covers)
+
+
+def entering(reverse, blocks, where_ref, marks_ref, *refs):
+    return chained(reverse, blocks, where_ref, marks_ref, refs, ((-18, -10), (-9, -1)))
 
 
 def intra_kernel(span_ref, packed_ref, intra_ref):
@@ -202,30 +205,42 @@
 
 
 def norm_kernel(blocks, where_ref, marks_ref, packed_ref, intra_ref, gain_ref, *refs):
-    span_refs, (normed_ref, grad_ref, part_ref, state_ref) = refs[:SPANS], refs[SPANS:]
+    far_ref, near_ref, normed_ref, grad_ref, part_ref, state_ref, held, sems = refs
     queries, cotangent = unpacked(packed_ref, 2), unpacked(packed_ref, 3)
-    state = entering(False, blocks, where_ref, marks_ref, span_refs)
+    state = entering(False, blocks, where_ref, marks_ref, far_ref, near_ref)
     state_ref[...] = state
     rows, width = intra_ref.shape
+    tile = HEAD_DIM
+    outward = []
+    for low in range(0, rows, tile):
+        here = slice(low, low + tile)
+        place = low + lax.broadcasted_iota(jnp.int32, (tile, HEAD_DIM), 0)
+        for head in range(width // HEAD_DIM):
+            cols = head_cols(head)
+            at = pl.multiple_of(where_ref[1] * width + head * HEAD_DIM, HEAD_DIM)
+            gain = gain_ref[:, pl.ds(at, HEAD_DIM)]
+            inter = dot(queries[here, cols], state[cols, :], PLAIN)
+            inter = jnp.where(place < marks_ref[2 * blocks + 1], inter, 0.0)
+            attended = intra_ref[here, cols] + inter
+            scale = lax.rsqrt(jnp.mean(attended * attended, axis=-1, keepdims=True) + epsilon)
+            unit = attended * scale
+            held[here, cols] = (unit * gain).astype(BF16)
+            pulled = cotangent[here, cols].astype(F32) * gain
+            along = jnp.mean(pulled * unit, axis=-1, keepdims=True)
+            grad_ref[here, cols] = (scale * (pulled - unit * along)).astype(BF16)
+        rows_here = pl.ds(low, tile)
+        copy = pltpu.make_async_copy(held.at[rows_here, :], normed_ref.at[rows_here, :], sems.at[low // tile])
+        copy.start()
+        outward.append(copy)
     place = lax.broadcasted_iota(jnp.int32, (rows, HEAD_DIM), 0)
     in_first = place < marks_ref[2 * blocks]
-    carried = place < marks_ref[2 * blocks + 1]
     for head in range(width // HEAD_DIM):
         cols = head_cols(head)
         q = queries[:, cols]
-        inter = dot(q, state[cols, :], PLAIN)
-        attended = intra_ref[:, cols] + jnp.where(carried, inter, 0.0)
-        at = pl.multiple_of(where_ref[1] * width + head * HEAD_DIM, HEAD_DIM)
-        gain = gain_ref[:, pl.ds(at, HEAD_DIM)]
-        scale = lax.rsqrt(jnp.mean(attended * attended, axis=-1, keepdims=True) + epsilon)
-        unit = attended * scale
-        normed_ref[:, cols] = (unit * gain).astype(BF16)
-        pulled = cotangent[:, cols].astype(F32) * gain
-        along = jnp.mean(pulled * unit, axis=-1, keepdims=True)
-        grad = (scale * (pulled - unit * along)).astype(BF16)
-        grad_ref[:, cols] = grad
         kept = jnp.where(in_first, q, jnp.zeros_like(q))
-        part_ref[cols, :] = dot(kept, grad, ROWS).astype(part_ref.dtype)
+        part_ref[cols, :] = dot(kept, grad_ref[:, cols], ROWS).astype(part_ref.dtype)
+    for copy in outward:
+        copy.wait()
 
 
 def grad_q_kernel(blocks, marks_ref, span_ref, packed_ref, grad_ref, state_ref, ended_ref, grad_q_ref):
@@ -269,17 +284,40 @@
             part_v_ref[low:high, cols] = dot(turned, grad[low:], PLAIN)
 
 
-def last_kernel(blocks, marks_ref, packed_ref, part_k_ref, part_v_ref, back_ref, grad_k_ref, grad_v_ref):
+def last_kernel(
+    blocks, where_ref, marks_ref, packed_ref, part_k_ref, part_v_ref, far_ref, near_ref,
+    grad_k_ref, grad_v_ref, held, sems,
+):
     keys, values = unpacked(packed_ref, 0), unpacked(packed_ref, 1)
+    back = entering(True, blocks, where_ref, marks_ref, far_ref, near_ref)
     rows, width = keys.shape
-    place = lax.broadcasted_iota(jnp.int32, (rows, HEAD_DIM), 0)
-    later = place >= marks_ref[2 * blocks + 3]
-    for head in range(width // HEAD_DIM):
-        cols = head_cols(head)
-        inter = dot(values[:, cols], back_ref[cols, :], FEATURES)
-        grad_k_ref[:, cols] = (part_k_ref[:, cols] + jnp.where(later, inter, 0.0)).astype(BF16)
-        inter = dot(keys[:, cols], back_ref[cols, :], PLAIN)
-        grad_v_ref[:, cols] = (part_v_ref[:, cols] + jnp.where(later, inter, 0.0)).astype(BF16)
+    outward = []
+    for low in range(0, rows, TILE):
+        here = slice(low, low + TILE)
+        place = low + lax.broadcasted_iota(jnp.int32, (TILE, HEAD_DIM), 0)
+        later = place >= marks_ref[2 * blocks + 3]
+        for head in range(width // HEAD_DIM):
+            cols = head_cols(head)
+            inter = dot(values[here, cols], back[cols, :], FEATURES)
+            held[0, here, cols] = (part_k_ref[here, cols] + jnp.where(later, inter, 0.0)).astype(BF16)
+            inter = dot(keys[here, cols], back[cols, :], PLAIN)
+            held[1, here, cols] = (part_v_ref[here, cols] + jnp.where(later, inter, 0.0)).astype(BF16)
+        rows_here = pl.ds(low, TILE)
+        for k, out_ref in enumerate((grad_k_ref, grad_v_ref)):
+            copy = pltpu.make_async_copy(
+                held.at[k, rows_here, :], out_ref.at[rows_here, :], sems.at[k, low // TILE]
+            )
+            copy.start()
+            outward.append(copy)
+    for copy in outward:
+        copy.wait()
+
+
+def unpack_kernel(parts_ref, ended_ref, out_ref):
+    ended_ref[...] = jnp.zeros_like(ended_ref)
+    groups, _, width = parts_ref.shape
+    for group in range(groups):
+        out_ref[:, group * width : (group + 1) * width] = parts_ref[group]
 
 
 SMEM = pl.BlockSpec(memory_space=pltpu.SMEM)
@@ -334,7 +372,7 @@
         [VMEM, ANYWHERE],
         60,
     )
-    return ended, across_head(packed)
+    return ended, packed
 
 
 def from_block(field, step):
@@ -342,39 +380,36 @@
     return lax.ppermute(field, "seq", [(at, (at + step) % blocks) for at in range(blocks)])
 
 
-def spans_before(part, where, marks, reverse):
-    sign = -1 if reverse else 1
-    parts = [from_block(part, sign * 2), from_block(part, sign), part, from_block(part, -sign)]
-    (span,) = call(
-        functools.partial(span_kernel, reverse, lax.axis_size("seq")),
-        "span_back" if reverse else "span_forward",
-        [jax.ShapeDtypeStruct(part.shape, BF16)],
+def span(kernel, parts, where, marks, reverse, after=()):
+    blocks = lax.axis_size("seq")
+    return call(
+        functools.partial(kernel, reverse, blocks),
+        kernel.__name__.replace("kernel", "back" if reverse else "forward"),
+        [jax.ShapeDtypeStruct(parts[0].shape, BF16)],
         [where, marks],
         parts,
-        SPAN * part.size,
-    )
-    spans = {k: from_block(span, sign * (2 + SPAN * k)) for k in (2, 1, 3, 0)}
-    return [spans[k] for k in reversed(range(SPANS))], parts[0]
-
-
-def carried_over(part, marks, reverse, beside):
-    blocks = lax.axis_size("seq")
-    height, width = part.shape
-    first = beside[0]([part])
-    sent = part.reshape(blocks, height // blocks, width)
-    got = lax.all_to_all(sent, "seq", split_axis=0, concat_axis=0, tiled=True)
-    (low,) = call(
-        functools.partial(scan_kernel, reverse),
-        "scan_back" if reverse else "scan_forward",
-        [jax.ShapeDtypeStruct(got.shape, BF16)],
-        [marks],
-        [got],
-        got.size,
-        after=first[:1],
-    )
-    second = beside[1]([low], first)
-    mine = lax.all_to_all(low, "seq", split_axis=0, concat_axis=0, tiled=True)
-    return mine.reshape(height, width), first, second
+        len(parts) * parts[0].size,
+        after=after,
+    )[0]
+
+
+def span_of_three(part, where, marks, reverse, after=()):
+    parts = [from_block(part, 1), part, from_block(part, -1)]
+    if reverse:
+        parts.reverse()
+    return span(three_kernel, parts, where, marks, reverse, after)
+
+
+def span_of_nine(three, where, marks, reverse, after=()):
+    parts = [from_block(three, 3), three, from_block(three, -3)]
+    if reverse:
+        parts.reverse()
+    return span(nine_kernel, parts, where, marks, reverse, after)
+
+
+def two_spans(nine, reverse):
+    sign = -1 if reverse else 1
+    return [from_block(nine, sign * 14), from_block(nine, sign * 5)]
 
 
 def on_device(queries, keys, values, cotangent, gain, lengths):
@@ -391,11 +426,17 @@
         parts_kernel,
         "parts",
         [ENDED, bf16((groups, width, HEAD_DIM))],
-        [lengths, where],
+        [lengths, lax.axis_index("seq").astype(jnp.int32).reshape(1), here.reshape(1)],
         [keys, values],
         2 * tokens * cols * HEAD_DIM,
-        [pltpu.VMEM((2, tokens, cols), BF16), pltpu.SemaphoreType.DMA((2,))],
+        [
+            pltpu.VMEM((2, tokens, cols), BF16),
+            pltpu.VMEM((groups, width, HEAD_DIM), BF16),
+            pltpu.SemaphoreType.DMA((2,)),
+            pltpu.SemaphoreType.DMA((groups,)),
+        ],
         in_specs=[ANYWHERE] * 2,
+        out_specs=[VMEM, ANYWHERE],
         limit=60,
     )
     (marks,) = call(
@@ -408,9 +449,9 @@
         after=[started],
         out_specs=[SMEM],
     )
-    (span,) = call(docs_kernel, "docs", [int32((2, rows))], [lengths, where], [], rows, after=[started])
+    (docs,) = call(docs_kernel, "docs", [int32((2, rows))], [lengths, where, marks], [], rows)
     gathered = across_head(parts)
-    ended, packed = to_heads([keys, values, queries, cotangent], [started])
+    ended, packed = to_heads([keys, values, queries, cotangent], [docs])
     (tail,) = call(
         tail_kernel,
         "tail",
@@ -418,10 +459,12 @@
         [marks],
         [gathered],
         gathered.size,
-        after=[ended, span],
-    )
-    before, _ = spans_before(tail, where, marks, False)
-    (inside,) = call(intra_kernel, "intra", [f32((rows, width))], [], [span, packed], 2 * square)
+        after=[ended],
+    )
+    packed = across_head(packed)
+    three = span_of_three(tail, where, marks, False)
+    before = two_spans(span_of_nine(three, where, marks, False), False)
+    (inside,) = call(intra_kernel, "intra", [f32((rows, width))], [], [docs, packed], 2 * square)
     normed, grad, part, state = call(
         functools.partial(norm_kernel, blocks),
         "norm",
@@ -429,53 +472,43 @@
         [where, marks],
         [packed, inside, gain.reshape(1, cols), *before],
         4 * rows * width * HEAD_DIM,
-    )
-
-    def grads_q(after):
-        return call(
-            functools.partial(grad_q_kernel, blocks),
-            "grads_q",
-            [ENDED, bf16((rows, width))],
-            [marks],
-            [span, packed, grad, state],
-            2 * square,
-            after=after,
-        )
-
-    def grads_kv(after, _):
-        return call(
-            grad_kv_kernel,
-            "grads_kv",
-            [f32((rows, width)), f32((rows, width))],
-            [],
-            [span, packed, grad],
-            4 * square,
-            after=after,
-        )
-
-    back, (_, grad_q), (part_k, part_v) = carried_over(part, marks, True, (grads_q, grads_kv))
-    (normed,) = call(
-        lambda *refs: None,
-        "normed",
-        [bf16((rows, width))],
+        [pltpu.VMEM((rows, width), BF16), pltpu.SemaphoreType.DMA((rows // HEAD_DIM,))],
+        out_specs=[ANYWHERE, VMEM, VMEM, VMEM],
+    )
+
+    normed = across_head(normed.reshape(groups, tokens, width))
+    ended, grad_q = call(
+        functools.partial(grad_q_kernel, blocks),
+        "grads_q",
+        [ENDED, bf16((rows, width))],
+        [marks],
+        [docs, packed, grad, state],
+        2 * square,
+    )
+    three = span_of_three(part, where, marks, True, [ended])
+    nine = span_of_nine(three, where, marks, True)
+    part_k, part_v = call(
+        grad_kv_kernel,
+        "grads_kv",
+        [f32((rows, width)), f32((rows, width))],
         [],
-        [normed],
-        0,
-        after=[back],
-        in_specs=[ANYWHERE],
-        out_specs=[ANYWHERE],
-        aliases={0: 0},
-    )
-    normed = across_head(normed.reshape(groups, tokens, width))
+        [docs, packed, grad],
+        4 * square,
+        after=[nine],
+    )
+    ended, normed = call(unpack_kernel, "unpack", [ENDED, bf16((tokens, cols))], [], [normed], 0)
     grad_k, grad_v = call(
         functools.partial(last_kernel, blocks),
         "last",
         [bf16((rows, width)), bf16((rows, width))],
-        [marks],
-        [packed, part_k, part_v, back],
+        [where, marks],
+        [packed, part_k, part_v, *two_spans(nine, True)],
         4 * rows * width * HEAD_DIM,
-    )
-    return normed.transpose(1, 0, 2).reshape(tokens, cols), grad_q, grad_k, grad_v
+        [pltpu.VMEM((2, rows, width), BF16), pltpu.SemaphoreType.DMA((2, rows // TILE))],
+        after=[ended],
+        out_specs=[ANYWHERE] * 2,
+    )
+    return normed, grad_q, grad_k, grad_v
 
 
 def solution(mesh):

time: 144 us -> 138 us (0.958)
  the two profiles are of different devices: /device:TPU:1 before, /device:TPU:10 now
where the time goes in v2:
time: 138 us; the launch traced here: 137 us
  starting transfers between devices  83.3 us (60%)
  Pallas kernels  28.9 us (21%)
  waiting for transfers between devices  17.7 us (13%)
  local copies, waits for them, and re-layouts  6.47 us (5%)
    ppermute x12, starting transfers between devices, from_block(): lax.ppermute(field, 'seq', [(at, (at + step) % blocks) for at in range(bl...  67.9 us
    pallas_call x15, Pallas kernels, call(): pl.pallas_call(body, name=name, out_shape=outs, in_specs=[SMEM] * len(sca...  28.9 us
    ppermute x12, waiting for transfers between devices, from_block(): lax.ppermute(field, 'seq', [(at, (at + step) % blocks) for at in range(bl...  16.9 us
    all_to_all x3, starting transfers between devices, across_head(): lax.all_to_all(parts, 'head', split_axis=0, concat_axis=0, tiled=True)  15.4 us
    unnamed x22, local copies, waits for them, and re-layouts  6.47 us
  transfers between devices with their start and end apart: 15, of which 7 were waited for; matrix products, arithmetic and copies ran while one was open for 0% of the time, Pallas kernels for 14%

profile of v2, /device:TPU:10, one launch (start us, length us, event | category | flops | bytes accessed | tf_op | source)
XLA Modules:
  0.0 137.3 jit_solution(185974426419808520)
XLA Ops:
  0.6 3.6 %parts.1 = (f32[8,128]{1,0:T(8,128)}, bf16[8,256,128]{2,1,0:T(8,128)(2,1)}) custom-call(s32[32]{0:T(128)} %refs_0_.6, s32[1]{0:T(128)} %bitcast.refs_1_, s32[1]{0:T(128)} %bitcast.1.refs_2_, bf16[128,2048]{1,0:T(8,128)(2,1)} %refs_0_.7, bf16[128,2048]{1,0:T(8,128)(2,1)} %refs_1_.1), custom_call_target="tpu_custom_call" | custom-call | flops 67108864 | bytes 1576960 | tf_op jit(solution)/shard_map/parts/pallas_call | solution.py:338
  4.3 4.8 %all-to-all-start.1 = ((bf16[8,256,128]{2,1,0:T(8,128)(2,1)}), bf16[8,256,128]{2,1,0:T(8,128)(2,1)S(1)}, u32[]{:S(2)}, u32[]{:S(2)}) async-start(bf16[8,256,128]{2,1,0:T(8,128)(2,1)} %get-tuple-element.22), calls=%async_computation.1 | async-start | bytes 1048576 | tf_op jit(solution)/shard_map/all_to_all | solution.py:352
  9.9 2.5 %meta.1.refs_2_.refs_0_.refs_1_ = s32[132]{0:T(256)S(1)} custom-call(s32[32]{0:T(128)S(1)} %copy-done.8, s32[2]{0:T(128)S(1)} %pad_add_fusion.refs_1_.refs_0_, f32[8,128]{1,0:T(8,128)S(1)} %copy-done.10), custom_call_target="tpu_custom_call" | custom-call | flops 1024 | bytes 528 | tf_op jit(solution)/shard_map/meta/pallas_call | solution.py:338
  13.9 3.3 %pack.1 = (f32[8,128]{1,0:T(8,128)}, bf16[8,512,256]{2,1,0:T(8,128)(2,1)}) custom-call(bf16[128,2048]{1,0:T(8,128)(2,1)} %refs_0_.7, bf16[128,2048]{1,0:T(8,128)(2,1)} %refs_1_.1, bf16[128,2048]{1,0:T(8,128)(2,1)} %refs_2_.1, bf16[128,2048]{1,0:T(8,128)(2,1)} %refs_3_.3, s32[2,1024]{1,0:T(2,128)} %copy-done.5), custom_call_target="tpu_custom_call" | custom-call | bytes 4198400 | tf_op jit(solution)/shard_map/pack/pallas_call | solution.py:338
  18.0 5.1 %all-to-all-start = ((bf16[8,512,256]{2,1,0:T(8,128)(2,1)}), bf16[8,512,256]{2,1,0:T(8,128)(2,1)S(1)}, u32[]{:S(2)}, u32[]{:S(2)}) async-start(bf16[8,512,256]{2,1,0:T(8,128)(2,1)} %get-tuple-element.21), calls=%async_computation | async-start | bytes 4194304 | tf_op jit(solution)/shard_map/all_to_all | solution.py:352
  23.7 11.3 %collective-permute-start.1 = (bf16[256,128]{1,0:T(8,128)(2,1)S(1)}, bf16[256,128]{1,0:T(8,128)(2,1)S(1)}, u32[]{:S(2)}, u32[]{:S(2)}) collective-permute-start(bf16[256,128]{1,0:T(8,128)(2,1)S(1)} %tail.1.refs_3_), channel_id=1, source_target_pairs={{0,504},{8,0},{16,8},{24,16},{32,24},{40,32},{48,40},{56,48},{64,5... | collective-permute-start | bytes 196616 | tf_op jit(solution)/shard_map/ppermute | solution.py:380
  35.0 1.9 %collective-permute-start = (bf16[256,128]{1,0:T(8,128)(2,1)S(1)}, bf16[256,128]{1,0:T(8,128)(2,1)S(1)}, u32[]{:S(2)}, u32[]{:S(2)}) collective-permute-start(bf16[256,128]{1,0:T(8,128)(2,1)S(1)} %tail.1.refs_3_), channel_id=1, source_target_pairs={{0,8},{8,16},{16,24},{24,32},{32,40},{40,48},{48,56},{56,64},{64,7... | collective-permute-start | bytes 196616 | tf_op jit(solution)/shard_map/ppermute | solution.py:380
  37.0 6.3 %collective-permute-done.refs_2_ = bf16[256,128]{1,0:T(8,128)(2,1)S(1)} collective-permute-done((bf16[256,128]{1,0:T(8,128)(2,1)S(1)}, bf16[256,128]{1,0:T(8,128)(2,1)S(1)}, u32[]{:S(2)}, u32[]{:S(2)}) %collective-permute-start) | collective-permute-done | bytes 65568 | tf_op jit(solution)/shard_map/ppermute | solution.py:380
  43.9 1.9 %collective-permute-start.3 = (bf16[256,128]{1,0:T(8,128)(2,1)S(1)}, bf16[256,128]{1,0:T(8,128)(2,1)S(1)}, u32[]{:S(2)}, u32[]{:S(2)}) collective-permute-start(bf16[256,128]{1,0:T(8,128)(2,1)S(1)} %three_forward.1.refs_3_), channel_id=1, source_target_pairs={{0,488},{8,496},{16,504},{24,0},{32,8},{40,16},{48,24},{56,32},{64... | collective-permute-start | bytes 196616 | tf_op jit(solution)/shard_map/ppermute | solution.py:380
  45.8 5.7 %collective-permute-start.2 = (bf16[256,128]{1,0:T(8,128)(2,1)S(1)}, bf16[256,128]{1,0:T(8,128)(2,1)S(1)}, u32[]{:S(2)}, u32[]{:S(2)}) collective-permute-start(bf16[256,128]{1,0:T(8,128)(2,1)S(1)} %three_forward.1.refs_3_), channel_id=1, source_target_pairs={{0,24},{8,32},{16,40},{24,48},{32,56},{40,64},{48,72},{56,80},{64,... | collective-permute-start | bytes 196616 | tf_op jit(solution)/shard_map/ppermute | solution.py:380
  51.9 4.5 %collective-permute-done.2.refs_2_ = bf16[256,128]{1,0:T(8,128)(2,1)S(1)} collective-permute-done((bf16[256,128]{1,0:T(8,128)(2,1)S(1)}, bf16[256,128]{1,0:T(8,128)(2,1)S(1)}, u32[]{:S(2)}, u32[]{:S(2)}) %collective-permute-start.2) | collective-permute-done | bytes 65568 | tf_op jit(solution)/shard_map/ppermute | solution.py:380
  56.9 2.6 %collective-permute-start.5 = (bf16[256,128]{1,0:T(8,128)(2,1)S(1)}, bf16[256,128]{1,0:T(8,128)(2,1)S(1)}, u32[]{:S(2)}, u32[]{:S(2)}) collective-permute-start(bf16[256,128]{1,0:T(8,128)(2,1)S(1)} %nine_forward.1), channel_id=1, source_target_pairs={{0,40},{8,48},{16,56},{24,64},{32,72},{40,80},{48,88},{56,96},{64,... | collective-permute-start | bytes 196616 | tf_op jit(solution)/shard_map/ppermute | solution.py:380
  59.6 7.3 %collective-permute-start.4 = (bf16[256,128]{1,0:T(8,128)(2,1)S(1)}, bf16[256,128]{1,0:T(8,128)(2,1)S(1)}, u32[]{:S(2)}, u32[]{:S(2)}) collective-permute-start(bf16[256,128]{1,0:T(8,128)(2,1)S(1)} %nine_forward.1), channel_id=1, source_target_pairs={{0,112},{8,120},{16,128},{24,136},{32,144},{40,152},{48,160},{56,1... | collective-permute-start | bytes 196616 | tf_op jit(solution)/shard_map/ppermute | solution.py:380
  68.8 3.0 %collective-permute-done.5.refs_6_ = bf16[256,128]{1,0:T(8,128)(2,1)S(1)} collective-permute-done((bf16[256,128]{1,0:T(8,128)(2,1)S(1)}, bf16[256,128]{1,0:T(8,128)(2,1)S(1)}, u32[]{:S(2)}, u32[]{:S(2)}) %collective-permute-start.5) | collective-permute-done | bytes 65568 | tf_op jit(solution)/shard_map/ppermute | solution.py:380
  71.8 4.4 %norm.1 = (bf16[1024,256]{1,0:T(8,128)(2,1)S(1)}, bf16[1024,256]{1,0:T(8,128)(2,1)S(1)}, bf16[256,128]{1,0:T(8,128)(2,1)S(1)}, bf16[256,128]{1,0:T(8,128)(2,1)S(1)}) custom-call(s32[2]{0:T(128)S(1)} %pad_add_fusion.refs_1_.refs_0_, s32[132]{0:T(256)S(1)} %meta.1.refs_2_.refs_0_.refs_1_, bf16[8,512,256]{2,1,0:T(8,128)(2,1)S(1)} %all-to-all-done.refs_1_.refs_2_, ...), custom_call_target="tpu_custom_call" | custom-call | flops 134217728 | bytes 4464640 | tf_op jit(solution)/shard_map/norm/pallas_call | solution.py:338
  77.0 5.4 %all-to-all-start.2 = ((bf16[8,128,256]{2,1,0:T(8,128)(2,1)}), bf16[8,128,256]{2,1,0:T(8,128)(2,1)S(1)}, u32[]{:S(2)}, u32[]{:S(2)}) async-start(bf16[8,128,256]{2,1,0:T(8,128)(2,1)} %bitcast.4), calls=%async_computation.2 | async-start | bytes 1048576 | tf_op jit(solution)/shard_map/all_to_all | solution.py:352
  82.4 3.0 %collective-permute-start.7 = (bf16[256,128]{1,0:T(8,128)(2,1)S(1)}, bf16[256,128]{1,0:T(8,128)(2,1)S(1)}, u32[]{:S(2)}, u32[]{:S(2)}) collective-permute-start(bf16[256,128]{1,0:T(8,128)(2,1)S(1)} %get-tuple-element.29.refs_3_), channel_id=1, source_target_pairs={{0,8},{8,16},{16,24},{24,32},{32,40},{40,48},{48,56},{56,64},{64,7... | collective-permute-start | bytes 196616 | tf_op jit(solution)/shard_map/ppermute | solution.py:380
  85.4 5.0 %collective-permute-start.6 = (bf16[256,128]{1,0:T(8,128)(2,1)S(1)}, bf16[256,128]{1,0:T(8,128)(2,1)S(1)}, u32[]{:S(2)}, u32[]{:S(2)}) collective-permute-start(bf16[256,128]{1,0:T(8,128)(2,1)S(1)} %get-tuple-element.29.refs_3_), channel_id=1, source_target_pairs={{0,504},{8,0},{16,8},{24,16},{32,24},{40,32},{48,40},{56,48},{64,5... | collective-permute-start | bytes 196616 | tf_op jit(solution)/shard_map/ppermute | solution.py:380
  90.4 3.2 %grads_q.1 = (f32[8,128]{1,0:T(8,128)S(1)}, bf16[1024,256]{1,0:T(8,128)(2,1)}) custom-call(s32[132]{0:T(256)S(1)} %meta.1.refs_2_.refs_0_.refs_1_, s32[2,1024]{1,0:T(2,128)S(1)} %copy-done.6, bf16[8,512,256]{2,1,0:T(8,128)(2,1)S(1)} %all-to-all-done.refs_1_.refs_2_, bf16[1024,256]{1,0:T(8,128)(2,1)S(1)} %get-tuple-element.26.refs_3_.refs_2_, ...), custom_call_target="tpu_custom_call" | custom-call | flops 536870912 | bytes 3223552 | tf_op jit(solution)/shard_map/grads_q/pallas_call | solution.py:338
  94.2 2.6 %collective-permute-start.9 = (bf16[256,128]{1,0:T(8,128)(2,1)S(1)}, bf16[256,128]{1,0:T(8,128)(2,1)S(1)}, u32[]{:S(2)}, u32[]{:S(2)}) collective-permute-start(bf16[256,128]{1,0:T(8,128)(2,1)S(1)} %three_back.1.refs_3_), channel_id=1, source_target_pairs={{0,24},{8,32},{16,40},{24,48},{32,56},{40,64},{48,72},{56,80},{64,... | collective-permute-start | bytes 196616 | tf_op jit(solution)/shard_map/ppermute | solution.py:380
  96.8 7.2 %collective-permute-start.8 = (bf16[256,128]{1,0:T(8,128)(2,1)S(1)}, bf16[256,128]{1,0:T(8,128)(2,1)S(1)}, u32[]{:S(2)}, u32[]{:S(2)}) collective-permute-start(bf16[256,128]{1,0:T(8,128)(2,1)S(1)} %three_back.1.refs_3_), channel_id=1, source_target_pairs={{0,488},{8,496},{16,504},{24,0},{32,8},{40,16},{48,24},{56,32},{64... | collective-permute-start | bytes 196616 | tf_op jit(solution)/shard_map/ppermute | solution.py:380
  107.3 6.8 %collective-permute-start.11 = (bf16[256,128]{1,0:T(8,128)(2,1)S(1)}, bf16[256,128]{1,0:T(8,128)(2,1)S(1)}, u32[]{:S(2)}, u32[]{:S(2)}) collective-permute-start(bf16[256,128]{1,0:T(8,128)(2,1)S(1)} %nine_back.1.refs_3_), channel_id=1, source_target_pairs={{0,472},{8,480},{16,488},{24,496},{32,504},{40,0},{48,8},{56,16},{... | collective-permute-start | bytes 196616 | tf_op jit(solution)/shard_map/ppermute | solution.py:380
  114.1 12.7 %collective-permute-start.10 = (bf16[256,128]{1,0:T(8,128)(2,1)S(1)}, bf16[256,128]{1,0:T(8,128)(2,1)S(1)}, u32[]{:S(2)}, u32[]{:S(2)}) collective-permute-start(bf16[256,128]{1,0:T(8,128)(2,1)S(1)} %nine_back.1.refs_3_), channel_id=1, source_target_pairs={{0,400},{8,408},{16,416},{24,424},{32,432},{40,440},{48,448},{56,4... | collective-permute-start | bytes 196616 | tf_op jit(solution)/shard_map/ppermute | solution.py:380
  126.8 3.3 %grads_kv.1 = (f32[1024,256]{1,0:T(8,128)S(1)}, f32[1024,256]{1,0:T(8,128)S(1)}) custom-call(s32[2,1024]{1,0:T(2,128)S(1)} %copy-done.6, bf16[8,512,256]{2,1,0:T(8,128)(2,1)S(1)} %all-to-all-done.refs_1_.refs_2_, bf16[1024,256]{1,0:T(8,128)(2,1)S(1)} %get-tuple-element.26.refs_3_.refs_2_, bf16[256,128]{1,0:T(8,128)(2,1)S(1)} %nine_back.1.refs_3_), custom_call_target="tpu_custom_call" | custom-call | flops 1073741824 | bytes 4726784 | tf_op jit(solution)/shard_map/grads_kv/pallas_call | solution.py:338
  (44 shorter events, 18.9 us)
Async XLA Ops:
  0.6 8.5 %copy-start.8 = (s32[32]{0:T(128)S(1)}, s32[32]{0:T(128)}, u32[]{:S(2)}) copy-start(s32[32]{0:T(128)} %refs_0_.6) | copy-start | bytes 388
  4.3 13.7 %all-to-all-start.1 = ((bf16[8,256,128]{2,1,0:T(8,128)(2,1)}), bf16[8,256,128]{2,1,0:T(8,128)(2,1)S(1)}, u32[]{:S(2)}, u32[]{:S(2)}) async-start(bf16[8,256,128]{2,1,0:T(8,128)(2,1)} %get-tuple-element.22), calls=%async_computation.1 | async-start | bytes 1048576 | tf_op jit(solution)/shard_map/all_to_all | solution.py:352
  18.0 5.1 %copy-start.9 = (f32[8,128]{1,0:T(8,128)S(1)}, f32[8,128]{1,0:T(8,128)}, u32[]{:S(2)}) copy-start(f32[8,128]{1,0:T(8,128)} %get-tuple-element.23.refs_2_) | copy-start | bytes 12292
  18.0 48.8 %copy-start.6 = (s32[2,1024]{1,0:T(2,128)S(1)}, s32[2,1024]{1,0:T(2,128)}, u32[]{:S(2)}) copy-start(s32[2,1024]{1,0:T(2,128)} %copy-done.5) | copy-start | bytes 24580
  18.0 48.8 %all-to-all-start = ((bf16[8,512,256]{2,1,0:T(8,128)(2,1)}), bf16[8,512,256]{2,1,0:T(8,128)(2,1)S(1)}, u32[]{:S(2)}, u32[]{:S(2)}) async-start(bf16[8,512,256]{2,1,0:T(8,128)(2,1)} %get-tuple-element.21), calls=%async_computation | async-start | bytes 4194304 | tf_op jit(solution)/shard_map/all_to_all | solution.py:352
  23.1 48.7 %copy-start.7 = (f32[2048]{0:T(1024)S(1)}, f32[2048]{0:T(1024)}, u32[]{:S(2)}) copy-start(f32[2048]{0:T(1024)} %param.10) | copy-start | bytes 24580
  23.7 13.2 %collective-permute-start.1 = (bf16[256,128]{1,0:T(8,128)(2,1)S(1)}, bf16[256,128]{1,0:T(8,128)(2,1)S(1)}, u32[]{:S(2)}, u32[]{:S(2)}) collective-permute-start(bf16[256,128]{1,0:T(8,128)(2,1)S(1)} %tail.1.refs_3_), channel_id=1, source_target_pairs={{0,504},{8,0},{16,8},{24,16},{32,24},{40,32},{48,40},{56,48},{64,5... | collective-permute-start | bytes 196616 | tf_op jit(solution)/shard_map/ppermute | solution.py:380
  35.0 8.3 %collective-permute-start = (bf16[256,128]{1,0:T(8,128)(2,1)S(1)}, bf16[256,128]{1,0:T(8,128)(2,1)S(1)}, u32[]{:S(2)}, u32[]{:S(2)}) collective-permute-start(bf16[256,128]{1,0:T(8,128)(2,1)S(1)} %tail.1.refs_3_), channel_id=1, source_target_pairs={{0,8},{8,16},{16,24},{24,32},{32,40},{40,48},{48,56},{56,64},{64,7... | collective-permute-start | bytes 196616 | tf_op jit(solution)/shard_map/ppermute | solution.py:380
  43.9 8.0 %collective-permute-start.3 = (bf16[256,128]{1,0:T(8,128)(2,1)S(1)}, bf16[256,128]{1,0:T(8,128)(2,1)S(1)}, u32[]{:S(2)}, u32[]{:S(2)}) collective-permute-start(bf16[256,128]{1,0:T(8,128)(2,1)S(1)} %three_forward.1.refs_3_), channel_id=1, source_target_pairs={{0,488},{8,496},{16,504},{24,0},{32,8},{40,16},{48,24},{56,32},{64... | collective-permute-start | bytes 196616 | tf_op jit(solution)/shard_map/ppermute | solution.py:380
  45.8 10.5 %collective-permute-start.2 = (bf16[256,128]{1,0:T(8,128)(2,1)S(1)}, bf16[256,128]{1,0:T(8,128)(2,1)S(1)}, u32[]{:S(2)}, u32[]{:S(2)}) collective-permute-start(bf16[256,128]{1,0:T(8,128)(2,1)S(1)} %three_forward.1.refs_3_), channel_id=1, source_target_pairs={{0,24},{8,32},{16,40},{24,48},{32,56},{40,64},{48,72},{56,80},{64,... | collective-permute-start | bytes 196616 | tf_op jit(solution)/shard_map/ppermute | solution.py:380
  56.9 14.9 %collective-permute-start.5 = (bf16[256,128]{1,0:T(8,128)(2,1)S(1)}, bf16[256,128]{1,0:T(8,128)(2,1)S(1)}, u32[]{:S(2)}, u32[]{:S(2)}) collective-permute-start(bf16[256,128]{1,0:T(8,128)(2,1)S(1)} %nine_forward.1), channel_id=1, source_target_pairs={{0,40},{8,48},{16,56},{24,64},{32,72},{40,80},{48,88},{56,96},{64,... | collective-permute-start | bytes 196616 | tf_op jit(solution)/shard_map/ppermute | solution.py:380
  59.6 12.2 %collective-permute-start.4 = (bf16[256,128]{1,0:T(8,128)(2,1)S(1)}, bf16[256,128]{1,0:T(8,128)(2,1)S(1)}, u32[]{:S(2)}, u32[]{:S(2)}) collective-permute-start(bf16[256,128]{1,0:T(8,128)(2,1)S(1)} %nine_forward.1), channel_id=1, source_target_pairs={{0,112},{8,120},{16,128},{24,136},{32,144},{40,152},{48,160},{56,1... | collective-permute-start | bytes 196616 | tf_op jit(solution)/shard_map/ppermute | solution.py:380
  76.2 0.8 copy-start.4
  77.0 55.1 %all-to-all-start.2 = ((bf16[8,128,256]{2,1,0:T(8,128)(2,1)}), bf16[8,128,256]{2,1,0:T(8,128)(2,1)S(1)}, u32[]{:S(2)}, u32[]{:S(2)}) async-start(bf16[8,128,256]{2,1,0:T(8,128)(2,1)} %bitcast.4), calls=%async_computation.2 | async-start | bytes 1048576 | tf_op jit(solution)/shard_map/all_to_all | solution.py:352
  82.4 11.2 %collective-permute-start.7 = (bf16[256,128]{1,0:T(8,128)(2,1)S(1)}, bf16[256,128]{1,0:T(8,128)(2,1)S(1)}, u32[]{:S(2)}, u32[]{:S(2)}) collective-permute-start(bf16[256,128]{1,0:T(8,128)(2,1)S(1)} %get-tuple-element.29.refs_3_), channel_id=1, source_target_pairs={{0,8},{8,16},{16,24},{24,32},{32,40},{40,48},{48,56},{56,64},{64,7... | collective-permute-start | bytes 196616 | tf_op jit(solution)/shard_map/ppermute | solution.py:380
  85.4 8.2 %collective-permute-start.6 = (bf16[256,128]{1,0:T(8,128)(2,1)S(1)}, bf16[256,128]{1,0:T(8,128)(2,1)S(1)}, u32[]{:S(2)}, u32[]{:S(2)}) collective-permute-start(bf16[256,128]{1,0:T(8,128)(2,1)S(1)} %get-tuple-element.29.refs_3_), channel_id=1, source_target_pairs={{0,504},{8,0},{16,8},{24,16},{32,24},{40,32},{48,40},{56,48},{64,5... | collective-permute-start | bytes 196616 | tf_op jit(solution)/shard_map/ppermute | solution.py:380
  94.2 10.8 %collective-permute-start.9 = (bf16[256,128]{1,0:T(8,128)(2,1)S(1)}, bf16[256,128]{1,0:T(8,128)(2,1)S(1)}, u32[]{:S(2)}, u32[]{:S(2)}) collective-permute-start(bf16[256,128]{1,0:T(8,128)(2,1)S(1)} %three_back.1.refs_3_), channel_id=1, source_target_pairs={{0,24},{8,32},{16,40},{24,48},{32,56},{40,64},{48,72},{56,80},{64,... | collective-permute-start | bytes 196616 | tf_op jit(solution)/shard_map/ppermute | solution.py:380
  96.8 9.9 %collective-permute-start.8 = (bf16[256,128]{1,0:T(8,128)(2,1)S(1)}, bf16[256,128]{1,0:T(8,128)(2,1)S(1)}, u32[]{:S(2)}, u32[]{:S(2)}) collective-permute-start(bf16[256,128]{1,0:T(8,128)(2,1)S(1)} %three_back.1.refs_3_), channel_id=1, source_target_pairs={{0,488},{8,496},{16,504},{24,0},{32,8},{40,16},{48,24},{56,32},{64... | collective-permute-start | bytes 196616 | tf_op jit(solution)/shard_map/ppermute | solution.py:380
  107.3 25.6 %collective-permute-start.11 = (bf16[256,128]{1,0:T(8,128)(2,1)S(1)}, bf16[256,128]{1,0:T(8,128)(2,1)S(1)}, u32[]{:S(2)}, u32[]{:S(2)}) collective-permute-start(bf16[256,128]{1,0:T(8,128)(2,1)S(1)} %nine_back.1.refs_3_), channel_id=1, source_target_pairs={{0,472},{8,480},{16,488},{24,496},{32,504},{40,0},{48,8},{56,16},{... | collective-permute-start | bytes 196616 | tf_op jit(solution)/shard_map/ppermute | solution.py:380
  114.1 18.9 %collective-permute-start.10 = (bf16[256,128]{1,0:T(8,128)(2,1)S(1)}, bf16[256,128]{1,0:T(8,128)(2,1)S(1)}, u32[]{:S(2)}, u32[]{:S(2)}) collective-permute-start(bf16[256,128]{1,0:T(8,128)(2,1)S(1)} %nine_back.1.refs_3_), channel_id=1, source_target_pairs={{0,400},{8,408},{16,416},{24,424},{32,432},{40,440},{48,448},{56,4... | collective-permute-start | bytes 196616 | tf_op jit(solution)/shard_map/ppermute | solution.py:380
  130.2 1.0 copy-start
  131.1 1.0 copy-start.2
  133.0 1.2 copy-start.1
  134.2 1.2 copy-start.3
  (2 other events, 1.3 us)

commit v3 on v2

--- a/solution.py
+++ b/solution.py
@@ -205,33 +205,28 @@
 
 
 def norm_kernel(blocks, where_ref, marks_ref, packed_ref, intra_ref, gain_ref, *refs):
-    far_ref, near_ref, normed_ref, grad_ref, part_ref, state_ref, held, sems = refs
+    far_ref, near_ref, normed_ref, grad_ref, part_ref, state_ref = refs
     queries, cotangent = unpacked(packed_ref, 2), unpacked(packed_ref, 3)
     state = entering(False, blocks, where_ref, marks_ref, far_ref, near_ref)
     state_ref[...] = state
     rows, width = intra_ref.shape
     tile = HEAD_DIM
-    outward = []
-    for low in range(0, rows, tile):
-        here = slice(low, low + tile)
-        place = low + lax.broadcasted_iota(jnp.int32, (tile, HEAD_DIM), 0)
-        for head in range(width // HEAD_DIM):
-            cols = head_cols(head)
-            at = pl.multiple_of(where_ref[1] * width + head * HEAD_DIM, HEAD_DIM)
-            gain = gain_ref[:, pl.ds(at, HEAD_DIM)]
+    for head in range(width // HEAD_DIM):
+        cols = head_cols(head)
+        at = pl.multiple_of(where_ref[1] * width + head * HEAD_DIM, HEAD_DIM)
+        gain = gain_ref[:, pl.ds(at, HEAD_DIM)]
+        for low in range(0, rows, tile):
+            here = slice(low, low + tile)
+            place = low + lax.broadcasted_iota(jnp.int32, (tile, HEAD_DIM), 0)
             inter = dot(queries[here, cols], state[cols, :], PLAIN)
             inter = jnp.where(place < marks_ref[2 * blocks + 1], inter, 0.0)
             attended = intra_ref[here, cols] + inter
             scale = lax.rsqrt(jnp.mean(attended * attended, axis=-1, keepdims=True) + epsilon)
             unit = attended * scale
-            held[here, cols] = (unit * gain).astype(BF16)
+            normed_ref[here, cols] = (unit * gain).astype(BF16)
             pulled = cotangent[here, cols].astype(F32) * gain
             along = jnp.mean(pulled * unit, axis=-1, keepdims=True)
             grad_ref[here, cols] = (scale * (pulled - unit * along)).astype(BF16)
-        rows_here = pl.ds(low, tile)
-        copy = pltpu.make_async_copy(held.at[rows_here, :], normed_ref.at[rows_here, :], sems.at[low // tile])
-        copy.start()
-        outward.append(copy)
     place = lax.broadcasted_iota(jnp.int32, (rows, HEAD_DIM), 0)
     in_first = place < marks_ref[2 * blocks]
     for head in range(width // HEAD_DIM):
@@ -239,8 +234,6 @@
         q = queries[:, cols]
         kept = jnp.where(in_first, q, jnp.zeros_like(q))
         part_ref[cols, :] = dot(kept, grad_ref[:, cols], ROWS).astype(part_ref.dtype)
-    for copy in outward:
-        copy.wait()
 
 
 def grad_q_kernel(blocks, marks_ref, span_ref, packed_ref, grad_ref, state_ref, ended_ref, grad_q_ref):
@@ -285,39 +278,19 @@
 
 
 def last_kernel(
-    blocks, where_ref, marks_ref, packed_ref, part_k_ref, part_v_ref, far_ref, near_ref,
-    grad_k_ref, grad_v_ref, held, sems,
+    blocks, where_ref, marks_ref, packed_ref, part_k_ref, part_v_ref, far_ref, near_ref, grad_k_ref, grad_v_ref
 ):
     keys, values = unpacked(packed_ref, 0), unpacked(packed_ref, 1)
     back = entering(True, blocks, where_ref, marks_ref, far_ref, near_ref)
     rows, width = keys.shape
-    outward = []
-    for low in range(0, rows, TILE):
-        here = slice(low, low + TILE)
-        place = low + lax.broadcasted_iota(jnp.int32, (TILE, HEAD_DIM), 0)
-        later = place >= marks_ref[2 * blocks + 3]
-        for head in range(width // HEAD_DIM):
-            cols = head_cols(head)
-            inter = dot(values[here, cols], back[cols, :], FEATURES)
-            held[0, here, cols] = (part_k_ref[here, cols] + jnp.where(later, inter, 0.0)).astype(BF16)
-            inter = dot(keys[here, cols], back[cols, :], PLAIN)
-            held[1, here, cols] = (part_v_ref[here, cols] + jnp.where(later, inter, 0.0)).astype(BF16)
-        rows_here = pl.ds(low, TILE)
-        for k, out_ref in enumerate((grad_k_ref, grad_v_ref)):
-            copy = pltpu.make_async_copy(
-                held.at[k, rows_here, :], out_ref.at[rows_here, :], sems.at[k, low // TILE]
-            )
-            copy.start()
-            outward.append(copy)
-    for copy in outward:
-        copy.wait()
-
-
-def unpack_kernel(parts_ref, ended_ref, out_ref):
-    ended_ref[...] = jnp.zeros_like(ended_ref)
-    groups, _, width = parts_ref.shape
-    for group in range(groups):
-        out_ref[:, group * width : (group + 1) * width] = parts_ref[group]
+    place = lax.broadcasted_iota(jnp.int32, (rows, HEAD_DIM), 0)
+    later = place >= marks_ref[2 * blocks + 3]
+    for head in range(width // HEAD_DIM):
+        cols = head_cols(head)
+        inter = dot(values[:, cols], back[cols, :], FEATURES)
+        grad_k_ref[:, cols] = (part_k_ref[:, cols] + jnp.where(later, inter, 0.0)).astype(BF16)
+        inter = dot(keys[:, cols], back[cols, :], PLAIN)
+        grad_v_ref[:, cols] = (part_v_ref[:, cols] + jnp.where(later, inter, 0.0)).astype(BF16)
 
 
 SMEM = pl.BlockSpec(memory_space=pltpu.SMEM)
@@ -472,8 +445,6 @@
         [where, marks],
         [packed, inside, gain.reshape(1, cols), *before],
         4 * rows * width * HEAD_DIM,
-        [pltpu.VMEM((rows, width), BF16), pltpu.SemaphoreType.DMA((rows // HEAD_DIM,))],
-        out_specs=[ANYWHERE, VMEM, VMEM, VMEM],
     )
 
     normed = across_head(normed.reshape(groups, tokens, width))
@@ -496,7 +467,6 @@
         4 * square,
         after=[nine],
     )
-    ended, normed = call(unpack_kernel, "unpack", [ENDED, bf16((tokens, cols))], [], [normed], 0)
     grad_k, grad_v = call(
         functools.partial(last_kernel, blocks),
         "last",
@@ -504,11 +474,8 @@
         [where, marks],
         [packed, part_k, part_v, *two_spans(nine, True)],
         4 * rows * width * HEAD_DIM,
-        [pltpu.VMEM((2, rows, width), BF16), pltpu.SemaphoreType.DMA((2, rows // TILE))],
-        after=[ended],
-        out_specs=[ANYWHERE] * 2,
-    )
-    return normed, grad_q, grad_k, grad_v
+    )
+    return normed.transpose(1, 0, 2).reshape(tokens, cols), grad_q, grad_k, grad_v
 
 
 def solution(mesh):

time: 138 us -> 131 us (0.949)
  local copies, waits for them, and re-layouts: 6.47 us -> 2.14 us
  Pallas kernels: 28.9 us -> 26.2 us
    unnamed x22 -> x12, local copies, waits for them, and re-layouts: 6.47 us -> 1.3 us
    pallas_call x15 -> x14, Pallas kernels: 28.9 us -> 26.2 us  [call(): pl.pallas_call(body, name=name, out_shape=outs, in_specs=[SMEM] * len(sca...]
  transfers between devices with their start and end apart: 15 -> 15, of which waited for: 7 -> 7; matrix products, arithmetic and copies ran while one was open for 0% -> 0% of each run, Pallas kernels for 14% -> 16%
where the time goes in v3:
time: 131 us; the launch traced here: 130 us
  starting transfers between devices  83.3 us (64%)
  Pallas kernels  26.2 us (20%)
  waiting for transfers between devices  17.6 us (13%)
  local copies, waits for them, and re-layouts  2.14 us (2%)
    ppermute x12, starting transfers between devices, from_block(): lax.ppermute(field, 'seq', [(at, (at + step) % blocks) for at in range(bl...  67.9 us
    pallas_call x14, Pallas kernels, call(): pl.pallas_call(body, name=name, out_shape=outs, in_specs=[SMEM] * len(sca...  26.2 us
    ppermute x12, waiting for transfers between devices, from_block(): lax.ppermute(field, 'seq', [(at, (at + step) % blocks) for at in range(bl...  16.9 us
    all_to_all x3, starting transfers between devices, across_head(): lax.all_to_all(parts, 'head', split_axis=0, concat_axis=0, tiled=True)  15.4 us
  transfers between devices with their start and end apart: 15, of which 7 were waited for; matrix products, arithmetic and copies ran while one was open for 0% of the time, Pallas kernels for 16%

profile of v3, /device:TPU:10, one launch (start us, length us, event | category | flops | bytes accessed | tf_op | source)
XLA Modules:
  0.0 130.2 jit_solution(4276213149516934228)
XLA Ops:
  0.6 3.6 %parts.1 = (f32[8,128]{1,0:T(8,128)}, bf16[8,256,128]{2,1,0:T(8,128)(2,1)}) custom-call(s32[32]{0:T(128)} %refs_0_.6, s32[1]{0:T(128)} %bitcast.refs_1_, s32[1]{0:T(128)} %bitcast.1.refs_2_, bf16[128,2048]{1,0:T(8,128)(2,1)} %refs_0_.7, bf16[128,2048]{1,0:T(8,128)(2,1)} %refs_1_.1), custom_call_target="tpu_custom_call" | custom-call | flops 67108864 | bytes 1576960 | tf_op jit(solution)/shard_map/parts/pallas_call | solution.py:311
  4.3 4.8 %all-to-all-start.1 = ((bf16[8,256,128]{2,1,0:T(8,128)(2,1)}), bf16[8,256,128]{2,1,0:T(8,128)(2,1)S(1)}, u32[]{:S(2)}, u32[]{:S(2)}) async-start(bf16[8,256,128]{2,1,0:T(8,128)(2,1)} %get-tuple-element.20), calls=%async_computation.1 | async-start | bytes 1048576 | tf_op jit(solution)/shard_map/all_to_all | solution.py:325
  9.9 2.5 %meta.1.refs_2_.refs_0_.refs_1_ = s32[132]{0:T(256)S(1)} custom-call(s32[32]{0:T(128)S(1)} %copy-done.3, s32[2]{0:T(128)S(1)} %pad_add_fusion.refs_1_.refs_0_, f32[8,128]{1,0:T(8,128)S(1)} %copy-done.5), custom_call_target="tpu_custom_call" | custom-call | flops 1024 | bytes 528 | tf_op jit(solution)/shard_map/meta/pallas_call | solution.py:311
  13.9 3.3 %pack.1 = (f32[8,128]{1,0:T(8,128)}, bf16[8,512,256]{2,1,0:T(8,128)(2,1)}) custom-call(bf16[128,2048]{1,0:T(8,128)(2,1)} %refs_0_.7, bf16[128,2048]{1,0:T(8,128)(2,1)} %refs_1_.1, bf16[128,2048]{1,0:T(8,128)(2,1)} %refs_2_.1, bf16[128,2048]{1,0:T(8,128)(2,1)} %refs_3_.3, s32[2,1024]{1,0:T(2,128)} %copy-done), custom_call_target="tpu_custom_call" | custom-call | bytes 4198400 | tf_op jit(solution)/shard_map/pack/pallas_call | solution.py:311
  18.0 5.1 %all-to-all-start = ((bf16[8,512,256]{2,1,0:T(8,128)(2,1)}), bf16[8,512,256]{2,1,0:T(8,128)(2,1)S(1)}, u32[]{:S(2)}, u32[]{:S(2)}) async-start(bf16[8,512,256]{2,1,0:T(8,128)(2,1)} %get-tuple-element.19), calls=%async_computation | async-start | bytes 4194304 | tf_op jit(solution)/shard_map/all_to_all | solution.py:325
  23.7 11.3 %collective-permute-start.1 = (bf16[256,128]{1,0:T(8,128)(2,1)S(1)}, bf16[256,128]{1,0:T(8,128)(2,1)S(1)}, u32[]{:S(2)}, u32[]{:S(2)}) collective-permute-start(bf16[256,128]{1,0:T(8,128)(2,1)S(1)} %tail.1.refs_3_), channel_id=1, source_target_pairs={{0,504},{8,0},{16,8},{24,16},{32,24},{40,32},{48,40},{56,48},{64,5... | collective-permute-start | bytes 196616 | tf_op jit(solution)/shard_map/ppermute | solution.py:353
  35.0 1.9 %collective-permute-start = (bf16[256,128]{1,0:T(8,128)(2,1)S(1)}, bf16[256,128]{1,0:T(8,128)(2,1)S(1)}, u32[]{:S(2)}, u32[]{:S(2)}) collective-permute-start(bf16[256,128]{1,0:T(8,128)(2,1)S(1)} %tail.1.refs_3_), channel_id=1, source_target_pairs={{0,8},{8,16},{16,24},{24,32},{32,40},{40,48},{48,56},{56,64},{64,7... | collective-permute-start | bytes 196616 | tf_op jit(solution)/shard_map/ppermute | solution.py:353
  37.0 6.3 %collective-permute-done.refs_2_ = bf16[256,128]{1,0:T(8,128)(2,1)S(1)} collective-permute-done((bf16[256,128]{1,0:T(8,128)(2,1)S(1)}, bf16[256,128]{1,0:T(8,128)(2,1)S(1)}, u32[]{:S(2)}, u32[]{:S(2)}) %collective-permute-start) | collective-permute-done | bytes 65568 | tf_op jit(solution)/shard_map/ppermute | solution.py:353
  45.8 5.7 %collective-permute-start.2 = (bf16[256,128]{1,0:T(8,128)(2,1)S(1)}, bf16[256,128]{1,0:T(8,128)(2,1)S(1)}, u32[]{:S(2)}, u32[]{:S(2)}) collective-permute-start(bf16[256,128]{1,0:T(8,128)(2,1)S(1)} %three_forward.1.refs_3_), channel_id=1, source_target_pairs={{0,24},{8,32},{16,40},{24,48},{32,56},{40,64},{48,72},{56,80},{64,... | collective-permute-start | bytes 196616 | tf_op jit(solution)/shard_map/ppermute | solution.py:353
  51.9 4.5 %collective-permute-done.2.refs_2_ = bf16[256,128]{1,0:T(8,128)(2,1)S(1)} collective-permute-done((bf16[256,128]{1,0:T(8,128)(2,1)S(1)}, bf16[256,128]{1,0:T(8,128)(2,1)S(1)}, u32[]{:S(2)}, u32[]{:S(2)}) %collective-permute-start.2) | collective-permute-done | bytes 65568 | tf_op jit(solution)/shard_map/ppermute | solution.py:353
  56.9 2.6 %collective-permute-start.5 = (bf16[256,128]{1,0:T(8,128)(2,1)S(1)}, bf16[256,128]{1,0:T(8,128)(2,1)S(1)}, u32[]{:S(2)}, u32[]{:S(2)}) collective-permute-start(bf16[256,128]{1,0:T(8,128)(2,1)S(1)} %nine_forward.1), channel_id=1, source_target_pairs={{0,40},{8,48},{16,56},{24,64},{32,72},{40,80},{48,88},{56,96},{64,... | collective-permute-start | bytes 196616 | tf_op jit(solution)/shard_map/ppermute | solution.py:353
  59.6 7.3 %collective-permute-start.4 = (bf16[256,128]{1,0:T(8,128)(2,1)S(1)}, bf16[256,128]{1,0:T(8,128)(2,1)S(1)}, u32[]{:S(2)}, u32[]{:S(2)}) collective-permute-start(bf16[256,128]{1,0:T(8,128)(2,1)S(1)} %nine_forward.1), channel_id=1, source_target_pairs={{0,112},{8,120},{16,128},{24,136},{32,144},{40,152},{48,160},{56,1... | collective-permute-start | bytes 196616 | tf_op jit(solution)/shard_map/ppermute | solution.py:353
  68.8 3.0 %collective-permute-done.5.refs_6_ = bf16[256,128]{1,0:T(8,128)(2,1)S(1)} collective-permute-done((bf16[256,128]{1,0:T(8,128)(2,1)S(1)}, bf16[256,128]{1,0:T(8,128)(2,1)S(1)}, u32[]{:S(2)}, u32[]{:S(2)}) %collective-permute-start.5) | collective-permute-done | bytes 65568 | tf_op jit(solution)/shard_map/ppermute | solution.py:353
  71.8 2.3 %norm.1 = (bf16[1024,256]{1,0:T(8,128)(2,1)}, bf16[1024,256]{1,0:T(8,128)(2,1)S(1)}, bf16[256,128]{1,0:T(8,128)(2,1)S(1)}, bf16[256,128]{1,0:T(8,128)(2,1)S(1)}) custom-call(s32[2]{0:T(128)S(1)} %pad_add_fusion.refs_1_.refs_0_, s32[132]{0:T(256)S(1)} %meta.1.refs_2_.refs_0_.refs_1_, bf16[8,512,256]{2,1,0:T(8,128)(2,1)S(1)} %all-to-all-done.refs_1_.refs_2_, ...), custom_call_target="tpu_custom_call" | custom-call | flops 134217728 | bytes 4464640 | tf_op jit(solution)/shard_map/norm/pallas_call | solution.py:311
  74.1 5.4 %all-to-all-start.2 = ((bf16[8,128,256]{2,1,0:T(8,128)(2,1)}), bf16[8,128,256]{2,1,0:T(8,128)(2,1)S(1)}, u32[]{:S(2)}, u32[]{:S(2)}) async-start(bf16[8,128,256]{2,1,0:T(8,128)(2,1)} %bitcast.3), calls=%async_computation.2 | async-start | bytes 1048576 | tf_op jit(solution)/shard_map/all_to_all | solution.py:325
  79.6 3.0 %collective-permute-start.7 = (bf16[256,128]{1,0:T(8,128)(2,1)S(1)}, bf16[256,128]{1,0:T(8,128)(2,1)S(1)}, u32[]{:S(2)}, u32[]{:S(2)}) collective-permute-start(bf16[256,128]{1,0:T(8,128)(2,1)S(1)} %get-tuple-element.26.refs_3_), channel_id=1, source_target_pairs={{0,8},{8,16},{16,24},{24,32},{32,40},{40,48},{48,56},{56,64},{64,7... | collective-permute-start | bytes 196616 | tf_op jit(solution)/shard_map/ppermute | solution.py:353
  82.5 5.0 %collective-permute-start.6 = (bf16[256,128]{1,0:T(8,128)(2,1)S(1)}, bf16[256,128]{1,0:T(8,128)(2,1)S(1)}, u32[]{:S(2)}, u32[]{:S(2)}) collective-permute-start(bf16[256,128]{1,0:T(8,128)(2,1)S(1)} %get-tuple-element.26.refs_3_), channel_id=1, source_target_pairs={{0,504},{8,0},{16,8},{24,16},{32,24},{40,32},{48,40},{56,48},{64,5... | collective-permute-start | bytes 196616 | tf_op jit(solution)/shard_map/ppermute | solution.py:353
  87.5 3.2 %grads_q.1 = (f32[8,128]{1,0:T(8,128)S(1)}, bf16[1024,256]{1,0:T(8,128)(2,1)}) custom-call(s32[132]{0:T(256)S(1)} %meta.1.refs_2_.refs_0_.refs_1_, s32[2,1024]{1,0:T(2,128)S(1)} %copy-done.1, bf16[8,512,256]{2,1,0:T(8,128)(2,1)S(1)} %all-to-all-done.refs_1_.refs_2_, bf16[1024,256]{1,0:T(8,128)(2,1)S(1)} %get-tuple-element.23.refs_3_.refs_2_, ...), custom_call_target="tpu_custom_call" | custom-call | flops 536870912 | bytes 3223552 | tf_op jit(solution)/shard_map/grads_q/pallas_call | solution.py:311
  91.3 2.6 %collective-permute-start.9 = (bf16[256,128]{1,0:T(8,128)(2,1)S(1)}, bf16[256,128]{1,0:T(8,128)(2,1)S(1)}, u32[]{:S(2)}, u32[]{:S(2)}) collective-permute-start(bf16[256,128]{1,0:T(8,128)(2,1)S(1)} %three_back.1.refs_3_), channel_id=1, source_target_pairs={{0,24},{8,32},{16,40},{24,48},{32,56},{40,64},{48,72},{56,80},{64,... | collective-permute-start | bytes 196616 | tf_op jit(solution)/shard_map/ppermute | solution.py:353
  93.9 7.2 %collective-permute-start.8 = (bf16[256,128]{1,0:T(8,128)(2,1)S(1)}, bf16[256,128]{1,0:T(8,128)(2,1)S(1)}, u32[]{:S(2)}, u32[]{:S(2)}) collective-permute-start(bf16[256,128]{1,0:T(8,128)(2,1)S(1)} %three_back.1.refs_3_), channel_id=1, source_target_pairs={{0,488},{8,496},{16,504},{24,0},{32,8},{40,16},{48,24},{56,32},{64... | collective-permute-start | bytes 196616 | tf_op jit(solution)/shard_map/ppermute | solution.py:353
  104.5 6.8 %collective-permute-start.11 = (bf16[256,128]{1,0:T(8,128)(2,1)S(1)}, bf16[256,128]{1,0:T(8,128)(2,1)S(1)}, u32[]{:S(2)}, u32[]{:S(2)}) collective-permute-start(bf16[256,128]{1,0:T(8,128)(2,1)S(1)} %nine_back.1.refs_3_), channel_id=1, source_target_pairs={{0,472},{8,480},{16,488},{24,496},{32,504},{40,0},{48,8},{56,16},{... | collective-permute-start | bytes 196616 | tf_op jit(solution)/shard_map/ppermute | solution.py:353
  111.2 12.7 %collective-permute-start.10 = (bf16[256,128]{1,0:T(8,128)(2,1)S(1)}, bf16[256,128]{1,0:T(8,128)(2,1)S(1)}, u32[]{:S(2)}, u32[]{:S(2)}) collective-permute-start(bf16[256,128]{1,0:T(8,128)(2,1)S(1)} %nine_back.1.refs_3_), channel_id=1, source_target_pairs={{0,400},{8,408},{16,416},{24,424},{32,432},{40,440},{48,448},{56,4... | collective-permute-start | bytes 196616 | tf_op jit(solution)/shard_map/ppermute | solution.py:353
  124.0 3.3 %grads_kv.1 = (f32[1024,256]{1,0:T(8,128)S(1)}, f32[1024,256]{1,0:T(8,128)S(1)}) custom-call(s32[2,1024]{1,0:T(2,128)S(1)} %copy-done.1, bf16[8,512,256]{2,1,0:T(8,128)(2,1)S(1)} %all-to-all-done.refs_1_.refs_2_, bf16[1024,256]{1,0:T(8,128)(2,1)S(1)} %get-tuple-element.23.refs_3_.refs_2_, bf16[256,128]{1,0:T(8,128)(2,1)S(1)} %nine_back.1.refs_3_), custom_call_target="tpu_custom_call" | custom-call | flops 1073741824 | bytes 4726784 | tf_op jit(solution)/shard_map/grads_kv/pallas_call | solution.py:311
  127.3 2.0 %last.1 = (bf16[1024,256]{1,0:T(8,128)(2,1)}, bf16[1024,256]{1,0:T(8,128)(2,1)}) custom-call(s32[2]{0:T(128)S(1)} %pad_add_fusion.refs_1_.refs_0_, s32[132]{0:T(256)S(1)} %meta.1.refs_2_.refs_0_.refs_1_, bf16[8,512,256]{2,1,0:T(8,128)(2,1)S(1)} %all-to-all-done.refs_1_.refs_2_, f32[1024,256]{1,0:T(8,128)S(1)} %get-tuple-element.28.refs_3_, ...), custom_call_target="tpu_custom_call" | custom-call | flops 134217728 | bytes 5373952 | tf_op jit(solution)/shard_map/last/pallas_call | solution.py:311
  (34 shorter events, 13.8 us)
Async XLA Ops:
  0.6 8.5 %copy-start.3 = (s32[32]{0:T(128)S(1)}, s32[32]{0:T(128)}, u32[]{:S(2)}) copy-start(s32[32]{0:T(128)} %refs_0_.6) | copy-start | bytes 388
  4.3 13.7 %all-to-all-start.1 = ((bf16[8,256,128]{2,1,0:T(8,128)(2,1)}), bf16[8,256,128]{2,1,0:T(8,128)(2,1)S(1)}, u32[]{:S(2)}, u32[]{:S(2)}) async-start(bf16[8,256,128]{2,1,0:T(8,128)(2,1)} %get-tuple-element.20), calls=%async_computation.1 | async-start | bytes 1048576 | tf_op jit(solution)/shard_map/all_to_all | solution.py:325
  9.2 0.7 copy-start.5
  13.3 0.6 copy-start
  18.0 5.1 %copy-start.4 = (f32[8,128]{1,0:T(8,128)S(1)}, f32[8,128]{1,0:T(8,128)}, u32[]{:S(2)}) copy-start(f32[8,128]{1,0:T(8,128)} %get-tuple-element.21.refs_2_) | copy-start | bytes 12292
  18.0 48.8 %copy-start.1 = (s32[2,1024]{1,0:T(2,128)S(1)}, s32[2,1024]{1,0:T(2,128)}, u32[]{:S(2)}) copy-start(s32[2,1024]{1,0:T(2,128)} %copy-done) | copy-start | bytes 24580
  18.0 48.8 %all-to-all-start = ((bf16[8,512,256]{2,1,0:T(8,128)(2,1)}), bf16[8,512,256]{2,1,0:T(8,128)(2,1)S(1)}, u32[]{:S(2)}, u32[]{:S(2)}) async-start(bf16[8,512,256]{2,1,0:T(8,128)(2,1)} %get-tuple-element.19), calls=%async_computation | async-start | bytes 4194304 | tf_op jit(solution)/shard_map/all_to_all | solution.py:325
  23.1 48.7 %copy-start.2 = (f32[2048]{0:T(1024)S(1)}, f32[2048]{0:T(1024)}, u32[]{:S(2)}) copy-start(f32[2048]{0:T(1024)} %param.10) | copy-start | bytes 24580
  23.7 13.2 %collective-permute-start.1 = (bf16[256,128]{1,0:T(8,128)(2,1)S(1)}, bf16[256,128]{1,0:T(8,128)(2,1)S(1)}, u32[]{:S(2)}, u32[]{:S(2)}) collective-permute-start(bf16[256,128]{1,0:T(8,128)(2,1)S(1)} %tail.1.refs_3_), channel_id=1, source_target_pairs={{0,504},{8,0},{16,8},{24,16},{32,24},{40,32},{48,40},{56,48},{64,5... | collective-permute-start | bytes 196616 | tf_op jit(solution)/shard_map/ppermute | solution.py:353
  35.0 8.3 %collective-permute-start = (bf16[256,128]{1,0:T(8,128)(2,1)S(1)}, bf16[256,128]{1,0:T(8,128)(2,1)S(1)}, u32[]{:S(2)}, u32[]{:S(2)}) collective-permute-start(bf16[256,128]{1,0:T(8,128)(2,1)S(1)} %tail.1.refs_3_), channel_id=1, source_target_pairs={{0,8},{8,16},{16,24},{24,32},{32,40},{40,48},{48,56},{56,64},{64,7... | collective-permute-start | bytes 196616 | tf_op jit(solution)/shard_map/ppermute | solution.py:353
  43.9 8.0 %collective-permute-start.3 = (bf16[256,128]{1,0:T(8,128)(2,1)S(1)}, bf16[256,128]{1,0:T(8,128)(2,1)S(1)}, u32[]{:S(2)}, u32[]{:S(2)}) collective-permute-start(bf16[256,128]{1,0:T(8,128)(2,1)S(1)} %three_forward.1.refs_3_), channel_id=1, source_target_pairs={{0,488},{8,496},{16,504},{24,0},{32,8},{40,16},{48,24},{56,32},{64... | collective-permute-start | bytes 196616 | tf_op jit(solution)/shard_map/ppermute | solution.py:353
  45.8 10.5 %collective-permute-start.2 = (bf16[256,128]{1,0:T(8,128)(2,1)S(1)}, bf16[256,128]{1,0:T(8,128)(2,1)S(1)}, u32[]{:S(2)}, u32[]{:S(2)}) collective-permute-start(bf16[256,128]{1,0:T(8,128)(2,1)S(1)} %three_forward.1.refs_3_), channel_id=1, source_target_pairs={{0,24},{8,32},{16,40},{24,48},{32,56},{40,64},{48,72},{56,80},{64,... | collective-permute-start | bytes 196616 | tf_op jit(solution)/shard_map/ppermute | solution.py:353
  56.9 14.9 %collective-permute-start.5 = (bf16[256,128]{1,0:T(8,128)(2,1)S(1)}, bf16[256,128]{1,0:T(8,128)(2,1)S(1)}, u32[]{:S(2)}, u32[]{:S(2)}) collective-permute-start(bf16[256,128]{1,0:T(8,128)(2,1)S(1)} %nine_forward.1), channel_id=1, source_target_pairs={{0,40},{8,48},{16,56},{24,64},{32,72},{40,80},{48,88},{56,96},{64,... | collective-permute-start | bytes 196616 | tf_op jit(solution)/shard_map/ppermute | solution.py:353
  59.6 12.2 %collective-permute-start.4 = (bf16[256,128]{1,0:T(8,128)(2,1)S(1)}, bf16[256,128]{1,0:T(8,128)(2,1)S(1)}, u32[]{:S(2)}, u32[]{:S(2)}) collective-permute-start(bf16[256,128]{1,0:T(8,128)(2,1)S(1)} %nine_forward.1), channel_id=1, source_target_pairs={{0,112},{8,120},{16,128},{24,136},{32,144},{40,152},{48,160},{56,1... | collective-permute-start | bytes 196616 | tf_op jit(solution)/shard_map/ppermute | solution.py:353
  74.1 55.2 %all-to-all-start.2 = ((bf16[8,128,256]{2,1,0:T(8,128)(2,1)}), bf16[8,128,256]{2,1,0:T(8,128)(2,1)S(1)}, u32[]{:S(2)}, u32[]{:S(2)}) async-start(bf16[8,128,256]{2,1,0:T(8,128)(2,1)} %bitcast.3), calls=%async_computation.2 | async-start | bytes 1048576 | tf_op jit(solution)/shard_map/all_to_all | solution.py:325
  79.6 11.2 %collective-permute-start.7 = (bf16[256,128]{1,0:T(8,128)(2,1)S(1)}, bf16[256,128]{1,0:T(8,128)(2,1)S(1)}, u32[]{:S(2)}, u32[]{:S(2)}) collective-permute-start(bf16[256,128]{1,0:T(8,128)(2,1)S(1)} %get-tuple-element.26.refs_3_), channel_id=1, source_target_pairs={{0,8},{8,16},{16,24},{24,32},{32,40},{40,48},{48,56},{56,64},{64,7... | collective-permute-start | bytes 196616 | tf_op jit(solution)/shard_map/ppermute | solution.py:353
  82.5 8.2 %collective-permute-start.6 = (bf16[256,128]{1,0:T(8,128)(2,1)S(1)}, bf16[256,128]{1,0:T(8,128)(2,1)S(1)}, u32[]{:S(2)}, u32[]{:S(2)}) collective-permute-start(bf16[256,128]{1,0:T(8,128)(2,1)S(1)} %get-tuple-element.26.refs_3_), channel_id=1, source_target_pairs={{0,504},{8,0},{16,8},{24,16},{32,24},{40,32},{48,40},{56,48},{64,5... | collective-permute-start | bytes 196616 | tf_op jit(solution)/shard_map/ppermute | solution.py:353
  91.3 10.8 %collective-permute-start.9 = (bf16[256,128]{1,0:T(8,128)(2,1)S(1)}, bf16[256,128]{1,0:T(8,128)(2,1)S(1)}, u32[]{:S(2)}, u32[]{:S(2)}) collective-permute-start(bf16[256,128]{1,0:T(8,128)(2,1)S(1)} %three_back.1.refs_3_), channel_id=1, source_target_pairs={{0,24},{8,32},{16,40},{24,48},{32,56},{40,64},{48,72},{56,80},{64,... | collective-permute-start | bytes 196616 | tf_op jit(solution)/shard_map/ppermute | solution.py:353
  93.9 9.9 %collective-permute-start.8 = (bf16[256,128]{1,0:T(8,128)(2,1)S(1)}, bf16[256,128]{1,0:T(8,128)(2,1)S(1)}, u32[]{:S(2)}, u32[]{:S(2)}) collective-permute-start(bf16[256,128]{1,0:T(8,128)(2,1)S(1)} %three_back.1.refs_3_), channel_id=1, source_target_pairs={{0,488},{8,496},{16,504},{24,0},{32,8},{40,16},{48,24},{56,32},{64... | collective-permute-start | bytes 196616 | tf_op jit(solution)/shard_map/ppermute | solution.py:353
  104.5 22.8 %collective-permute-start.11 = (bf16[256,128]{1,0:T(8,128)(2,1)S(1)}, bf16[256,128]{1,0:T(8,128)(2,1)S(1)}, u32[]{:S(2)}, u32[]{:S(2)}) collective-permute-start(bf16[256,128]{1,0:T(8,128)(2,1)S(1)} %nine_back.1.refs_3_), channel_id=1, source_target_pairs={{0,472},{8,480},{16,488},{24,496},{32,504},{40,0},{48,8},{56,16},{... | collective-permute-start | bytes 196616 | tf_op jit(solution)/shard_map/ppermute | solution.py:353
  111.2 16.1 %collective-permute-start.10 = (bf16[256,128]{1,0:T(8,128)(2,1)S(1)}, bf16[256,128]{1,0:T(8,128)(2,1)S(1)}, u32[]{:S(2)}, u32[]{:S(2)}) collective-permute-start(bf16[256,128]{1,0:T(8,128)(2,1)S(1)} %nine_back.1.refs_3_), channel_id=1, source_target_pairs={{0,400},{8,408},{16,416},{24,424},{32,432},{40,440},{48,448},{56,4... | collective-permute-start | bytes 196616 | tf_op jit(solution)/shard_map/ppermute | solution.py:353

commit v4 on v3

--- a/solution.py
+++ b/solution.py
@@ -115,14 +115,12 @@
             part.wait()
 
 
-def parts_kernel(
-    lengths_ref, seq_ref, head_ref, keys_ref, values_ref, ended_ref, out_ref, held, sums, in_sems, out_sems
-):
-    inward = [
-        pltpu.make_async_copy(ref, held.at[k], in_sems.at[k])
+def parts_kernel(lengths_ref, seq_ref, head_ref, keys_ref, values_ref, ended_ref, out_ref, held, sems):
+    copies = [
+        pltpu.make_async_copy(ref, held.at[k], sems.at[k])
         for k, ref in enumerate((keys_ref, values_ref))
     ]
-    for copy in inward:
+    for copy in copies:
         copy.start()
     ended_ref[...] = jnp.zeros_like(ended_ref)
     groups, width, _ = out_ref.shape
@@ -133,22 +131,15 @@
         bound = jnp.where(begin <= last, begin, bound)
         begin = begin + lengths_ref[i]
     mine = last + 1 - (groups - head_ref[0]) * tokens
-    place = mine + lax.broadcasted_iota(jnp.int32, (tokens, HEAD_DIM), 0)
-    for copy in inward:
+    for copy in copies:
         copy.wait()
-    outward = []
-    for group in range(groups):
-        for head in range(width // HEAD_DIM):
-            at = slice(group * width + head * HEAD_DIM, group * width + (head + 1) * HEAD_DIM)
-            keys = held[0, :, at]
-            keys = jnp.where(place >= bound, keys, jnp.zeros_like(keys))
-            part = dot(keys, held[1, :, at], ROWS)
-            sums[group, head_cols(head), :] = part.astype(sums.dtype)
-        copy = pltpu.make_async_copy(sums.at[group], out_ref.at[group], out_sems.at[group])
-        copy.start()
-        outward.append(copy)
-    for copy in outward:
-        copy.wait()
+    place = mine + lax.broadcasted_iota(jnp.int32, (tokens, cols), 0)
+    keys = held[0]
+    keys = jnp.where(place >= bound, keys, jnp.zeros_like(keys))
+    for head in range(cols // HEAD_DIM):
+        part = dot(keys[:, head_cols(head)], held[1, :, head_cols(head)], ROWS)
+        group, at = divmod(head * HEAD_DIM, width)
+        out_ref[group, at : at + HEAD_DIM, :] = part.astype(out_ref.dtype)
 
 
 def tail_kernel(marks_ref, parts_ref, tail_ref):
@@ -257,24 +248,30 @@
             grad_q_ref[low:high, cols] = grad_q.astype(BF16)
 
 
-def grad_kv_kernel(span_ref, packed_ref, grad_ref, part_k_ref, part_v_ref):
-    keys, values, queries = (unpacked(packed_ref, at) for at in range(3))
-    rows, width = keys.shape
+def turned_kernel(docs_ref, left_ref, right_ref, rows_ref, ended_ref, part_ref):
+    ended_ref[...] = jnp.zeros_like(ended_ref)
+    left, right, summed = (
+        unpacked(*field) if isinstance(field, tuple) else field for field in (left_ref, right_ref, rows_ref)
+    )
+    rows, width = part_ref.shape
     for low in range(0, rows, TILE):
         high = low + TILE
         row = low + lax.broadcasted_iota(jnp.int32, (TILE, rows - low), 0)
         column = low + lax.broadcasted_iota(jnp.int32, (TILE, rows - low), 1)
-        mask = (row <= column) & (row >= span_ref[0:1, low:])
+        mask = (row <= column) & (row >= docs_ref[0:1, low:])
         for head in range(width // HEAD_DIM):
             cols = head_cols(head)
-            q, k, v = (field[:, cols] for field in (queries, keys, values))
-            grad = grad_ref[:, cols]
-            turned = dot(v[low:high], grad[low:], FEATURES)
+            turned = dot(left[low:high, cols], right[low:, cols], FEATURES)
             turned = jnp.where(mask, turned, 0.0).astype(BF16)
-            part_k_ref[low:high, cols] = dot(turned, q[low:], PLAIN)
-            turned = dot(k[low:high], q[low:], FEATURES)
-            turned = jnp.where(mask, turned, 0.0).astype(BF16)
-            part_v_ref[low:high, cols] = dot(turned, grad[low:], PLAIN)
+            part_ref[low:high, cols] = dot(turned, summed[low:, cols], PLAIN)
+
+
+def grad_k_kernel(docs_ref, packed_ref, grad_ref, ended_ref, part_ref):
+    turned_kernel(docs_ref, (packed_ref, 1), grad_ref, (packed_ref, 2), ended_ref, part_ref)
+
+
+def grad_v_kernel(docs_ref, packed_ref, grad_ref, ended_ref, part_ref):
+    turned_kernel(docs_ref, (packed_ref, 0), (packed_ref, 2), grad_ref, ended_ref, part_ref)
 
 
 def last_kernel(
@@ -348,9 +345,16 @@
     return ended, packed
 
 
-def from_block(field, step):
+def from_block(field, step, reach, reverse):
     blocks = lax.axis_size("seq")
-    return lax.ppermute(field, "seq", [(at, (at + step) % blocks) for at in range(blocks)])
+    pairs = []
+    for at in range(blocks):
+        to = at + step
+        if to < blocks or to - blocks - step + reach >= 0:
+            pairs.append((at, to % blocks))
+    if reverse:
+        pairs = [(blocks - 1 - at, blocks - 1 - to) for at, to in pairs]
+    return lax.ppermute(field, "seq", pairs)
 
 
 def span(kernel, parts, where, marks, reverse, after=()):
@@ -367,22 +371,17 @@
 
 
 def span_of_three(part, where, marks, reverse, after=()):
-    parts = [from_block(part, 1), part, from_block(part, -1)]
-    if reverse:
-        parts.reverse()
+    parts = [from_block(part, 1, 0, reverse), part, from_block(part, -1, 0, reverse)]
     return span(three_kernel, parts, where, marks, reverse, after)
 
 
 def span_of_nine(three, where, marks, reverse, after=()):
-    parts = [from_block(three, 3), three, from_block(three, -3)]
-    if reverse:
-        parts.reverse()
+    parts = [from_block(three, 3, 1, reverse), three, from_block(three, -3, 1, reverse)]
     return span(nine_kernel, parts, where, marks, reverse, after)
 
 
 def two_spans(nine, reverse):
-    sign = -1 if reverse else 1
-    return [from_block(nine, sign * 14), from_block(nine, sign * 5)]
+    return [from_block(nine, 14, 4, reverse), from_block(nine, 5, 4, reverse)]
 
 
 def on_device(queries, keys, values, cotangent, gain, lengths):
@@ -404,12 +403,9 @@
         2 * tokens * cols * HEAD_DIM,
         [
             pltpu.VMEM((2, tokens, cols), BF16),
-            pltpu.VMEM((groups, width, HEAD_DIM), BF16),
             pltpu.SemaphoreType.DMA((2,)),
-            pltpu.SemaphoreType.DMA((groups,)),
         ],
         in_specs=[ANYWHERE] * 2,
-        out_specs=[VMEM, ANYWHERE],
         limit=60,
     )
     (marks,) = call(
@@ -457,16 +453,14 @@
         2 * square,
     )
     three = span_of_three(part, where, marks, True, [ended])
-    nine = span_of_nine(three, where, marks, True)
-    part_k, part_v = call(
-        grad_kv_kernel,
-        "grads_kv",
-        [f32((rows, width)), f32((rows, width))],
-        [],
-        [docs, packed, grad],
-        4 * square,
-        after=[nine],
-    )
+
+    def turned(kernel, name, after):
+        outs = [ENDED, f32((rows, width))]
+        return call(kernel, name, outs, [], [docs, packed, grad], 2 * square, after=[after])
+
+    ended, part_k = turned(grad_k_kernel, "grads_k", three)
+    nine = span_of_nine(three, where, marks, True, [ended])
+    _, part_v = turned(grad_v_kernel, "grads_v", nine)
     grad_k, grad_v = call(
         functools.partial(last_kernel, blocks),
         "last",

time: 131 us -> 125 us (0.954)
  the two profiles are of different devices: /device:TPU:10 before, /device:TPU:1 now
where the time goes in v4:
time: 125 us; the launch traced here: 124 us
  starting transfers between devices  85.3 us (68%)
  Pallas kernels  26.6 us (21%)
  waiting for transfers between devices  8.86 us (7%)
  local copies, waits for them, and re-layouts  2.14 us (2%)
    ppermute x12, starting transfers between devices, from_block(): return lax.ppermute(field, 'seq', pairs)  61.6 us
    pallas_call x15, Pallas kernels, call(): pl.pallas_call(body, name=name, out_shape=outs, in_specs=[SMEM] * len(sca...  26.6 us
    all_to_all x3, starting transfers between devices, across_head(): lax.all_to_all(parts, 'head', split_axis=0, concat_axis=0, tiled=True)  23.7 us
    ppermute x12, waiting for transfers between devices, from_block(): return lax.ppermute(field, 'seq', pairs)  7.59 us
  transfers between devices with their start and end apart: 15, of which 6 were waited for; matrix products, arithmetic and copies ran while one was open for 0% of the time, Pallas kernels for 17%

profile of v4, /device:TPU:1, one launch (start us, length us, event | category | flops | bytes accessed | tf_op | source)
XLA Modules:
  0.0 123.8 jit_solution(8805112916083493420)
XLA Ops:
  0.6 3.1 %parts.1 = (f32[8,128]{1,0:T(8,128)}, bf16[8,256,128]{2,1,0:T(8,128)(2,1)}) custom-call(s32[32]{0:T(128)} %refs_0_.6, s32[1]{0:T(128)} %bitcast.refs_1_, s32[1]{0:T(128)} %bitcast.1.refs_2_, bf16[128,2048]{1,0:T(8,128)(2,1)} %refs_0_.7, bf16[128,2048]{1,0:T(8,128)(2,1)} %refs_1_.1), custom_call_target="tpu_custom_call" | custom-call | flops 67108864 | bytes 1576960 | tf_op jit(solution)/shard_map/parts/pallas_call | solution.py:308
  3.7 10.3 %all-to-all-start.1 = ((bf16[8,256,128]{2,1,0:T(8,128)(2,1)}), bf16[8,256,128]{2,1,0:T(8,128)(2,1)S(1)}, u32[]{:S(2)}, u32[]{:S(2)}) async-start(bf16[8,256,128]{2,1,0:T(8,128)(2,1)} %get-tuple-element.21), calls=%async_computation.1 | async-start | bytes 1048576 | tf_op jit(solution)/shard_map/all_to_all | solution.py:322
  14.8 2.5 %meta.1.refs_2_.refs_0_.refs_1_ = s32[132]{0:T(256)S(1)} custom-call(s32[32]{0:T(128)S(1)} %copy-done.3, s32[2]{0:T(128)S(1)} %pad_add_fusion.refs_1_.refs_0_, f32[8,128]{1,0:T(8,128)S(1)} %copy-done.5), custom_call_target="tpu_custom_call" | custom-call | flops 1024 | bytes 528 | tf_op jit(solution)/shard_map/meta/pallas_call | solution.py:308
  18.9 3.4 %pack.1 = (f32[8,128]{1,0:T(8,128)}, bf16[8,512,256]{2,1,0:T(8,128)(2,1)}) custom-call(bf16[128,2048]{1,0:T(8,128)(2,1)} %refs_0_.7, bf16[128,2048]{1,0:T(8,128)(2,1)} %refs_1_.1, bf16[128,2048]{1,0:T(8,128)(2,1)} %refs_2_.1, bf16[128,2048]{1,0:T(8,128)(2,1)} %refs_3_.3, s32[2,1024]{1,0:T(2,128)} %copy-done), custom_call_target="tpu_custom_call" | custom-call | bytes 4198400 | tf_op jit(solution)/shard_map/pack/pallas_call | solution.py:308
  23.5 4.5 %all-to-all-start = ((bf16[8,512,256]{2,1,0:T(8,128)(2,1)}), bf16[8,512,256]{2,1,0:T(8,128)(2,1)S(1)}, u32[]{:S(2)}, u32[]{:S(2)}) async-start(bf16[8,512,256]{2,1,0:T(8,128)(2,1)} %get-tuple-element.20), calls=%async_computation | async-start | bytes 4194304 | tf_op jit(solution)/shard_map/all_to_all | solution.py:322
  28.7 9.1 %collective-permute-start.1 = (bf16[256,128]{1,0:T(8,128)(2,1)S(1)}, bf16[256,128]{1,0:T(8,128)(2,1)S(1)}, u32[]{:S(2)}, u32[]{:S(2)}) collective-permute-start(bf16[256,128]{1,0:T(8,128)(2,1)S(1)} %tail.1.refs_3_), channel_id=1, source_target_pairs={{0,504},{8,0},{16,8},{24,16},{32,24},{40,32},{48,40},{56,48},{64,5... | collective-permute-start | bytes 196616 | tf_op jit(solution)/shard_map/ppermute | solution.py:357
  39.1 1.3 %collective-permute-done.refs_2_ = bf16[256,128]{1,0:T(8,128)(2,1)S(1)} collective-permute-done((bf16[256,128]{1,0:T(8,128)(2,1)S(1)}, bf16[256,128]{1,0:T(8,128)(2,1)S(1)}, u32[]{:S(2)}, u32[]{:S(2)}) %collective-permute-start) | collective-permute-done | bytes 65568 | tf_op jit(solution)/shard_map/ppermute | solution.py:357
  41.0 6.9 %collective-permute-start.3 = (bf16[256,128]{1,0:T(8,128)(2,1)S(1)}, bf16[256,128]{1,0:T(8,128)(2,1)S(1)}, u32[]{:S(2)}, u32[]{:S(2)}) collective-permute-start(bf16[256,128]{1,0:T(8,128)(2,1)S(1)} %three_forward.1.refs_3_), channel_id=1, source_target_pairs={{0,488},{8,496},{16,504},{24,0},{32,8},{40,16},{48,24},{56,32},{64... | collective-permute-start | bytes 196616 | tf_op jit(solution)/shard_map/ppermute | solution.py:357
  51.0 10.9 %collective-permute-start.5 = (bf16[256,128]{1,0:T(8,128)(2,1)S(1)}, bf16[256,128]{1,0:T(8,128)(2,1)S(1)}, u32[]{:S(2)}, u32[]{:S(2)}) collective-permute-start(bf16[256,128]{1,0:T(8,128)(2,1)S(1)} %nine_forward.1), channel_id=1, source_target_pairs={{0,40},{8,48},{16,56},{24,64},{32,72},{40,80},{48,88},{56,96},{64,... | collective-permute-start | bytes 196616 | tf_op jit(solution)/shard_map/ppermute | solution.py:357
  62.0 1.7 %collective-permute-start.4 = (bf16[256,128]{1,0:T(8,128)(2,1)S(1)}, bf16[256,128]{1,0:T(8,128)(2,1)S(1)}, u32[]{:S(2)}, u32[]{:S(2)}) collective-permute-start(bf16[256,128]{1,0:T(8,128)(2,1)S(1)} %nine_forward.1), channel_id=1, source_target_pairs={{0,112},{8,120},{16,128},{24,136},{32,144},{40,152},{48,160},{56,1... | collective-permute-start | bytes 196616 | tf_op jit(solution)/shard_map/ppermute | solution.py:357
  63.7 1.9 %intra.1.refs_3_ = f32[1024,256]{1,0:T(8,128)S(1)} custom-call(s32[2,1024]{1,0:T(2,128)S(1)} %copy-done.1, bf16[8,512,256]{2,1,0:T(8,128)(2,1)S(1)} %all-to-all-done.refs_1_.refs_2_), custom_call_target="tpu_custom_call" | custom-call | flops 536870912 | bytes 3153920 | tf_op jit(solution)/shard_map/intra/pallas_call | solution.py:308
  65.7 2.3 %norm.1 = (bf16[1024,256]{1,0:T(8,128)(2,1)}, bf16[1024,256]{1,0:T(8,128)(2,1)S(1)}, bf16[256,128]{1,0:T(8,128)(2,1)S(1)}, bf16[256,128]{1,0:T(8,128)(2,1)S(1)}) custom-call(s32[2]{0:T(128)S(1)} %pad_add_fusion.refs_1_.refs_0_, s32[132]{0:T(256)S(1)} %meta.1.refs_2_.refs_0_.refs_1_, bf16[8,512,256]{2,1,0:T(8,128)(2,1)S(1)} %all-to-all-done.refs_1_.refs_2_, ...), custom_call_target="tpu_custom_call" | custom-call | flops 134217728 | bytes 4464640 | tf_op jit(solution)/shard_map/norm/pallas_call | solution.py:308
  68.0 8.9 %all-to-all-start.2 = ((bf16[8,128,256]{2,1,0:T(8,128)(2,1)}), bf16[8,128,256]{2,1,0:T(8,128)(2,1)S(1)}, u32[]{:S(2)}, u32[]{:S(2)}) async-start(bf16[8,128,256]{2,1,0:T(8,128)(2,1)} %bitcast.3), calls=%async_computation.2 | async-start | bytes 1048576 | tf_op jit(solution)/shard_map/all_to_all | solution.py:322
  76.9 2.4 %collective-permute-start.7 = (bf16[256,128]{1,0:T(8,128)(2,1)S(1)}, bf16[256,128]{1,0:T(8,128)(2,1)S(1)}, u32[]{:S(2)}, u32[]{:S(2)}) collective-permute-start(bf16[256,128]{1,0:T(8,128)(2,1)S(1)} %get-tuple-element.27.refs_3_), channel_id=1, source_target_pairs={{504,0},{496,504},{488,496},{480,488},{472,480},{464,472},{456,464... | collective-permute-start | bytes 196616 | tf_op jit(solution)/shard_map/ppermute | solution.py:357
  80.6 3.2 %grads_q.1 = (f32[8,128]{1,0:T(8,128)S(1)}, bf16[1024,256]{1,0:T(8,128)(2,1)}) custom-call(s32[132]{0:T(256)S(1)} %meta.1.refs_2_.refs_0_.refs_1_, s32[2,1024]{1,0:T(2,128)S(1)} %copy-done.1, bf16[8,512,256]{2,1,0:T(8,128)(2,1)S(1)} %all-to-all-done.refs_1_.refs_2_, bf16[1024,256]{1,0:T(8,128)(2,1)S(1)} %get-tuple-element.24.refs_3_.refs_2_, ...), custom_call_target="tpu_custom_call" | custom-call | flops 536870912 | bytes 3223552 | tf_op jit(solution)/shard_map/grads_q/pallas_call | solution.py:308
  83.8 3.4 %collective-permute-done.7.refs_4_ = bf16[256,128]{1,0:T(8,128)(2,1)S(1)} collective-permute-done((bf16[256,128]{1,0:T(8,128)(2,1)S(1)}, bf16[256,128]{1,0:T(8,128)(2,1)S(1)}, u32[]{:S(2)}, u32[]{:S(2)}) %collective-permute-start.7) | collective-permute-done | bytes 65568 | tf_op jit(solution)/shard_map/ppermute | solution.py:357
  87.2 1.6 %collective-permute-done.6.refs_2_ = bf16[256,128]{1,0:T(8,128)(2,1)S(1)} collective-permute-done((bf16[256,128]{1,0:T(8,128)(2,1)S(1)}, bf16[256,128]{1,0:T(8,128)(2,1)S(1)}, u32[]{:S(2)}, u32[]{:S(2)}) %collective-permute-start.6) | collective-permute-done | bytes 65568 | tf_op jit(solution)/shard_map/ppermute | solution.py:357
  89.4 4.3 %collective-permute-start.9 = (bf16[256,128]{1,0:T(8,128)(2,1)S(1)}, bf16[256,128]{1,0:T(8,128)(2,1)S(1)}, u32[]{:S(2)}, u32[]{:S(2)}) collective-permute-start(bf16[256,128]{1,0:T(8,128)(2,1)S(1)} %three_back.1.refs_3_), channel_id=1, source_target_pairs={{504,16},{496,8},{488,0},{480,504},{472,496},{464,488},{456,480},{... | collective-permute-start | bytes 196616 | tf_op jit(solution)/shard_map/ppermute | solution.py:357
  93.6 6.1 %collective-permute-start.8 = (bf16[256,128]{1,0:T(8,128)(2,1)S(1)}, bf16[256,128]{1,0:T(8,128)(2,1)S(1)}, u32[]{:S(2)}, u32[]{:S(2)}) collective-permute-start(bf16[256,128]{1,0:T(8,128)(2,1)S(1)} %three_back.1.refs_3_), channel_id=1, source_target_pairs={{504,480},{496,472},{488,464},{480,456},{472,448},{464,440},{456,4... | collective-permute-start | bytes 196616 | tf_op jit(solution)/shard_map/ppermute | solution.py:357
  99.8 1.8 %grads_k.1 = (f32[8,128]{1,0:T(8,128)S(1)}, f32[1024,256]{1,0:T(8,128)S(1)}) custom-call(s32[2,1024]{1,0:T(2,128)S(1)} %copy-done.1, bf16[8,512,256]{2,1,0:T(8,128)(2,1)S(1)} %all-to-all-done.refs_1_.refs_2_, bf16[1024,256]{1,0:T(8,128)(2,1)S(1)} %get-tuple-element.24.refs_3_.refs_2_, bf16[256,128]{1,0:T(8,128)(2,1)S(1)} %three_back.1.refs_3_), custom_call_target="tpu_custom_call" | custom-call | flops 536870912 | bytes 3682304 | tf_op jit(solution)/shard_map/grads_k/pallas_call | solution.py:308
  102.2 8.2 %collective-permute-start.11 = (bf16[256,128]{1,0:T(8,128)(2,1)S(1)}, bf16[256,128]{1,0:T(8,128)(2,1)S(1)}, u32[]{:S(2)}, u32[]{:S(2)}) collective-permute-start(bf16[256,128]{1,0:T(8,128)(2,1)S(1)} %nine_back.1.refs_3_), channel_id=1, source_target_pairs={{504,464},{496,456},{488,448},{480,440},{472,432},{464,424},{456,4... | collective-permute-start | bytes 196616 | tf_op jit(solution)/shard_map/ppermute | solution.py:357
  110.4 8.2 %collective-permute-start.10 = (bf16[256,128]{1,0:T(8,128)(2,1)S(1)}, bf16[256,128]{1,0:T(8,128)(2,1)S(1)}, u32[]{:S(2)}, u32[]{:S(2)}) collective-permute-start(bf16[256,128]{1,0:T(8,128)(2,1)S(1)} %nine_back.1.refs_3_), channel_id=1, source_target_pairs={{504,392},{496,384},{488,376},{480,368},{472,360},{464,352},{456,3... | collective-permute-start | bytes 196616 | tf_op jit(solution)/shard_map/ppermute | solution.py:357
  118.6 2.3 %grads_v.1 = (f32[8,128]{1,0:T(8,128)}, f32[1024,256]{1,0:T(8,128)S(1)}) custom-call(s32[2,1024]{1,0:T(2,128)S(1)} %copy-done.1, bf16[8,512,256]{2,1,0:T(8,128)(2,1)S(1)} %all-to-all-done.refs_1_.refs_2_, bf16[1024,256]{1,0:T(8,128)(2,1)S(1)} %get-tuple-element.24.refs_3_.refs_2_, bf16[256,128]{1,0:T(8,128)(2,1)S(1)} %nine_back.1.refs_3_), custom_call_target="tpu_custom_call" | custom-call | flops 536870912 | bytes 3682304 | tf_op jit(solution)/shard_map/grads_v/pallas_call | solution.py:308
  120.9 2.0 %last.1 = (bf16[1024,256]{1,0:T(8,128)(2,1)}, bf16[1024,256]{1,0:T(8,128)(2,1)}) custom-call(s32[2]{0:T(128)S(1)} %pad_add_fusion.refs_1_.refs_0_, s32[132]{0:T(256)S(1)} %meta.1.refs_2_.refs_0_.refs_1_, bf16[8,512,256]{2,1,0:T(8,128)(2,1)S(1)} %all-to-all-done.refs_1_.refs_2_, f32[1024,256]{1,0:T(8,128)S(1)} %get-tuple-element.29.refs_3_, ...), custom_call_target="tpu_custom_call" | custom-call | flops 134217728 | bytes 5373952 | tf_op jit(solution)/shard_map/last/pallas_call | solution.py:308
  (35 shorter events, 12.6 us)
Async XLA Ops:
  0.6 13.5 %copy-start.3 = (s32[32]{0:T(128)S(1)}, s32[32]{0:T(128)}, u32[]{:S(2)}) copy-start(s32[32]{0:T(128)} %refs_0_.6) | copy-start | bytes 388
  3.7 19.8 %all-to-all-start.1 = ((bf16[8,256,128]{2,1,0:T(8,128)(2,1)}), bf16[8,256,128]{2,1,0:T(8,128)(2,1)S(1)}, u32[]{:S(2)}, u32[]{:S(2)}) async-start(bf16[8,256,128]{2,1,0:T(8,128)(2,1)} %get-tuple-element.21), calls=%async_computation.1 | async-start | bytes 1048576 | tf_op jit(solution)/shard_map/all_to_all | solution.py:322
  14.1 0.7 copy-start.5
  18.3 0.6 copy-start
  23.5 4.5 %copy-start.4 = (f32[8,128]{1,0:T(8,128)S(1)}, f32[8,128]{1,0:T(8,128)}, u32[]{:S(2)}) copy-start(f32[8,128]{1,0:T(8,128)} %get-tuple-element.22.refs_2_) | copy-start | bytes 12292
  23.5 40.2 %copy-start.1 = (s32[2,1024]{1,0:T(2,128)S(1)}, s32[2,1024]{1,0:T(2,128)}, u32[]{:S(2)}) copy-start(s32[2,1024]{1,0:T(2,128)} %copy-done) | copy-start | bytes 24580
  23.5 40.2 %all-to-all-start = ((bf16[8,512,256]{2,1,0:T(8,128)(2,1)}), bf16[8,512,256]{2,1,0:T(8,128)(2,1)S(1)}, u32[]{:S(2)}, u32[]{:S(2)}) async-start(bf16[8,512,256]{2,1,0:T(8,128)(2,1)} %get-tuple-element.20), calls=%async_computation | async-start | bytes 4194304 | tf_op jit(solution)/shard_map/all_to_all | solution.py:322
  28.0 37.6 %copy-start.2 = (f32[2048]{0:T(1024)S(1)}, f32[2048]{0:T(1024)}, u32[]{:S(2)}) copy-start(f32[2048]{0:T(1024)} %param.10) | copy-start | bytes 24580
  28.7 10.4 %collective-permute-start.1 = (bf16[256,128]{1,0:T(8,128)(2,1)S(1)}, bf16[256,128]{1,0:T(8,128)(2,1)S(1)}, u32[]{:S(2)}, u32[]{:S(2)}) collective-permute-start(bf16[256,128]{1,0:T(8,128)(2,1)S(1)} %tail.1.refs_3_), channel_id=1, source_target_pairs={{0,504},{8,0},{16,8},{24,16},{32,24},{40,32},{48,40},{56,48},{64,5... | collective-permute-start | bytes 196616 | tf_op jit(solution)/shard_map/ppermute | solution.py:357
  37.8 2.6 %collective-permute-start = (bf16[256,128]{1,0:T(8,128)(2,1)S(1)}, bf16[256,128]{1,0:T(8,128)(2,1)S(1)}, u32[]{:S(2)}, u32[]{:S(2)}) collective-permute-start(bf16[256,128]{1,0:T(8,128)(2,1)S(1)} %tail.1.refs_3_), channel_id=1, source_target_pairs={{0,8},{8,16},{16,24},{24,32},{32,40},{40,48},{48,56},{56,64},{64,7... | collective-permute-start | bytes 196616 | tf_op jit(solution)/shard_map/ppermute | solution.py:357
  41.0 8.9 %collective-permute-start.3 = (bf16[256,128]{1,0:T(8,128)(2,1)S(1)}, bf16[256,128]{1,0:T(8,128)(2,1)S(1)}, u32[]{:S(2)}, u32[]{:S(2)}) collective-permute-start(bf16[256,128]{1,0:T(8,128)(2,1)S(1)} %three_forward.1.refs_3_), channel_id=1, source_target_pairs={{0,488},{8,496},{16,504},{24,0},{32,8},{40,16},{48,24},{56,32},{64... | collective-permute-start | bytes 196616 | tf_op jit(solution)/shard_map/ppermute | solution.py:357
  47.8 2.6 %collective-permute-start.2 = (bf16[256,128]{1,0:T(8,128)(2,1)S(1)}, bf16[256,128]{1,0:T(8,128)(2,1)S(1)}, u32[]{:S(2)}, u32[]{:S(2)}) collective-permute-start(bf16[256,128]{1,0:T(8,128)(2,1)S(1)} %three_forward.1.refs_3_), channel_id=1, source_target_pairs={{0,24},{8,32},{16,40},{24,48},{32,56},{40,64},{48,72},{56,80},{64,... | collective-permute-start | bytes 196616 | tf_op jit(solution)/shard_map/ppermute | solution.py:357
  51.0 14.6 %collective-permute-start.5 = (bf16[256,128]{1,0:T(8,128)(2,1)S(1)}, bf16[256,128]{1,0:T(8,128)(2,1)S(1)}, u32[]{:S(2)}, u32[]{:S(2)}) collective-permute-start(bf16[256,128]{1,0:T(8,128)(2,1)S(1)} %nine_forward.1), channel_id=1, source_target_pairs={{0,40},{8,48},{16,56},{24,64},{32,72},{40,80},{48,88},{56,96},{64,... | collective-permute-start | bytes 196616 | tf_op jit(solution)/shard_map/ppermute | solution.py:357
  62.0 3.7 %collective-permute-start.4 = (bf16[256,128]{1,0:T(8,128)(2,1)S(1)}, bf16[256,128]{1,0:T(8,128)(2,1)S(1)}, u32[]{:S(2)}, u32[]{:S(2)}) collective-permute-start(bf16[256,128]{1,0:T(8,128)(2,1)S(1)} %nine_forward.1), channel_id=1, source_target_pairs={{0,112},{8,120},{16,128},{24,136},{32,144},{40,152},{48,160},{56,1... | collective-permute-start | bytes 196616 | tf_op jit(solution)/shard_map/ppermute | solution.py:357
  68.0 55.0 %all-to-all-start.2 = ((bf16[8,128,256]{2,1,0:T(8,128)(2,1)}), bf16[8,128,256]{2,1,0:T(8,128)(2,1)S(1)}, u32[]{:S(2)}, u32[]{:S(2)}) async-start(bf16[8,128,256]{2,1,0:T(8,128)(2,1)} %bitcast.3), calls=%async_computation.2 | async-start | bytes 1048576 | tf_op jit(solution)/shard_map/all_to_all | solution.py:322
  76.9 10.3 %collective-permute-start.7 = (bf16[256,128]{1,0:T(8,128)(2,1)S(1)}, bf16[256,128]{1,0:T(8,128)(2,1)S(1)}, u32[]{:S(2)}, u32[]{:S(2)}) collective-permute-start(bf16[256,128]{1,0:T(8,128)(2,1)S(1)} %get-tuple-element.27.refs_3_), channel_id=1, source_target_pairs={{504,0},{496,504},{488,496},{480,488},{472,480},{464,472},{456,464... | collective-permute-start | bytes 196616 | tf_op jit(solution)/shard_map/ppermute | solution.py:357
  79.3 9.5 %collective-permute-start.6 = (bf16[256,128]{1,0:T(8,128)(2,1)S(1)}, bf16[256,128]{1,0:T(8,128)(2,1)S(1)}, u32[]{:S(2)}, u32[]{:S(2)}) collective-permute-start(bf16[256,128]{1,0:T(8,128)(2,1)S(1)} %get-tuple-element.27.refs_3_), channel_id=1, source_target_pairs={{504,496},{496,488},{488,480},{480,472},{472,464},{464,456},{456,4... | collective-permute-start | bytes 196616 | tf_op jit(solution)/shard_map/ppermute | solution.py:357
  89.4 12.2 %collective-permute-start.9 = (bf16[256,128]{1,0:T(8,128)(2,1)S(1)}, bf16[256,128]{1,0:T(8,128)(2,1)S(1)}, u32[]{:S(2)}, u32[]{:S(2)}) collective-permute-start(bf16[256,128]{1,0:T(8,128)(2,1)S(1)} %three_back.1.refs_3_), channel_id=1, source_target_pairs={{504,16},{496,8},{488,0},{480,504},{472,496},{464,488},{456,480},{... | collective-permute-start | bytes 196616 | tf_op jit(solution)/shard_map/ppermute | solution.py:357
  93.6 8.0 %collective-permute-start.8 = (bf16[256,128]{1,0:T(8,128)(2,1)S(1)}, bf16[256,128]{1,0:T(8,128)(2,1)S(1)}, u32[]{:S(2)}, u32[]{:S(2)}) collective-permute-start(bf16[256,128]{1,0:T(8,128)(2,1)S(1)} %three_back.1.refs_3_), channel_id=1, source_target_pairs={{504,480},{496,472},{488,464},{480,456},{472,448},{464,440},{456,4... | collective-permute-start | bytes 196616 | tf_op jit(solution)/shard_map/ppermute | solution.py:357
  102.2 18.7 %collective-permute-start.11 = (bf16[256,128]{1,0:T(8,128)(2,1)S(1)}, bf16[256,128]{1,0:T(8,128)(2,1)S(1)}, u32[]{:S(2)}, u32[]{:S(2)}) collective-permute-start(bf16[256,128]{1,0:T(8,128)(2,1)S(1)} %nine_back.1.refs_3_), channel_id=1, source_target_pairs={{504,464},{496,456},{488,448},{480,440},{472,432},{464,424},{456,4... | collective-permute-start | bytes 196616 | tf_op jit(solution)/shard_map/ppermute | solution.py:357
  110.4 10.5 %collective-permute-start.10 = (bf16[256,128]{1,0:T(8,128)(2,1)S(1)}, bf16[256,128]{1,0:T(8,128)(2,1)S(1)}, u32[]{:S(2)}, u32[]{:S(2)}) collective-permute-start(bf16[256,128]{1,0:T(8,128)(2,1)S(1)} %nine_back.1.refs_3_), channel_id=1, source_target_pairs={{504,392},{496,384},{488,376},{480,368},{472,360},{464,352},{456,3... | collective-permute-start | bytes 196616 | tf_op jit(solution)/shard_map/ppermute | solution.py:357

commit v5 on v4

--- a/solution.py
+++ b/solution.py
@@ -248,8 +248,7 @@
             grad_q_ref[low:high, cols] = grad_q.astype(BF16)
 
 
-def turned_kernel(docs_ref, left_ref, right_ref, rows_ref, ended_ref, part_ref):
-    ended_ref[...] = jnp.zeros_like(ended_ref)
+def turned_kernel(docs_ref, left_ref, right_ref, rows_ref, part_ref):
     left, right, summed = (
         unpacked(*field) if isinstance(field, tuple) else field for field in (left_ref, right_ref, rows_ref)
     )
@@ -267,11 +266,12 @@
 
 
 def grad_k_kernel(docs_ref, packed_ref, grad_ref, ended_ref, part_ref):
-    turned_kernel(docs_ref, (packed_ref, 1), grad_ref, (packed_ref, 2), ended_ref, part_ref)
-
-
-def grad_v_kernel(docs_ref, packed_ref, grad_ref, ended_ref, part_ref):
-    turned_kernel(docs_ref, (packed_ref, 0), (packed_ref, 2), grad_ref, ended_ref, part_ref)
+    ended_ref[...] = jnp.zeros_like(ended_ref)
+    turned_kernel(docs_ref, (packed_ref, 1), grad_ref, (packed_ref, 2), part_ref)
+
+
+def grad_v_kernel(docs_ref, packed_ref, grad_ref, part_ref):
+    turned_kernel(docs_ref, (packed_ref, 0), (packed_ref, 2), grad_ref, part_ref)
 
 
 def last_kernel(
@@ -444,6 +444,10 @@
     )
 
     normed = across_head(normed.reshape(groups, tokens, width))
+    ended, part_k = call(
+        grad_k_kernel, "grads_k", [ENDED, f32((rows, width))], [], [docs, packed, grad], 2 * square
+    )
+    three = span_of_three(part, where, marks, True, [ended])
     ended, grad_q = call(
         functools.partial(grad_q_kernel, blocks),
         "grads_q",
@@ -451,16 +455,12 @@
         [marks],
         [docs, packed, grad, state],
         2 * square,
-    )
-    three = span_of_three(part, where, marks, True, [ended])
-
-    def turned(kernel, name, after):
-        outs = [ENDED, f32((rows, width))]
-        return call(kernel, name, outs, [], [docs, packed, grad], 2 * square, after=[after])
-
-    ended, part_k = turned(grad_k_kernel, "grads_k", three)
+        after=[three],
+    )
     nine = span_of_nine(three, where, marks, True, [ended])
-    _, part_v = turned(grad_v_kernel, "grads_v", nine)
+    (part_v,) = call(
+        grad_v_kernel, "grads_v", [f32((rows, width))], [], [docs, packed, grad], 2 * square, after=[nine]
+    )
     grad_k, grad_v = call(
         functools.partial(last_kernel, blocks),
         "last",

time: 125 us -> 124 us (level)
  starting transfers between devices: 85.3 us -> 82.9 us
  waiting for transfers between devices: 8.86 us -> 10.3 us
    ppermute x12, starting transfers between devices: 61.6 us -> 59.2 us  [from_block(): return lax.ppermute(field, 'seq', pairs)]
    ppermute x12, waiting for transfers between devices: 7.59 us -> 8.97 us  [from_block(): return lax.ppermute(field, 'seq', pairs)]
where the time goes in v5:
time: 124 us; the launch traced here: 122 us
  starting transfers between devices  82.9 us (67%)
  Pallas kernels  26 us (21%)
  waiting for transfers between devices  10.3 us (8%)
  local copies, waits for them, and re-layouts  2.14 us (2%)
    ppermute x12, starting transfers between devices, from_block(): return lax.ppermute(field, 'seq', pairs)  59.2 us
    pallas_call x15, Pallas kernels, call(): pl.pallas_call(body, name=name, out_shape=outs, in_specs=[SMEM] * len(sca...  26 us
    all_to_all x3, starting transfers between devices, across_head(): lax.all_to_all(parts, 'head', split_axis=0, concat_axis=0, tiled=True)  23.7 us
    ppermute x12, waiting for transfers between devices, from_block(): return lax.ppermute(field, 'seq', pairs)  8.97 us
  transfers between devices with their start and end apart: 15, of which 6 were waited for; matrix products, arithmetic and copies ran while one was open for 0% of the time, Pallas kernels for 17%

profile of v5, /device:TPU:1, one launch (start us, length us, event | category | flops | bytes accessed | tf_op | source)
XLA Modules:
  0.0 122.4 jit_solution(4619511811098657496)
XLA Ops:
  0.6 3.1 %parts.1 = (f32[8,128]{1,0:T(8,128)}, bf16[8,256,128]{2,1,0:T(8,128)(2,1)}) custom-call(s32[32]{0:T(128)} %refs_0_.6, s32[1]{0:T(128)} %bitcast.refs_1_, s32[1]{0:T(128)} %bitcast.1.refs_2_, bf16[128,2048]{1,0:T(8,128)(2,1)} %refs_0_.7, bf16[128,2048]{1,0:T(8,128)(2,1)} %refs_1_.1), custom_call_target="tpu_custom_call" | custom-call | flops 67108864 | bytes 1576960 | tf_op jit(solution)/shard_map/parts/pallas_call | solution.py:308
  3.7 10.3 %all-to-all-start.1 = ((bf16[8,256,128]{2,1,0:T(8,128)(2,1)}), bf16[8,256,128]{2,1,0:T(8,128)(2,1)S(1)}, u32[]{:S(2)}, u32[]{:S(2)}) async-start(bf16[8,256,128]{2,1,0:T(8,128)(2,1)} %get-tuple-element.20), calls=%async_computation.1 | async-start | bytes 1048576 | tf_op jit(solution)/shard_map/all_to_all | solution.py:322
  14.8 2.5 %meta.1.refs_2_.refs_0_.refs_1_ = s32[132]{0:T(256)S(1)} custom-call(s32[32]{0:T(128)S(1)} %copy-done.3, s32[2]{0:T(128)S(1)} %pad_add_fusion.refs_1_.refs_0_, f32[8,128]{1,0:T(8,128)S(1)} %copy-done.5), custom_call_target="tpu_custom_call" | custom-call | flops 1024 | bytes 528 | tf_op jit(solution)/shard_map/meta/pallas_call | solution.py:308
  18.9 3.3 %pack.1 = (f32[8,128]{1,0:T(8,128)}, bf16[8,512,256]{2,1,0:T(8,128)(2,1)}) custom-call(bf16[128,2048]{1,0:T(8,128)(2,1)} %refs_0_.7, bf16[128,2048]{1,0:T(8,128)(2,1)} %refs_1_.1, bf16[128,2048]{1,0:T(8,128)(2,1)} %refs_2_.1, bf16[128,2048]{1,0:T(8,128)(2,1)} %refs_3_.3, s32[2,1024]{1,0:T(2,128)} %copy-done), custom_call_target="tpu_custom_call" | custom-call | bytes 4198400 | tf_op jit(solution)/shard_map/pack/pallas_call | solution.py:308
  22.2 1.4 %all-to-all-done.1.refs_1_ = bf16[8,256,128]{2,1,0:T(8,128)(2,1)S(1)} async-done(((bf16[8,256,128]{2,1,0:T(8,128)(2,1)}), bf16[8,256,128]{2,1,0:T(8,128)(2,1)S(1)}, u32[]{:S(2)}, u32[]{:S(2)}) %all-to-all-start.1) | async-done | bytes 524320 | tf_op jit(solution)/shard_map/all_to_all | solution.py:322
  23.5 4.5 %all-to-all-start = ((bf16[8,512,256]{2,1,0:T(8,128)(2,1)}), bf16[8,512,256]{2,1,0:T(8,128)(2,1)S(1)}, u32[]{:S(2)}, u32[]{:S(2)}) async-start(bf16[8,512,256]{2,1,0:T(8,128)(2,1)} %get-tuple-element.19), calls=%async_computation | async-start | bytes 4194304 | tf_op jit(solution)/shard_map/all_to_all | solution.py:322
  28.7 9.1 %collective-permute-start.1 = (bf16[256,128]{1,0:T(8,128)(2,1)S(1)}, bf16[256,128]{1,0:T(8,128)(2,1)S(1)}, u32[]{:S(2)}, u32[]{:S(2)}) collective-permute-start(bf16[256,128]{1,0:T(8,128)(2,1)S(1)} %tail.1.refs_3_), channel_id=1, source_target_pairs={{0,504},{8,0},{16,8},{24,16},{32,24},{40,32},{48,40},{56,48},{64,5... | collective-permute-start | bytes 196616 | tf_op jit(solution)/shard_map/ppermute | solution.py:357
  41.0 6.9 %collective-permute-start.3 = (bf16[256,128]{1,0:T(8,128)(2,1)S(1)}, bf16[256,128]{1,0:T(8,128)(2,1)S(1)}, u32[]{:S(2)}, u32[]{:S(2)}) collective-permute-start(bf16[256,128]{1,0:T(8,128)(2,1)S(1)} %three_forward.1.refs_3_), channel_id=1, source_target_pairs={{0,488},{8,496},{16,504},{24,0},{32,8},{40,16},{48,24},{56,32},{64... | collective-permute-start | bytes 196616 | tf_op jit(solution)/shard_map/ppermute | solution.py:357
  51.0 10.9 %collective-permute-start.5 = (bf16[256,128]{1,0:T(8,128)(2,1)S(1)}, bf16[256,128]{1,0:T(8,128)(2,1)S(1)}, u32[]{:S(2)}, u32[]{:S(2)}) collective-permute-start(bf16[256,128]{1,0:T(8,128)(2,1)S(1)} %nine_forward.1), channel_id=1, source_target_pairs={{0,40},{8,48},{16,56},{24,64},{32,72},{40,80},{48,88},{56,96},{64,... | collective-permute-start | bytes 196616 | tf_op jit(solution)/shard_map/ppermute | solution.py:357
  62.0 1.7 %collective-permute-start.4 = (bf16[256,128]{1,0:T(8,128)(2,1)S(1)}, bf16[256,128]{1,0:T(8,128)(2,1)S(1)}, u32[]{:S(2)}, u32[]{:S(2)}) collective-permute-start(bf16[256,128]{1,0:T(8,128)(2,1)S(1)} %nine_forward.1), channel_id=1, source_target_pairs={{0,112},{8,120},{16,128},{24,136},{32,144},{40,152},{48,160},{56,1... | collective-permute-start | bytes 196616 | tf_op jit(solution)/shard_map/ppermute | solution.py:357
  63.7 1.9 %intra.1.refs_3_ = f32[1024,256]{1,0:T(8,128)S(1)} custom-call(s32[2,1024]{1,0:T(2,128)S(1)} %copy-done.1, bf16[8,512,256]{2,1,0:T(8,128)(2,1)S(1)} %all-to-all-done.refs_1_.refs_2_), custom_call_target="tpu_custom_call" | custom-call | flops 536870912 | bytes 3153920 | tf_op jit(solution)/shard_map/intra/pallas_call | solution.py:308
  65.7 2.3 %norm.1 = (bf16[1024,256]{1,0:T(8,128)(2,1)}, bf16[1024,256]{1,0:T(8,128)(2,1)S(1)}, bf16[256,128]{1,0:T(8,128)(2,1)S(1)}, bf16[256,128]{1,0:T(8,128)(2,1)S(1)}) custom-call(s32[2]{0:T(128)S(1)} %pad_add_fusion.refs_1_.refs_0_, s32[132]{0:T(256)S(1)} %meta.1.refs_2_.refs_0_.refs_1_, bf16[8,512,256]{2,1,0:T(8,128)(2,1)S(1)} %all-to-all-done.refs_1_.refs_2_, ...), custom_call_target="tpu_custom_call" | custom-call | flops 134217728 | bytes 4464640 | tf_op jit(solution)/shard_map/norm/pallas_call | solution.py:308
  68.0 8.9 %all-to-all-start.2 = ((bf16[8,128,256]{2,1,0:T(8,128)(2,1)}), bf16[8,128,256]{2,1,0:T(8,128)(2,1)S(1)}, u32[]{:S(2)}, u32[]{:S(2)}) async-start(bf16[8,128,256]{2,1,0:T(8,128)(2,1)} %bitcast.3), calls=%async_computation.2 | async-start | bytes 1048576 | tf_op jit(solution)/shard_map/all_to_all | solution.py:322
  76.9 2.4 %collective-permute-start.7 = (bf16[256,128]{1,0:T(8,128)(2,1)S(1)}, bf16[256,128]{1,0:T(8,128)(2,1)S(1)}, u32[]{:S(2)}, u32[]{:S(2)}) collective-permute-start(bf16[256,128]{1,0:T(8,128)(2,1)S(1)} %get-tuple-element.25.refs_3_), channel_id=1, source_target_pairs={{504,0},{496,504},{488,496},{480,488},{472,480},{464,472},{456,464... | collective-permute-start | bytes 196616 | tf_op jit(solution)/shard_map/ppermute | solution.py:357
  80.6 1.8 %grads_k.1 = (f32[8,128]{1,0:T(8,128)S(1)}, f32[1024,256]{1,0:T(8,128)S(1)}) custom-call(s32[2,1024]{1,0:T(2,128)S(1)} %copy-done.1, bf16[8,512,256]{2,1,0:T(8,128)(2,1)S(1)} %all-to-all-done.refs_1_.refs_2_, bf16[1024,256]{1,0:T(8,128)(2,1)S(1)} %get-tuple-element.23.refs_2_.refs_3_), custom_call_target="tpu_custom_call" | custom-call | flops 536870912 | bytes 3682304 | tf_op jit(solution)/shard_map/grads_k/pallas_call | solution.py:308
  82.4 4.8 %collective-permute-done.7.refs_4_ = bf16[256,128]{1,0:T(8,128)(2,1)S(1)} collective-permute-done((bf16[256,128]{1,0:T(8,128)(2,1)S(1)}, bf16[256,128]{1,0:T(8,128)(2,1)S(1)}, u32[]{:S(2)}, u32[]{:S(2)}) %collective-permute-start.7) | collective-permute-done | bytes 65568 | tf_op jit(solution)/shard_map/ppermute | solution.py:357
  87.2 1.6 %collective-permute-done.6.refs_2_ = bf16[256,128]{1,0:T(8,128)(2,1)S(1)} collective-permute-done((bf16[256,128]{1,0:T(8,128)(2,1)S(1)}, bf16[256,128]{1,0:T(8,128)(2,1)S(1)}, u32[]{:S(2)}, u32[]{:S(2)}) %collective-permute-start.6) | collective-permute-done | bytes 65568 | tf_op jit(solution)/shard_map/ppermute | solution.py:357
  89.4 4.3 %collective-permute-start.9 = (bf16[256,128]{1,0:T(8,128)(2,1)S(1)}, bf16[256,128]{1,0:T(8,128)(2,1)S(1)}, u32[]{:S(2)}, u32[]{:S(2)}) collective-permute-start(bf16[256,128]{1,0:T(8,128)(2,1)S(1)} %three_back.1.refs_5_.refs_3_), channel_id=1, source_target_pairs={{504,16},{496,8},{488,0},{480,504},{472,496},{464,488},{456,480},{... | collective-permute-start | bytes 196616 | tf_op jit(solution)/shard_map/ppermute | solution.py:357
  93.6 6.1 %collective-permute-start.8 = (bf16[256,128]{1,0:T(8,128)(2,1)S(1)}, bf16[256,128]{1,0:T(8,128)(2,1)S(1)}, u32[]{:S(2)}, u32[]{:S(2)}) collective-permute-start(bf16[256,128]{1,0:T(8,128)(2,1)S(1)} %three_back.1.refs_5_.refs_3_), channel_id=1, source_target_pairs={{504,480},{496,472},{488,464},{480,456},{472,448},{464,440},{456,4... | collective-permute-start | bytes 196616 | tf_op jit(solution)/shard_map/ppermute | solution.py:357
  99.8 3.2 %grads_q.1 = (f32[8,128]{1,0:T(8,128)S(1)}, bf16[1024,256]{1,0:T(8,128)(2,1)}) custom-call(s32[132]{0:T(256)S(1)} %meta.1.refs_2_.refs_0_.refs_1_, s32[2,1024]{1,0:T(2,128)S(1)} %copy-done.1, bf16[8,512,256]{2,1,0:T(8,128)(2,1)S(1)} %all-to-all-done.refs_1_.refs_2_, bf16[1024,256]{1,0:T(8,128)(2,1)S(1)} %get-tuple-element.23.refs_2_.refs_3_, ...), custom_call_target="tpu_custom_call" | custom-call | flops 536870912 | bytes 3223552 | tf_op jit(solution)/shard_map/grads_q/pallas_call | solution.py:308
  103.6 5.3 %collective-permute-start.11 = (bf16[256,128]{1,0:T(8,128)(2,1)S(1)}, bf16[256,128]{1,0:T(8,128)(2,1)S(1)}, u32[]{:S(2)}, u32[]{:S(2)}) collective-permute-start(bf16[256,128]{1,0:T(8,128)(2,1)S(1)} %nine_back.1.refs_3_), channel_id=1, source_target_pairs={{504,464},{496,456},{488,448},{480,440},{472,432},{464,424},{456,4... | collective-permute-start | bytes 196616 | tf_op jit(solution)/shard_map/ppermute | solution.py:357
  109.0 8.7 %collective-permute-start.10 = (bf16[256,128]{1,0:T(8,128)(2,1)S(1)}, bf16[256,128]{1,0:T(8,128)(2,1)S(1)}, u32[]{:S(2)}, u32[]{:S(2)}) collective-permute-start(bf16[256,128]{1,0:T(8,128)(2,1)S(1)} %nine_back.1.refs_3_), channel_id=1, source_target_pairs={{504,392},{496,384},{488,376},{480,368},{472,360},{464,352},{456,3... | collective-permute-start | bytes 196616 | tf_op jit(solution)/shard_map/ppermute | solution.py:357
  117.6 1.8 %grads_v.1.refs_4_ = f32[1024,256]{1,0:T(8,128)S(1)} custom-call(s32[2,1024]{1,0:T(2,128)S(1)} %copy-done.1, bf16[8,512,256]{2,1,0:T(8,128)(2,1)S(1)} %all-to-all-done.refs_1_.refs_2_, bf16[1024,256]{1,0:T(8,128)(2,1)S(1)} %get-tuple-element.23.refs_2_.refs_3_, bf16[256,128]{1,0:T(8,128)(2,1)S(1)} %nine_back.1.refs_3_), custom_call_target="tpu_custom_call" | custom-call | flops 536870912 | bytes 3678208 | tf_op jit(solution)/shard_map/grads_v/pallas_call | solution.py:308
  119.5 2.0 %last.1 = (bf16[1024,256]{1,0:T(8,128)(2,1)}, bf16[1024,256]{1,0:T(8,128)(2,1)}) custom-call(s32[2]{0:T(128)S(1)} %pad_add_fusion.refs_1_.refs_0_, s32[132]{0:T(256)S(1)} %meta.1.refs_2_.refs_0_.refs_1_, bf16[8,512,256]{2,1,0:T(8,128)(2,1)S(1)} %all-to-all-done.refs_1_.refs_2_, f32[1024,256]{1,0:T(8,128)S(1)} %get-tuple-element.28.refs_3_, ...), custom_call_target="tpu_custom_call" | custom-call | flops 134217728 | bytes 5373952 | tf_op jit(solution)/shard_map/last/pallas_call | solution.py:308
  (35 shorter events, 12.7 us)
Async XLA Ops:
  0.6 13.5 %copy-start.3 = (s32[32]{0:T(128)S(1)}, s32[32]{0:T(128)}, u32[]{:S(2)}) copy-start(s32[32]{0:T(128)} %refs_0_.6) | copy-start | bytes 388
  3.7 19.8 %all-to-all-start.1 = ((bf16[8,256,128]{2,1,0:T(8,128)(2,1)}), bf16[8,256,128]{2,1,0:T(8,128)(2,1)S(1)}, u32[]{:S(2)}, u32[]{:S(2)}) async-start(bf16[8,256,128]{2,1,0:T(8,128)(2,1)} %get-tuple-element.20), calls=%async_computation.1 | async-start | bytes 1048576 | tf_op jit(solution)/shard_map/all_to_all | solution.py:322
  14.1 0.7 copy-start.5
  18.3 0.6 copy-start
  23.5 4.5 %copy-start.4 = (f32[8,128]{1,0:T(8,128)S(1)}, f32[8,128]{1,0:T(8,128)}, u32[]{:S(2)}) copy-start(f32[8,128]{1,0:T(8,128)} %get-tuple-element.21.refs_2_) | copy-start | bytes 12292
  23.5 40.2 %copy-start.1 = (s32[2,1024]{1,0:T(2,128)S(1)}, s32[2,1024]{1,0:T(2,128)}, u32[]{:S(2)}) copy-start(s32[2,1024]{1,0:T(2,128)} %copy-done) | copy-start | bytes 24580
  23.5 40.2 %all-to-all-start = ((bf16[8,512,256]{2,1,0:T(8,128)(2,1)}), bf16[8,512,256]{2,1,0:T(8,128)(2,1)S(1)}, u32[]{:S(2)}, u32[]{:S(2)}) async-start(bf16[8,512,256]{2,1,0:T(8,128)(2,1)} %get-tuple-element.19), calls=%async_computation | async-start | bytes 4194304 | tf_op jit(solution)/shard_map/all_to_all | solution.py:322
  28.0 37.6 %copy-start.2 = (f32[2048]{0:T(1024)S(1)}, f32[2048]{0:T(1024)}, u32[]{:S(2)}) copy-start(f32[2048]{0:T(1024)} %param.10) | copy-start | bytes 24580
  28.7 10.4 %collective-permute-start.1 = (bf16[256,128]{1,0:T(8,128)(2,1)S(1)}, bf16[256,128]{1,0:T(8,128)(2,1)S(1)}, u32[]{:S(2)}, u32[]{:S(2)}) collective-permute-start(bf16[256,128]{1,0:T(8,128)(2,1)S(1)} %tail.1.refs_3_), channel_id=1, source_target_pairs={{0,504},{8,0},{16,8},{24,16},{32,24},{40,32},{48,40},{56,48},{64,5... | collective-permute-start | bytes 196616 | tf_op jit(solution)/shard_map/ppermute | solution.py:357
  37.8 2.6 %collective-permute-start = (bf16[256,128]{1,0:T(8,128)(2,1)S(1)}, bf16[256,128]{1,0:T(8,128)(2,1)S(1)}, u32[]{:S(2)}, u32[]{:S(2)}) collective-permute-start(bf16[256,128]{1,0:T(8,128)(2,1)S(1)} %tail.1.refs_3_), channel_id=1, source_target_pairs={{0,8},{8,16},{16,24},{24,32},{32,40},{40,48},{48,56},{56,64},{64,7... | collective-permute-start | bytes 196616 | tf_op jit(solution)/shard_map/ppermute | solution.py:357
  41.0 8.9 %collective-permute-start.3 = (bf16[256,128]{1,0:T(8,128)(2,1)S(1)}, bf16[256,128]{1,0:T(8,128)(2,1)S(1)}, u32[]{:S(2)}, u32[]{:S(2)}) collective-permute-start(bf16[256,128]{1,0:T(8,128)(2,1)S(1)} %three_forward.1.refs_3_), channel_id=1, source_target_pairs={{0,488},{8,496},{16,504},{24,0},{32,8},{40,16},{48,24},{56,32},{64... | collective-permute-start | bytes 196616 | tf_op jit(solution)/shard_map/ppermute | solution.py:357
  47.8 2.6 %collective-permute-start.2 = (bf16[256,128]{1,0:T(8,128)(2,1)S(1)}, bf16[256,128]{1,0:T(8,128)(2,1)S(1)}, u32[]{:S(2)}, u32[]{:S(2)}) collective-permute-start(bf16[256,128]{1,0:T(8,128)(2,1)S(1)} %three_forward.1.refs_3_), channel_id=1, source_target_pairs={{0,24},{8,32},{16,40},{24,48},{32,56},{40,64},{48,72},{56,80},{64,... | collective-permute-start | bytes 196616 | tf_op jit(solution)/shard_map/ppermute | solution.py:357
  51.0 14.6 %collective-permute-start.5 = (bf16[256,128]{1,0:T(8,128)(2,1)S(1)}, bf16[256,128]{1,0:T(8,128)(2,1)S(1)}, u32[]{:S(2)}, u32[]{:S(2)}) collective-permute-start(bf16[256,128]{1,0:T(8,128)(2,1)S(1)} %nine_forward.1), channel_id=1, source_target_pairs={{0,40},{8,48},{16,56},{24,64},{32,72},{40,80},{48,88},{56,96},{64,... | collective-permute-start | bytes 196616 | tf_op jit(solution)/shard_map/ppermute | solution.py:357
  62.0 3.7 %collective-permute-start.4 = (bf16[256,128]{1,0:T(8,128)(2,1)S(1)}, bf16[256,128]{1,0:T(8,128)(2,1)S(1)}, u32[]{:S(2)}, u32[]{:S(2)}) collective-permute-start(bf16[256,128]{1,0:T(8,128)(2,1)S(1)} %nine_forward.1), channel_id=1, source_target_pairs={{0,112},{8,120},{16,128},{24,136},{32,144},{40,152},{48,160},{56,1... | collective-permute-start | bytes 196616 | tf_op jit(solution)/shard_map/ppermute | solution.py:357
  68.0 53.5 %all-to-all-start.2 = ((bf16[8,128,256]{2,1,0:T(8,128)(2,1)}), bf16[8,128,256]{2,1,0:T(8,128)(2,1)S(1)}, u32[]{:S(2)}, u32[]{:S(2)}) async-start(bf16[8,128,256]{2,1,0:T(8,128)(2,1)} %bitcast.3), calls=%async_computation.2 | async-start | bytes 1048576 | tf_op jit(solution)/shard_map/all_to_all | solution.py:322
  76.9 10.3 %collective-permute-start.7 = (bf16[256,128]{1,0:T(8,128)(2,1)S(1)}, bf16[256,128]{1,0:T(8,128)(2,1)S(1)}, u32[]{:S(2)}, u32[]{:S(2)}) collective-permute-start(bf16[256,128]{1,0:T(8,128)(2,1)S(1)} %get-tuple-element.25.refs_3_), channel_id=1, source_target_pairs={{504,0},{496,504},{488,496},{480,488},{472,480},{464,472},{456,464... | collective-permute-start | bytes 196616 | tf_op jit(solution)/shard_map/ppermute | solution.py:357
  79.3 9.5 %collective-permute-start.6 = (bf16[256,128]{1,0:T(8,128)(2,1)S(1)}, bf16[256,128]{1,0:T(8,128)(2,1)S(1)}, u32[]{:S(2)}, u32[]{:S(2)}) collective-permute-start(bf16[256,128]{1,0:T(8,128)(2,1)S(1)} %get-tuple-element.25.refs_3_), channel_id=1, source_target_pairs={{504,496},{496,488},{488,480},{480,472},{472,464},{464,456},{456,4... | collective-permute-start | bytes 196616 | tf_op jit(solution)/shard_map/ppermute | solution.py:357
  89.4 13.6 %collective-permute-start.9 = (bf16[256,128]{1,0:T(8,128)(2,1)S(1)}, bf16[256,128]{1,0:T(8,128)(2,1)S(1)}, u32[]{:S(2)}, u32[]{:S(2)}) collective-permute-start(bf16[256,128]{1,0:T(8,128)(2,1)S(1)} %three_back.1.refs_5_.refs_3_), channel_id=1, source_target_pairs={{504,16},{496,8},{488,0},{480,504},{472,496},{464,488},{456,480},{... | collective-permute-start | bytes 196616 | tf_op jit(solution)/shard_map/ppermute | solution.py:357
  93.6 9.4 %collective-permute-start.8 = (bf16[256,128]{1,0:T(8,128)(2,1)S(1)}, bf16[256,128]{1,0:T(8,128)(2,1)S(1)}, u32[]{:S(2)}, u32[]{:S(2)}) collective-permute-start(bf16[256,128]{1,0:T(8,128)(2,1)S(1)} %three_back.1.refs_5_.refs_3_), channel_id=1, source_target_pairs={{504,480},{496,472},{488,464},{480,456},{472,448},{464,440},{456,4... | collective-permute-start | bytes 196616 | tf_op jit(solution)/shard_map/ppermute | solution.py:357
  103.6 15.9 %collective-permute-start.11 = (bf16[256,128]{1,0:T(8,128)(2,1)S(1)}, bf16[256,128]{1,0:T(8,128)(2,1)S(1)}, u32[]{:S(2)}, u32[]{:S(2)}) collective-permute-start(bf16[256,128]{1,0:T(8,128)(2,1)S(1)} %nine_back.1.refs_3_), channel_id=1, source_target_pairs={{504,464},{496,456},{488,448},{480,440},{472,432},{464,424},{456,4... | collective-permute-start | bytes 196616 | tf_op jit(solution)/shard_map/ppermute | solution.py:357
  109.0 10.5 %collective-permute-start.10 = (bf16[256,128]{1,0:T(8,128)(2,1)S(1)}, bf16[256,128]{1,0:T(8,128)(2,1)S(1)}, u32[]{:S(2)}, u32[]{:S(2)}) collective-permute-start(bf16[256,128]{1,0:T(8,128)(2,1)S(1)} %nine_back.1.refs_3_), channel_id=1, source_target_pairs={{504,392},{496,384},{488,376},{480,368},{472,360},{464,352},{456,3... | collective-permute-start | bytes 196616 | tf_op jit(solution)/shard_map/ppermute | solution.py:357

commit v6 on v5

--- a/solution.py
+++ b/solution.py
@@ -248,11 +248,10 @@
             grad_q_ref[low:high, cols] = grad_q.astype(BF16)
 
 
-def turned_kernel(docs_ref, left_ref, right_ref, rows_ref, part_ref):
-    left, right, summed = (
-        unpacked(*field) if isinstance(field, tuple) else field for field in (left_ref, right_ref, rows_ref)
-    )
-    rows, width = part_ref.shape
+def grad_kv_kernel(docs_ref, packed_ref, grad_ref, ended_ref, part_k_ref, part_v_ref):
+    ended_ref[...] = jnp.zeros_like(ended_ref)
+    keys, values, queries = (unpacked(packed_ref, at) for at in range(3))
+    rows, width = keys.shape
     for low in range(0, rows, TILE):
         high = low + TILE
         row = low + lax.broadcasted_iota(jnp.int32, (TILE, rows - low), 0)
@@ -260,18 +259,14 @@
         mask = (row <= column) & (row >= docs_ref[0:1, low:])
         for head in range(width // HEAD_DIM):
             cols = head_cols(head)
-            turned = dot(left[low:high, cols], right[low:, cols], FEATURES)
+            q, k, v = (field[:, cols] for field in (queries, keys, values))
+            grad = grad_ref[:, cols]
+            turned = dot(v[low:high], grad[low:], FEATURES)
             turned = jnp.where(mask, turned, 0.0).astype(BF16)
-            part_ref[low:high, cols] = dot(turned, summed[low:, cols], PLAIN)
-
-
-def grad_k_kernel(docs_ref, packed_ref, grad_ref, ended_ref, part_ref):
-    ended_ref[...] = jnp.zeros_like(ended_ref)
-    turned_kernel(docs_ref, (packed_ref, 1), grad_ref, (packed_ref, 2), part_ref)
-
-
-def grad_v_kernel(docs_ref, packed_ref, grad_ref, part_ref):
-    turned_kernel(docs_ref, (packed_ref, 0), (packed_ref, 2), grad_ref, part_ref)
+            part_k_ref[low:high, cols] = dot(turned, q[low:], PLAIN)
+            turned = dot(k[low:high], q[low:], FEATURES)
+            turned = jnp.where(mask, turned, 0.0).astype(BF16)
+            part_v_ref[low:high, cols] = dot(turned, grad[low:], PLAIN)
 
 
 def last_kernel(
@@ -444,8 +439,13 @@
     )
 
     normed = across_head(normed.reshape(groups, tokens, width))
-    ended, part_k = call(
-        grad_k_kernel, "grads_k", [ENDED, f32((rows, width))], [], [docs, packed, grad], 2 * square
+    ended, part_k, part_v = call(
+        grad_kv_kernel,
+        "grads_kv",
+        [ENDED, f32((rows, width)), f32((rows, width))],
+        [],
+        [docs, packed, grad],
+        4 * square,
     )
     three = span_of_three(part, where, marks, True, [ended])
     ended, grad_q = call(
@@ -458,9 +458,6 @@
         after=[three],
     )
     nine = span_of_nine(three, where, marks, True, [ended])
-    (part_v,) = call(
-        grad_v_kernel, "grads_v", [f32((rows, width))], [], [docs, packed, grad], 2 * square, after=[nine]
-    )
     grad_k, grad_v = call(
         functools.partial(last_kernel, blocks),
         "last",

time: 124 us -> 125 us (level)
    pallas_call x15 -> x14, Pallas kernels: 26 us -> 25.7 us  [call(): pl.pallas_call(body, name=name, out_shape=outs, in_specs=[SMEM] * len(sca...]
  transfers between devices with their start and end apart: 15 -> 15, of which waited for: 6 -> 7; matrix products, arithmetic and copies ran while one was open for 0% -> 0% of each run, Pallas kernels for 17% -> 16%
where the time goes in v6:
time: 125 us; the launch traced here: 123 us
  starting transfers between devices  84.1 us (67%)
  Pallas kernels  25.7 us (21%)
  waiting for transfers between devices  10.1 us (8%)
  local copies, waits for them, and re-layouts  2.14 us (2%)
    ppermute x12, starting transfers between devices, from_block(): return lax.ppermute(field, 'seq', pairs)  60.4 us
    pallas_call x14, Pallas kernels, call(): pl.pallas_call(body, name=name, out_shape=outs, in_specs=[SMEM] * len(sca...  25.7 us
    all_to_all x3, starting transfers between devices, across_head(): lax.all_to_all(parts, 'head', split_axis=0, concat_axis=0, tiled=True)  23.7 us
    ppermute x12, waiting for transfers between devices, from_block(): return lax.ppermute(field, 'seq', pairs)  8.75 us
  transfers between devices with their start and end apart: 15, of which 7 were waited for; matrix products, arithmetic and copies ran while one was open for 0% of the time, Pallas kernels for 16%

profile of v6, /device:TPU:1, one launch (start us, length us, event | category | flops | bytes accessed | tf_op | source)
XLA Modules:
  0.0 123.0 jit_solution(18400004780218479240)
XLA Ops:
  0.6 3.1 %parts.1 = (f32[8,128]{1,0:T(8,128)}, bf16[8,256,128]{2,1,0:T(8,128)(2,1)}) custom-call(s32[32]{0:T(128)} %refs_0_.6, s32[1]{0:T(128)} %bitcast.refs_1_, s32[1]{0:T(128)} %bitcast.1.refs_2_, bf16[128,2048]{1,0:T(8,128)(2,1)} %refs_0_.7, bf16[128,2048]{1,0:T(8,128)(2,1)} %refs_1_.1), custom_call_target="tpu_custom_call" | custom-call | flops 67108864 | bytes 1576960 | tf_op jit(solution)/shard_map/parts/pallas_call | solution.py:303
  3.7 10.3 %all-to-all-start.1 = ((bf16[8,256,128]{2,1,0:T(8,128)(2,1)}), bf16[8,256,128]{2,1,0:T(8,128)(2,1)S(1)}, u32[]{:S(2)}, u32[]{:S(2)}) async-start(bf16[8,256,128]{2,1,0:T(8,128)(2,1)} %get-tuple-element.21), calls=%async_computation.1 | async-start | bytes 1048576 | tf_op jit(solution)/shard_map/all_to_all | solution.py:317
  14.8 2.5 %meta.1.refs_2_.refs_0_.refs_1_ = s32[132]{0:T(256)S(1)} custom-call(s32[32]{0:T(128)S(1)} %copy-done.3, s32[2]{0:T(128)S(1)} %pad_add_fusion.refs_1_.refs_0_, f32[8,128]{1,0:T(8,128)S(1)} %copy-done.5), custom_call_target="tpu_custom_call" | custom-call | flops 1024 | bytes 528 | tf_op jit(solution)/shard_map/meta/pallas_call | solution.py:303
  18.9 3.3 %pack.1 = (f32[8,128]{1,0:T(8,128)}, bf16[8,512,256]{2,1,0:T(8,128)(2,1)}) custom-call(bf16[128,2048]{1,0:T(8,128)(2,1)} %refs_0_.7, bf16[128,2048]{1,0:T(8,128)(2,1)} %refs_1_.1, bf16[128,2048]{1,0:T(8,128)(2,1)} %refs_2_.1, bf16[128,2048]{1,0:T(8,128)(2,1)} %refs_3_.3, s32[2,1024]{1,0:T(2,128)} %copy-done), custom_call_target="tpu_custom_call" | custom-call | bytes 4198400 | tf_op jit(solution)/shard_map/pack/pallas_call | solution.py:303
  22.2 1.4 %all-to-all-done.1.refs_1_ = bf16[8,256,128]{2,1,0:T(8,128)(2,1)S(1)} async-done(((bf16[8,256,128]{2,1,0:T(8,128)(2,1)}), bf16[8,256,128]{2,1,0:T(8,128)(2,1)S(1)}, u32[]{:S(2)}, u32[]{:S(2)}) %all-to-all-start.1) | async-done | bytes 524320 | tf_op jit(solution)/shard_map/all_to_all | solution.py:317
  23.5 4.5 %all-to-all-start = ((bf16[8,512,256]{2,1,0:T(8,128)(2,1)}), bf16[8,512,256]{2,1,0:T(8,128)(2,1)S(1)}, u32[]{:S(2)}, u32[]{:S(2)}) async-start(bf16[8,512,256]{2,1,0:T(8,128)(2,1)} %get-tuple-element.20), calls=%async_computation | async-start | bytes 4194304 | tf_op jit(solution)/shard_map/all_to_all | solution.py:317
  28.7 9.1 %collective-permute-start.1 = (bf16[256,128]{1,0:T(8,128)(2,1)S(1)}, bf16[256,128]{1,0:T(8,128)(2,1)S(1)}, u32[]{:S(2)}, u32[]{:S(2)}) collective-permute-start(bf16[256,128]{1,0:T(8,128)(2,1)S(1)} %tail.1.refs_3_), channel_id=1, source_target_pairs={{0,504},{8,0},{16,8},{24,16},{32,24},{40,32},{48,40},{56,48},{64,5... | collective-permute-start | bytes 196616 | tf_op jit(solution)/shard_map/ppermute | solution.py:352
  39.1 1.3 %collective-permute-done.refs_2_ = bf16[256,128]{1,0:T(8,128)(2,1)S(1)} collective-permute-done((bf16[256,128]{1,0:T(8,128)(2,1)S(1)}, bf16[256,128]{1,0:T(8,128)(2,1)S(1)}, u32[]{:S(2)}, u32[]{:S(2)}) %collective-permute-start) | collective-permute-done | bytes 65568 | tf_op jit(solution)/shard_map/ppermute | solution.py:352
  41.0 6.9 %collective-permute-start.3 = (bf16[256,128]{1,0:T(8,128)(2,1)S(1)}, bf16[256,128]{1,0:T(8,128)(2,1)S(1)}, u32[]{:S(2)}, u32[]{:S(2)}) collective-permute-start(bf16[256,128]{1,0:T(8,128)(2,1)S(1)} %three_forward.1.refs_3_), channel_id=1, source_target_pairs={{0,488},{8,496},{16,504},{24,0},{32,8},{40,16},{48,24},{56,32},{64... | collective-permute-start | bytes 196616 | tf_op jit(solution)/shard_map/ppermute | solution.py:352
  51.0 10.9 %collective-permute-start.5 = (bf16[256,128]{1,0:T(8,128)(2,1)S(1)}, bf16[256,128]{1,0:T(8,128)(2,1)S(1)}, u32[]{:S(2)}, u32[]{:S(2)}) collective-permute-start(bf16[256,128]{1,0:T(8,128)(2,1)S(1)} %nine_forward.1), channel_id=1, source_target_pairs={{0,40},{8,48},{16,56},{24,64},{32,72},{40,80},{48,88},{56,96},{64,... | collective-permute-start | bytes 196616 | tf_op jit(solution)/shard_map/ppermute | solution.py:352
  62.0 1.7 %collective-permute-start.4 = (bf16[256,128]{1,0:T(8,128)(2,1)S(1)}, bf16[256,128]{1,0:T(8,128)(2,1)S(1)}, u32[]{:S(2)}, u32[]{:S(2)}) collective-permute-start(bf16[256,128]{1,0:T(8,128)(2,1)S(1)} %nine_forward.1), channel_id=1, source_target_pairs={{0,112},{8,120},{16,128},{24,136},{32,144},{40,152},{48,160},{56,1... | collective-permute-start | bytes 196616 | tf_op jit(solution)/shard_map/ppermute | solution.py:352
  63.7 1.9 %intra.1.refs_3_ = f32[1024,256]{1,0:T(8,128)S(1)} custom-call(s32[2,1024]{1,0:T(2,128)S(1)} %copy-done.1, bf16[8,512,256]{2,1,0:T(8,128)(2,1)S(1)} %all-to-all-done.refs_1_.refs_2_), custom_call_target="tpu_custom_call" | custom-call | flops 536870912 | bytes 3153920 | tf_op jit(solution)/shard_map/intra/pallas_call | solution.py:303
  65.7 2.3 %norm.1 = (bf16[1024,256]{1,0:T(8,128)(2,1)}, bf16[1024,256]{1,0:T(8,128)(2,1)S(1)}, bf16[256,128]{1,0:T(8,128)(2,1)S(1)}, bf16[256,128]{1,0:T(8,128)(2,1)S(1)}) custom-call(s32[2]{0:T(128)S(1)} %pad_add_fusion.refs_1_.refs_0_, s32[132]{0:T(256)S(1)} %meta.1.refs_2_.refs_0_.refs_1_, bf16[8,512,256]{2,1,0:T(8,128)(2,1)S(1)} %all-to-all-done.refs_1_.refs_2_, ...), custom_call_target="tpu_custom_call" | custom-call | flops 134217728 | bytes 4464640 | tf_op jit(solution)/shard_map/norm/pallas_call | solution.py:303
  68.0 8.9 %all-to-all-start.2 = ((bf16[8,128,256]{2,1,0:T(8,128)(2,1)}), bf16[8,128,256]{2,1,0:T(8,128)(2,1)S(1)}, u32[]{:S(2)}, u32[]{:S(2)}) async-start(bf16[8,128,256]{2,1,0:T(8,128)(2,1)} %bitcast.3), calls=%async_computation.2 | async-start | bytes 1048576 | tf_op jit(solution)/shard_map/all_to_all | solution.py:317
  76.9 2.4 %collective-permute-start.7 = (bf16[256,128]{1,0:T(8,128)(2,1)S(1)}, bf16[256,128]{1,0:T(8,128)(2,1)S(1)}, u32[]{:S(2)}, u32[]{:S(2)}) collective-permute-start(bf16[256,128]{1,0:T(8,128)(2,1)S(1)} %get-tuple-element.26.refs_3_), channel_id=1, source_target_pairs={{504,0},{496,504},{488,496},{480,488},{472,480},{464,472},{456,464... | collective-permute-start | bytes 196616 | tf_op jit(solution)/shard_map/ppermute | solution.py:352
  80.6 3.3 %grads_kv.1 = (f32[8,128]{1,0:T(8,128)S(1)}, f32[1024,256]{1,0:T(8,128)S(1)}, f32[1024,256]{1,0:T(8,128)S(1)}) custom-call(s32[2,1024]{1,0:T(2,128)S(1)} %copy-done.1, bf16[8,512,256]{2,1,0:T(8,128)(2,1)S(1)} %all-to-all-done.refs_1_.refs_2_, bf16[1024,256]{1,0:T(8,128)(2,1)S(1)} %get-tuple-element.24.refs_2_.refs_3_), custom_call_target="tpu_custom_call" | custom-call | flops 1073741824 | bytes 4730880 | tf_op jit(solution)/shard_map/grads_kv/pallas_call | solution.py:303
  83.9 3.2 %collective-permute-done.7.refs_4_ = bf16[256,128]{1,0:T(8,128)(2,1)S(1)} collective-permute-done((bf16[256,128]{1,0:T(8,128)(2,1)S(1)}, bf16[256,128]{1,0:T(8,128)(2,1)S(1)}, u32[]{:S(2)}, u32[]{:S(2)}) %collective-permute-start.7) | collective-permute-done | bytes 65568 | tf_op jit(solution)/shard_map/ppermute | solution.py:352
  87.2 1.6 %collective-permute-done.6.refs_2_ = bf16[256,128]{1,0:T(8,128)(2,1)S(1)} collective-permute-done((bf16[256,128]{1,0:T(8,128)(2,1)S(1)}, bf16[256,128]{1,0:T(8,128)(2,1)S(1)}, u32[]{:S(2)}, u32[]{:S(2)}) %collective-permute-start.6) | collective-permute-done | bytes 65568 | tf_op jit(solution)/shard_map/ppermute | solution.py:352
  89.4 4.3 %collective-permute-start.9 = (bf16[256,128]{1,0:T(8,128)(2,1)S(1)}, bf16[256,128]{1,0:T(8,128)(2,1)S(1)}, u32[]{:S(2)}, u32[]{:S(2)}) collective-permute-start(bf16[256,128]{1,0:T(8,128)(2,1)S(1)} %three_back.1.refs_5_.refs_3_), channel_id=1, source_target_pairs={{504,16},{496,8},{488,0},{480,504},{472,496},{464,488},{456,480},{... | collective-permute-start | bytes 196616 | tf_op jit(solution)/shard_map/ppermute | solution.py:352
  93.6 6.1 %collective-permute-start.8 = (bf16[256,128]{1,0:T(8,128)(2,1)S(1)}, bf16[256,128]{1,0:T(8,128)(2,1)S(1)}, u32[]{:S(2)}, u32[]{:S(2)}) collective-permute-start(bf16[256,128]{1,0:T(8,128)(2,1)S(1)} %three_back.1.refs_5_.refs_3_), channel_id=1, source_target_pairs={{504,480},{496,472},{488,464},{480,456},{472,448},{464,440},{456,4... | collective-permute-start | bytes 196616 | tf_op jit(solution)/shard_map/ppermute | solution.py:352
  99.8 3.2 %grads_q.1 = (f32[8,128]{1,0:T(8,128)S(1)}, bf16[1024,256]{1,0:T(8,128)(2,1)}) custom-call(s32[132]{0:T(256)S(1)} %meta.1.refs_2_.refs_0_.refs_1_, s32[2,1024]{1,0:T(2,128)S(1)} %copy-done.1, bf16[8,512,256]{2,1,0:T(8,128)(2,1)S(1)} %all-to-all-done.refs_1_.refs_2_, bf16[1024,256]{1,0:T(8,128)(2,1)S(1)} %get-tuple-element.24.refs_2_.refs_3_, ...), custom_call_target="tpu_custom_call" | custom-call | flops 536870912 | bytes 3223552 | tf_op jit(solution)/shard_map/grads_q/pallas_call | solution.py:303
  103.6 6.9 %collective-permute-start.11 = (bf16[256,128]{1,0:T(8,128)(2,1)S(1)}, bf16[256,128]{1,0:T(8,128)(2,1)S(1)}, u32[]{:S(2)}, u32[]{:S(2)}) collective-permute-start(bf16[256,128]{1,0:T(8,128)(2,1)S(1)} %nine_back.1), channel_id=1, source_target_pairs={{504,464},{496,456},{488,448},{480,440},{472,432},{464,424},{456,4... | collective-permute-start | bytes 196616 | tf_op jit(solution)/shard_map/ppermute | solution.py:352
  110.5 8.3 %collective-permute-start.10 = (bf16[256,128]{1,0:T(8,128)(2,1)S(1)}, bf16[256,128]{1,0:T(8,128)(2,1)S(1)}, u32[]{:S(2)}, u32[]{:S(2)}) collective-permute-start(bf16[256,128]{1,0:T(8,128)(2,1)S(1)} %nine_back.1), channel_id=1, source_target_pairs={{504,392},{496,384},{488,376},{480,368},{472,360},{464,352},{456,3... | collective-permute-start | bytes 196616 | tf_op jit(solution)/shard_map/ppermute | solution.py:352
  120.1 2.0 %last.1 = (bf16[1024,256]{1,0:T(8,128)(2,1)}, bf16[1024,256]{1,0:T(8,128)(2,1)}) custom-call(s32[2]{0:T(128)S(1)} %pad_add_fusion.refs_1_.refs_0_, s32[132]{0:T(256)S(1)} %meta.1.refs_2_.refs_0_.refs_1_, bf16[8,512,256]{2,1,0:T(8,128)(2,1)S(1)} %all-to-all-done.refs_1_.refs_2_, f32[1024,256]{1,0:T(8,128)S(1)} %get-tuple-element.29.refs_3_, ...), custom_call_target="tpu_custom_call" | custom-call | flops 134217728 | bytes 5373952 | tf_op jit(solution)/shard_map/last/pallas_call | solution.py:303
  (34 shorter events, 12.7 us)
Async XLA Ops:
  0.6 13.5 %copy-start.3 = (s32[32]{0:T(128)S(1)}, s32[32]{0:T(128)}, u32[]{:S(2)}) copy-start(s32[32]{0:T(128)} %refs_0_.6) | copy-start | bytes 388
  3.7 19.8 %all-to-all-start.1 = ((bf16[8,256,128]{2,1,0:T(8,128)(2,1)}), bf16[8,256,128]{2,1,0:T(8,128)(2,1)S(1)}, u32[]{:S(2)}, u32[]{:S(2)}) async-start(bf16[8,256,128]{2,1,0:T(8,128)(2,1)} %get-tuple-element.21), calls=%async_computation.1 | async-start | bytes 1048576 | tf_op jit(solution)/shard_map/all_to_all | solution.py:317
  14.1 0.7 copy-start.5
  18.3 0.6 copy-start
  23.5 4.5 %copy-start.4 = (f32[8,128]{1,0:T(8,128)S(1)}, f32[8,128]{1,0:T(8,128)}, u32[]{:S(2)}) copy-start(f32[8,128]{1,0:T(8,128)} %get-tuple-element.22.refs_2_) | copy-start | bytes 12292
  23.5 40.2 %copy-start.1 = (s32[2,1024]{1,0:T(2,128)S(1)}, s32[2,1024]{1,0:T(2,128)}, u32[]{:S(2)}) copy-start(s32[2,1024]{1,0:T(2,128)} %copy-done) | copy-start | bytes 24580
  23.5 40.2 %all-to-all-start = ((bf16[8,512,256]{2,1,0:T(8,128)(2,1)}), bf16[8,512,256]{2,1,0:T(8,128)(2,1)S(1)}, u32[]{:S(2)}, u32[]{:S(2)}) async-start(bf16[8,512,256]{2,1,0:T(8,128)(2,1)} %get-tuple-element.20), calls=%async_computation | async-start | bytes 4194304 | tf_op jit(solution)/shard_map/all_to_all | solution.py:317
  28.0 37.6 %copy-start.2 = (f32[2048]{0:T(1024)S(1)}, f32[2048]{0:T(1024)}, u32[]{:S(2)}) copy-start(f32[2048]{0:T(1024)} %param.10) | copy-start | bytes 24580
  28.7 10.4 %collective-permute-start.1 = (bf16[256,128]{1,0:T(8,128)(2,1)S(1)}, bf16[256,128]{1,0:T(8,128)(2,1)S(1)}, u32[]{:S(2)}, u32[]{:S(2)}) collective-permute-start(bf16[256,128]{1,0:T(8,128)(2,1)S(1)} %tail.1.refs_3_), channel_id=1, source_target_pairs={{0,504},{8,0},{16,8},{24,16},{32,24},{40,32},{48,40},{56,48},{64,5... | collective-permute-start | bytes 196616 | tf_op jit(solution)/shard_map/ppermute | solution.py:352
  37.8 2.6 %collective-permute-start = (bf16[256,128]{1,0:T(8,128)(2,1)S(1)}, bf16[256,128]{1,0:T(8,128)(2,1)S(1)}, u32[]{:S(2)}, u32[]{:S(2)}) collective-permute-start(bf16[256,128]{1,0:T(8,128)(2,1)S(1)} %tail.1.refs_3_), channel_id=1, source_target_pairs={{0,8},{8,16},{16,24},{24,32},{32,40},{40,48},{48,56},{56,64},{64,7... | collective-permute-start | bytes 196616 | tf_op jit(solution)/shard_map/ppermute | solution.py:352
  41.0 8.9 %collective-permute-start.3 = (bf16[256,128]{1,0:T(8,128)(2,1)S(1)}, bf16[256,128]{1,0:T(8,128)(2,1)S(1)}, u32[]{:S(2)}, u32[]{:S(2)}) collective-permute-start(bf16[256,128]{1,0:T(8,128)(2,1)S(1)} %three_forward.1.refs_3_), channel_id=1, source_target_pairs={{0,488},{8,496},{16,504},{24,0},{32,8},{40,16},{48,24},{56,32},{64... | collective-permute-start | bytes 196616 | tf_op jit(solution)/shard_map/ppermute | solution.py:352
  47.8 2.6 %collective-permute-start.2 = (bf16[256,128]{1,0:T(8,128)(2,1)S(1)}, bf16[256,128]{1,0:T(8,128)(2,1)S(1)}, u32[]{:S(2)}, u32[]{:S(2)}) collective-permute-start(bf16[256,128]{1,0:T(8,128)(2,1)S(1)} %three_forward.1.refs_3_), channel_id=1, source_target_pairs={{0,24},{8,32},{16,40},{24,48},{32,56},{40,64},{48,72},{56,80},{64,... | collective-permute-start | bytes 196616 | tf_op jit(solution)/shard_map/ppermute | solution.py:352
  51.0 14.6 %collective-permute-start.5 = (bf16[256,128]{1,0:T(8,128)(2,1)S(1)}, bf16[256,128]{1,0:T(8,128)(2,1)S(1)}, u32[]{:S(2)}, u32[]{:S(2)}) collective-permute-start(bf16[256,128]{1,0:T(8,128)(2,1)S(1)} %nine_forward.1), channel_id=1, source_target_pairs={{0,40},{8,48},{16,56},{24,64},{32,72},{40,80},{48,88},{56,96},{64,... | collective-permute-start | bytes 196616 | tf_op jit(solution)/shard_map/ppermute | solution.py:352
  62.0 3.7 %collective-permute-start.4 = (bf16[256,128]{1,0:T(8,128)(2,1)S(1)}, bf16[256,128]{1,0:T(8,128)(2,1)S(1)}, u32[]{:S(2)}, u32[]{:S(2)}) collective-permute-start(bf16[256,128]{1,0:T(8,128)(2,1)S(1)} %nine_forward.1), channel_id=1, source_target_pairs={{0,112},{8,120},{16,128},{24,136},{32,144},{40,152},{48,160},{56,1... | collective-permute-start | bytes 196616 | tf_op jit(solution)/shard_map/ppermute | solution.py:352
  68.0 54.1 %all-to-all-start.2 = ((bf16[8,128,256]{2,1,0:T(8,128)(2,1)}), bf16[8,128,256]{2,1,0:T(8,128)(2,1)S(1)}, u32[]{:S(2)}, u32[]{:S(2)}) async-start(bf16[8,128,256]{2,1,0:T(8,128)(2,1)} %bitcast.3), calls=%async_computation.2 | async-start | bytes 1048576 | tf_op jit(solution)/shard_map/all_to_all | solution.py:317
  76.9 10.3 %collective-permute-start.7 = (bf16[256,128]{1,0:T(8,128)(2,1)S(1)}, bf16[256,128]{1,0:T(8,128)(2,1)S(1)}, u32[]{:S(2)}, u32[]{:S(2)}) collective-permute-start(bf16[256,128]{1,0:T(8,128)(2,1)S(1)} %get-tuple-element.26.refs_3_), channel_id=1, source_target_pairs={{504,0},{496,504},{488,496},{480,488},{472,480},{464,472},{456,464... | collective-permute-start | bytes 196616 | tf_op jit(solution)/shard_map/ppermute | solution.py:352
  79.3 9.5 %collective-permute-start.6 = (bf16[256,128]{1,0:T(8,128)(2,1)S(1)}, bf16[256,128]{1,0:T(8,128)(2,1)S(1)}, u32[]{:S(2)}, u32[]{:S(2)}) collective-permute-start(bf16[256,128]{1,0:T(8,128)(2,1)S(1)} %get-tuple-element.26.refs_3_), channel_id=1, source_target_pairs={{504,496},{496,488},{488,480},{480,472},{472,464},{464,456},{456,4... | collective-permute-start | bytes 196616 | tf_op jit(solution)/shard_map/ppermute | solution.py:352
  89.4 13.6 %collective-permute-start.9 = (bf16[256,128]{1,0:T(8,128)(2,1)S(1)}, bf16[256,128]{1,0:T(8,128)(2,1)S(1)}, u32[]{:S(2)}, u32[]{:S(2)}) collective-permute-start(bf16[256,128]{1,0:T(8,128)(2,1)S(1)} %three_back.1.refs_5_.refs_3_), channel_id=1, source_target_pairs={{504,16},{496,8},{488,0},{480,504},{472,496},{464,488},{456,480},{... | collective-permute-start | bytes 196616 | tf_op jit(solution)/shard_map/ppermute | solution.py:352
  93.6 9.4 %collective-permute-start.8 = (bf16[256,128]{1,0:T(8,128)(2,1)S(1)}, bf16[256,128]{1,0:T(8,128)(2,1)S(1)}, u32[]{:S(2)}, u32[]{:S(2)}) collective-permute-start(bf16[256,128]{1,0:T(8,128)(2,1)S(1)} %three_back.1.refs_5_.refs_3_), channel_id=1, source_target_pairs={{504,480},{496,472},{488,464},{480,456},{472,448},{464,440},{456,4... | collective-permute-start | bytes 196616 | tf_op jit(solution)/shard_map/ppermute | solution.py:352
  103.6 15.2 %collective-permute-start.11 = (bf16[256,128]{1,0:T(8,128)(2,1)S(1)}, bf16[256,128]{1,0:T(8,128)(2,1)S(1)}, u32[]{:S(2)}, u32[]{:S(2)}) collective-permute-start(bf16[256,128]{1,0:T(8,128)(2,1)S(1)} %nine_back.1), channel_id=1, source_target_pairs={{504,464},{496,456},{488,448},{480,440},{472,432},{464,424},{456,4... | collective-permute-start | bytes 196616 | tf_op jit(solution)/shard_map/ppermute | solution.py:352
  110.5 9.6 %collective-permute-start.10 = (bf16[256,128]{1,0:T(8,128)(2,1)S(1)}, bf16[256,128]{1,0:T(8,128)(2,1)S(1)}, u32[]{:S(2)}, u32[]{:S(2)}) collective-permute-start(bf16[256,128]{1,0:T(8,128)(2,1)S(1)} %nine_back.1), channel_id=1, source_target_pairs={{504,392},{496,384},{488,376},{480,368},{472,360},{464,352},{456,3... | collective-permute-start | bytes 196616 | tf_op jit(solution)/shard_map/ppermute | solution.py:352

commit v7 on v5

--- a/solution.py
+++ b/solution.py
@@ -35,7 +35,7 @@
     return slice(head * HEAD_DIM, (head + 1) * HEAD_DIM)
 
 
-def meta_kernel(blocks, rows, lengths_ref, where_ref, marks_ref):
+def meta_kernel(blocks, rows, lengths_ref, where_ref, marks_ref, docs_ref):
     first = where_ref[0] * rows
     last = first + rows - 1
 
@@ -48,7 +48,10 @@
     marks_ref[2 * blocks + 1] = 0
     marks_ref[2 * blocks + 3] = rows
 
-    def step(i, begin):
+    place = first + lax.broadcasted_iota(jnp.int32, (1, rows), 1)
+
+    def step(i, carry):
+        begin, start, end = carry
         after = begin + lengths_ref[i]
         marks_ref[begin // rows] = 1
         marks_ref[blocks + jnp.maximum(begin - 1, 0) // rows] = 1
@@ -63,30 +66,17 @@
             marks_ref[2 * blocks + 2] = begin - first
             marks_ref[2 * blocks + 3] = jnp.where(after > last + 1, begin - first, rows)
 
-        return after
-
-    lax.fori_loop(0, lengths_ref.shape[0], step, jnp.int32(0))
-
-
-def docs_kernel(lengths_ref, where_ref, marks_ref, span_ref):
-    rows = span_ref.shape[1]
-    first = where_ref[0] * rows
-    place = first + lax.broadcasted_iota(jnp.int32, (1, rows), 1)
-
-    def step(i, carry):
-        begin, start, end = carry
-        after = begin + lengths_ref[i]
         inside = (place >= begin) & (place < after)
         return (after, jnp.where(inside, begin, start), jnp.where(inside, after, end))
 
     zero = jnp.zeros((1, rows), jnp.int32)
     _, start, end = lax.fori_loop(0, lengths_ref.shape[0], step, (jnp.int32(0), zero, zero))
-    span_ref[0:1, :] = start - first
-    span_ref[1:2, :] = end - first
+    docs_ref[0:1, :] = start - first
+    docs_ref[1:2, :] = end - first
 
 
 def pack_kernel(*refs):
-    *arrays, ended_ref, out_ref, held, in_sems, out_sems = refs
+    _, *arrays, ended_ref, out_ref, held, in_sems, out_sems = refs
     ended_ref[...] = jnp.zeros_like(ended_ref)
     groups, _, width = out_ref.shape
     tokens = arrays[0].shape[0]
@@ -322,14 +312,14 @@
     return lax.all_to_all(parts, "head", split_axis=0, concat_axis=0, tiled=True)
 
 
-def to_heads(arrays, after):
+def to_heads(arrays, marks):
     groups, count = lax.axis_size("head"), len(arrays)
     tokens, cols = arrays[0].shape
     ended, packed = call(
         pack_kernel,
         "pack",
         [ENDED, jax.ShapeDtypeStruct((groups, count * tokens, cols // groups), BF16)],
-        [],
+        [marks],
         arrays,
         0,
         [
@@ -337,7 +327,7 @@
             pltpu.SemaphoreType.DMA((count,)),
             pltpu.SemaphoreType.DMA((count, groups)),
         ],
-        after,
+        (),
         [ANYWHERE] * count,
         [VMEM, ANYWHERE],
         60,
@@ -408,19 +398,18 @@
         in_specs=[ANYWHERE] * 2,
         limit=60,
     )
-    (marks,) = call(
+    marks, docs = call(
         functools.partial(meta_kernel, blocks, rows),
         "meta",
-        [int32((2 * blocks + 4,))],
+        [int32((2 * blocks + 4,)), int32((2, rows))],
         [lengths, where],
         [],
         rows,
         after=[started],
-        out_specs=[SMEM],
-    )
-    (docs,) = call(docs_kernel, "docs", [int32((2, rows))], [lengths, where, marks], [], rows)
+        out_specs=[SMEM, VMEM],
+    )
     gathered = across_head(parts)
-    ended, packed = to_heads([keys, values, queries, cotangent], [docs])
+    ended, packed = to_heads([keys, values, queries, cotangent], marks)
     (tail,) = call(
         tail_kernel,
         "tail",

time: 124 us -> 124 us (level)
    pallas_call x15 -> x14, Pallas kernels: 26 us -> 25.8 us  [call(): pl.pallas_call(body, name=name, out_shape=outs, in_specs=[SMEM] * len(sca...]
where the time goes in v7:
time: 124 us; the launch traced here: 122 us
  starting transfers between devices  83 us (67%)
  Pallas kernels  25.8 us (21%)
  waiting for transfers between devices  10.5 us (8%)
  local copies, waits for them, and re-layouts  2.11 us (2%)
    ppermute x12, starting transfers between devices, from_block(): return lax.ppermute(field, 'seq', pairs)  59.3 us
    pallas_call x14, Pallas kernels, call(): pl.pallas_call(body, name=name, out_shape=outs, in_specs=[SMEM] * len(sca...  25.8 us
    all_to_all x3, starting transfers between devices, across_head(): lax.all_to_all(parts, 'head', split_axis=0, concat_axis=0, tiled=True)  23.7 us
    ppermute x12, waiting for transfers between devices, from_block(): return lax.ppermute(field, 'seq', pairs)  8.98 us
  transfers between devices with their start and end apart: 15, of which 6 were waited for; matrix products, arithmetic and copies ran while one was open for 0% of the time, Pallas kernels for 17%

profile of v7, /device:TPU:1, one launch (start us, length us, event | category | flops | bytes accessed | tf_op | source)
XLA Modules:
  0.0 122.3 jit_solution(12229655117101126648)
XLA Ops:
  0.6 3.1 %parts.1 = (f32[8,128]{1,0:T(8,128)}, bf16[8,256,128]{2,1,0:T(8,128)(2,1)}) custom-call(s32[32]{0:T(128)} %refs_0_.3, s32[1]{0:T(128)} %bitcast.refs_1_, s32[1]{0:T(128)} %bitcast.1.refs_2_, bf16[128,2048]{1,0:T(8,128)(2,1)} %refs_1_.1, bf16[128,2048]{1,0:T(8,128)(2,1)} %refs_2_.1), custom_call_target="tpu_custom_call" | custom-call | flops 67108864 | bytes 1576960 | tf_op jit(solution)/shard_map/parts/pallas_call | solution.py:298
  3.7 10.3 %all-to-all-start.1 = ((bf16[8,256,128]{2,1,0:T(8,128)(2,1)}), bf16[8,256,128]{2,1,0:T(8,128)(2,1)S(1)}, u32[]{:S(2)}, u32[]{:S(2)}) async-start(bf16[8,256,128]{2,1,0:T(8,128)(2,1)} %get-tuple-element.24), calls=%async_computation.1 | async-start | bytes 1048576 | tf_op jit(solution)/shard_map/all_to_all | solution.py:312
  14.8 2.6 %meta.1 = (s32[132]{0:T(256)S(1)}, s32[2,1024]{1,0:T(2,128)S(1)}) custom-call(s32[32]{0:T(128)S(1)} %copy-done.5, s32[2]{0:T(128)S(1)} %pad_add_fusion.refs_1_.refs_0_, f32[8,128]{1,0:T(8,128)S(1)} %copy-done.4), custom_call_target="tpu_custom_call" | custom-call | flops 1024 | bytes 8720 | tf_op jit(solution)/shard_map/meta/pallas_call | solution.py:298
  17.9 4.1 %pack.1 = (f32[8,128]{1,0:T(8,128)}, bf16[8,512,256]{2,1,0:T(8,128)(2,1)}) custom-call(s32[132]{0:T(256)} %copy-done, bf16[128,2048]{1,0:T(8,128)(2,1)} %refs_1_.1, bf16[128,2048]{1,0:T(8,128)(2,1)} %refs_2_.1, bf16[128,2048]{1,0:T(8,128)(2,1)} %refs_3_.3, bf16[128,2048]{1,0:T(8,128)(2,1)} %refs_4_.3), custom_call_target="tpu_custom_call" | custom-call | bytes 4198400 | tf_op jit(solution)/shard_map/pack/pallas_call | solution.py:298
  22.0 1.5 %all-to-all-done.1.refs_1_ = bf16[8,256,128]{2,1,0:T(8,128)(2,1)S(1)} async-done(((bf16[8,256,128]{2,1,0:T(8,128)(2,1)}), bf16[8,256,128]{2,1,0:T(8,128)(2,1)S(1)}, u32[]{:S(2)}, u32[]{:S(2)}) %all-to-all-start.1) | async-done | bytes 524320 | tf_op jit(solution)/shard_map/all_to_all | solution.py:312
  23.5 4.5 %all-to-all-start = ((bf16[8,512,256]{2,1,0:T(8,128)(2,1)}), bf16[8,512,256]{2,1,0:T(8,128)(2,1)S(1)}, u32[]{:S(2)}, u32[]{:S(2)}) async-start(bf16[8,512,256]{2,1,0:T(8,128)(2,1)} %get-tuple-element.22), calls=%async_computation | async-start | bytes 4194304 | tf_op jit(solution)/shard_map/all_to_all | solution.py:312
  28.7 9.1 %collective-permute-start.1 = (bf16[256,128]{1,0:T(8,128)(2,1)S(1)}, bf16[256,128]{1,0:T(8,128)(2,1)S(1)}, u32[]{:S(2)}, u32[]{:S(2)}) collective-permute-start(bf16[256,128]{1,0:T(8,128)(2,1)S(1)} %tail.1.refs_3_), channel_id=1, source_target_pairs={{0,504},{8,0},{16,8},{24,16},{32,24},{40,32},{48,40},{56,48},{64,5... | collective-permute-start | bytes 196616 | tf_op jit(solution)/shard_map/ppermute | solution.py:347
  41.0 6.9 %collective-permute-start.3 = (bf16[256,128]{1,0:T(8,128)(2,1)S(1)}, bf16[256,128]{1,0:T(8,128)(2,1)S(1)}, u32[]{:S(2)}, u32[]{:S(2)}) collective-permute-start(bf16[256,128]{1,0:T(8,128)(2,1)S(1)} %three_forward.1.refs_3_), channel_id=1, source_target_pairs={{0,488},{8,496},{16,504},{24,0},{32,8},{40,16},{48,24},{56,32},{64... | collective-permute-start | bytes 196616 | tf_op jit(solution)/shard_map/ppermute | solution.py:347
  51.1 10.9 %collective-permute-start.5 = (bf16[256,128]{1,0:T(8,128)(2,1)S(1)}, bf16[256,128]{1,0:T(8,128)(2,1)S(1)}, u32[]{:S(2)}, u32[]{:S(2)}) collective-permute-start(bf16[256,128]{1,0:T(8,128)(2,1)S(1)} %nine_forward.1), channel_id=1, source_target_pairs={{0,40},{8,48},{16,56},{24,64},{32,72},{40,80},{48,88},{56,96},{64,... | collective-permute-start | bytes 196616 | tf_op jit(solution)/shard_map/ppermute | solution.py:347
  62.0 1.7 %collective-permute-start.4 = (bf16[256,128]{1,0:T(8,128)(2,1)S(1)}, bf16[256,128]{1,0:T(8,128)(2,1)S(1)}, u32[]{:S(2)}, u32[]{:S(2)}) collective-permute-start(bf16[256,128]{1,0:T(8,128)(2,1)S(1)} %nine_forward.1), channel_id=1, source_target_pairs={{0,112},{8,120},{16,128},{24,136},{32,144},{40,152},{48,160},{56,1... | collective-permute-start | bytes 196616 | tf_op jit(solution)/shard_map/ppermute | solution.py:347
  63.7 1.9 %intra.1.refs_3_ = f32[1024,256]{1,0:T(8,128)S(1)} custom-call(s32[2,1024]{1,0:T(2,128)S(1)} %get-tuple-element.23.refs_0_.refs_1_, bf16[8,512,256]{2,1,0:T(8,128)(2,1)S(1)} %all-to-all-done.refs_1_.refs_2_), custom_call_target="tpu_custom_call" | custom-call | flops 536870912 | bytes 3153920 | tf_op jit(solution)/shard_map/intra/pallas_call | solution.py:298
  65.7 2.3 %norm.1 = (bf16[1024,256]{1,0:T(8,128)(2,1)}, bf16[1024,256]{1,0:T(8,128)(2,1)S(1)}, bf16[256,128]{1,0:T(8,128)(2,1)S(1)}, bf16[256,128]{1,0:T(8,128)(2,1)S(1)}) custom-call(s32[2]{0:T(128)S(1)} %pad_add_fusion.refs_1_.refs_0_, s32[132]{0:T(256)S(1)} %copy-done.1, bf16[8,512,256]{2,1,0:T(8,128)(2,1)S(1)} %all-to-all-done.refs_1_.refs_2_, ...), custom_call_target="tpu_custom_call" | custom-call | flops 134217728 | bytes 4464640 | tf_op jit(solution)/shard_map/norm/pallas_call | solution.py:298
  68.0 8.9 %all-to-all-start.2 = ((bf16[8,128,256]{2,1,0:T(8,128)(2,1)}), bf16[8,128,256]{2,1,0:T(8,128)(2,1)S(1)}, u32[]{:S(2)}, u32[]{:S(2)}) async-start(bf16[8,128,256]{2,1,0:T(8,128)(2,1)} %bitcast.3), calls=%async_computation.2 | async-start | bytes 1048576 | tf_op jit(solution)/shard_map/all_to_all | solution.py:312
  76.9 2.4 %collective-permute-start.7 = (bf16[256,128]{1,0:T(8,128)(2,1)S(1)}, bf16[256,128]{1,0:T(8,128)(2,1)S(1)}, u32[]{:S(2)}, u32[]{:S(2)}) collective-permute-start(bf16[256,128]{1,0:T(8,128)(2,1)S(1)} %get-tuple-element.29.refs_3_), channel_id=1, source_target_pairs={{504,0},{496,504},{488,496},{480,488},{472,480},{464,472},{456,464... | collective-permute-start | bytes 196616 | tf_op jit(solution)/shard_map/ppermute | solution.py:347
  80.6 1.8 %grads_k.1 = (f32[8,128]{1,0:T(8,128)S(1)}, f32[1024,256]{1,0:T(8,128)S(1)}) custom-call(s32[2,1024]{1,0:T(2,128)S(1)} %get-tuple-element.23.refs_0_.refs_1_, bf16[8,512,256]{2,1,0:T(8,128)(2,1)S(1)} %all-to-all-done.refs_1_.refs_2_, bf16[1024,256]{1,0:T(8,128)(2,1)S(1)} %get-tuple-element.27.refs_2_.refs_3_), custom_call_target="tpu_custom_call" | custom-call | flops 536870912 | bytes 3682304 | tf_op jit(solution)/shard_map/grads_k/pallas_call | solution.py:298
  82.4 4.8 %collective-permute-done.7.refs_4_ = bf16[256,128]{1,0:T(8,128)(2,1)S(1)} collective-permute-done((bf16[256,128]{1,0:T(8,128)(2,1)S(1)}, bf16[256,128]{1,0:T(8,128)(2,1)S(1)}, u32[]{:S(2)}, u32[]{:S(2)}) %collective-permute-start.7) | collective-permute-done | bytes 65568 | tf_op jit(solution)/shard_map/ppermute | solution.py:347
  87.2 1.6 %collective-permute-done.6.refs_2_ = bf16[256,128]{1,0:T(8,128)(2,1)S(1)} collective-permute-done((bf16[256,128]{1,0:T(8,128)(2,1)S(1)}, bf16[256,128]{1,0:T(8,128)(2,1)S(1)}, u32[]{:S(2)}, u32[]{:S(2)}) %collective-permute-start.6) | collective-permute-done | bytes 65568 | tf_op jit(solution)/shard_map/ppermute | solution.py:347
  89.4 4.3 %collective-permute-start.9 = (bf16[256,128]{1,0:T(8,128)(2,1)S(1)}, bf16[256,128]{1,0:T(8,128)(2,1)S(1)}, u32[]{:S(2)}, u32[]{:S(2)}) collective-permute-start(bf16[256,128]{1,0:T(8,128)(2,1)S(1)} %three_back.1.refs_5_.refs_3_), channel_id=1, source_target_pairs={{504,16},{496,8},{488,0},{480,504},{472,496},{464,488},{456,480},{... | collective-permute-start | bytes 196616 | tf_op jit(solution)/shard_map/ppermute | solution.py:347
  93.6 6.1 %collective-permute-start.8 = (bf16[256,128]{1,0:T(8,128)(2,1)S(1)}, bf16[256,128]{1,0:T(8,128)(2,1)S(1)}, u32[]{:S(2)}, u32[]{:S(2)}) collective-permute-start(bf16[256,128]{1,0:T(8,128)(2,1)S(1)} %three_back.1.refs_5_.refs_3_), channel_id=1, source_target_pairs={{504,480},{496,472},{488,464},{480,456},{472,448},{464,440},{456,4... | collective-permute-start | bytes 196616 | tf_op jit(solution)/shard_map/ppermute | solution.py:347
  99.8 3.2 %grads_q.1 = (f32[8,128]{1,0:T(8,128)S(1)}, bf16[1024,256]{1,0:T(8,128)(2,1)}) custom-call(s32[132]{0:T(256)S(1)} %copy-done.1, s32[2,1024]{1,0:T(2,128)S(1)} %get-tuple-element.23.refs_0_.refs_1_, bf16[8,512,256]{2,1,0:T(8,128)(2,1)S(1)} %all-to-all-done.refs_1_.refs_2_, bf16[1024,256]{1,0:T(8,128)(2,1)S(1)} %get-tuple-element.27.refs_2_.refs_3_, ...), custom_call_target="tpu_custom_call" | custom-call | flops 536870912 | bytes 3223552 | tf_op jit(solution)/shard_map/grads_q/pallas_call | solution.py:298
  103.6 5.4 %collective-permute-start.11 = (bf16[256,128]{1,0:T(8,128)(2,1)S(1)}, bf16[256,128]{1,0:T(8,128)(2,1)S(1)}, u32[]{:S(2)}, u32[]{:S(2)}) collective-permute-start(bf16[256,128]{1,0:T(8,128)(2,1)S(1)} %nine_back.1.refs_3_), channel_id=1, source_target_pairs={{504,464},{496,456},{488,448},{480,440},{472,432},{464,424},{456,4... | collective-permute-start | bytes 196616 | tf_op jit(solution)/shard_map/ppermute | solution.py:347
  108.9 8.7 %collective-permute-start.10 = (bf16[256,128]{1,0:T(8,128)(2,1)S(1)}, bf16[256,128]{1,0:T(8,128)(2,1)S(1)}, u32[]{:S(2)}, u32[]{:S(2)}) collective-permute-start(bf16[256,128]{1,0:T(8,128)(2,1)S(1)} %nine_back.1.refs_3_), channel_id=1, source_target_pairs={{504,392},{496,384},{488,376},{480,368},{472,360},{464,352},{456,3... | collective-permute-start | bytes 196616 | tf_op jit(solution)/shard_map/ppermute | solution.py:347
  117.6 1.8 %grads_v.1.refs_4_ = f32[1024,256]{1,0:T(8,128)S(1)} custom-call(s32[2,1024]{1,0:T(2,128)S(1)} %get-tuple-element.23.refs_0_.refs_1_, bf16[8,512,256]{2,1,0:T(8,128)(2,1)S(1)} %all-to-all-done.refs_1_.refs_2_, bf16[1024,256]{1,0:T(8,128)(2,1)S(1)} %get-tuple-element.27.refs_2_.refs_3_, bf16[256,128]{1,0:T(8,128)(2,1)S(1)} %nine_back.1.refs_3_), custom_call_target="tpu_custom_call" | custom-call | flops 536870912 | bytes 3678208 | tf_op jit(solution)/shard_map/grads_v/pallas_call | solution.py:298
  119.5 2.0 %last.1 = (bf16[1024,256]{1,0:T(8,128)(2,1)}, bf16[1024,256]{1,0:T(8,128)(2,1)}) custom-call(s32[2]{0:T(128)S(1)} %pad_add_fusion.refs_1_.refs_0_, s32[132]{0:T(256)S(1)} %copy-done.1, bf16[8,512,256]{2,1,0:T(8,128)(2,1)S(1)} %all-to-all-done.refs_1_.refs_2_, f32[1024,256]{1,0:T(8,128)S(1)} %get-tuple-element.32.refs_3_, f32[1024,256]{1,0:T(8,128)S(1)} %grads_v.1.refs_4_, ...), custom_call_target="tpu_custom_call" | custom-call | flops 134217728 | bytes 5373952 | tf_op jit(solution)/shard_map/last/pallas_call | solution.py:298
  (34 shorter events, 11.7 us)
Async XLA Ops:
  0.6 13.5 %copy-start.5 = (s32[32]{0:T(128)S(1)}, s32[32]{0:T(128)}, u32[]{:S(2)}) copy-start(s32[32]{0:T(128)} %refs_0_.3) | copy-start | bytes 388
  3.7 19.8 %all-to-all-start.1 = ((bf16[8,256,128]{2,1,0:T(8,128)(2,1)}), bf16[8,256,128]{2,1,0:T(8,128)(2,1)S(1)}, u32[]{:S(2)}, u32[]{:S(2)}) async-start(bf16[8,256,128]{2,1,0:T(8,128)(2,1)} %get-tuple-element.24), calls=%async_computation.1 | async-start | bytes 1048576 | tf_op jit(solution)/shard_map/all_to_all | solution.py:312
  14.1 0.7 copy-start.4
  17.4 0.6 copy-start
  23.5 4.5 %copy-start.1 = (s32[132]{0:T(256)S(1)}, s32[132]{0:T(256)}, u32[]{:S(2)}) copy-start(s32[132]{0:T(256)} %copy-done) | copy-start | bytes 1588
  23.5 4.5 %copy-start.3 = (f32[8,128]{1,0:T(8,128)S(1)}, f32[8,128]{1,0:T(8,128)}, u32[]{:S(2)}) copy-start(f32[8,128]{1,0:T(8,128)} %get-tuple-element.25.refs_2_) | copy-start | bytes 12292
  23.5 40.2 %all-to-all-start = ((bf16[8,512,256]{2,1,0:T(8,128)(2,1)}), bf16[8,512,256]{2,1,0:T(8,128)(2,1)S(1)}, u32[]{:S(2)}, u32[]{:S(2)}) async-start(bf16[8,512,256]{2,1,0:T(8,128)(2,1)} %get-tuple-element.22), calls=%async_computation | async-start | bytes 4194304 | tf_op jit(solution)/shard_map/all_to_all | solution.py:312
  28.0 37.6 %copy-start.2 = (f32[2048]{0:T(1024)S(1)}, f32[2048]{0:T(1024)}, u32[]{:S(2)}) copy-start(f32[2048]{0:T(1024)} %param.10) | copy-start | bytes 24580
  28.7 10.4 %collective-permute-start.1 = (bf16[256,128]{1,0:T(8,128)(2,1)S(1)}, bf16[256,128]{1,0:T(8,128)(2,1)S(1)}, u32[]{:S(2)}, u32[]{:S(2)}) collective-permute-start(bf16[256,128]{1,0:T(8,128)(2,1)S(1)} %tail.1.refs_3_), channel_id=1, source_target_pairs={{0,504},{8,0},{16,8},{24,16},{32,24},{40,32},{48,40},{56,48},{64,5... | collective-permute-start | bytes 196616 | tf_op jit(solution)/shard_map/ppermute | solution.py:347
  37.8 2.6 %collective-permute-start = (bf16[256,128]{1,0:T(8,128)(2,1)S(1)}, bf16[256,128]{1,0:T(8,128)(2,1)S(1)}, u32[]{:S(2)}, u32[]{:S(2)}) collective-permute-start(bf16[256,128]{1,0:T(8,128)(2,1)S(1)} %tail.1.refs_3_), channel_id=1, source_target_pairs={{0,8},{8,16},{16,24},{24,32},{32,40},{40,48},{48,56},{56,64},{64,7... | collective-permute-start | bytes 196616 | tf_op jit(solution)/shard_map/ppermute | solution.py:347
  41.0 8.9 %collective-permute-start.3 = (bf16[256,128]{1,0:T(8,128)(2,1)S(1)}, bf16[256,128]{1,0:T(8,128)(2,1)S(1)}, u32[]{:S(2)}, u32[]{:S(2)}) collective-permute-start(bf16[256,128]{1,0:T(8,128)(2,1)S(1)} %three_forward.1.refs_3_), channel_id=1, source_target_pairs={{0,488},{8,496},{16,504},{24,0},{32,8},{40,16},{48,24},{56,32},{64... | collective-permute-start | bytes 196616 | tf_op jit(solution)/shard_map/ppermute | solution.py:347
  47.8 2.6 %collective-permute-start.2 = (bf16[256,128]{1,0:T(8,128)(2,1)S(1)}, bf16[256,128]{1,0:T(8,128)(2,1)S(1)}, u32[]{:S(2)}, u32[]{:S(2)}) collective-permute-start(bf16[256,128]{1,0:T(8,128)(2,1)S(1)} %three_forward.1.refs_3_), channel_id=1, source_target_pairs={{0,24},{8,32},{16,40},{24,48},{32,56},{40,64},{48,72},{56,80},{64,... | collective-permute-start | bytes 196616 | tf_op jit(solution)/shard_map/ppermute | solution.py:347
  51.1 14.6 %collective-permute-start.5 = (bf16[256,128]{1,0:T(8,128)(2,1)S(1)}, bf16[256,128]{1,0:T(8,128)(2,1)S(1)}, u32[]{:S(2)}, u32[]{:S(2)}) collective-permute-start(bf16[256,128]{1,0:T(8,128)(2,1)S(1)} %nine_forward.1), channel_id=1, source_target_pairs={{0,40},{8,48},{16,56},{24,64},{32,72},{40,80},{48,88},{56,96},{64,... | collective-permute-start | bytes 196616 | tf_op jit(solution)/shard_map/ppermute | solution.py:347
  62.0 3.7 %collective-permute-start.4 = (bf16[256,128]{1,0:T(8,128)(2,1)S(1)}, bf16[256,128]{1,0:T(8,128)(2,1)S(1)}, u32[]{:S(2)}, u32[]{:S(2)}) collective-permute-start(bf16[256,128]{1,0:T(8,128)(2,1)S(1)} %nine_forward.1), channel_id=1, source_target_pairs={{0,112},{8,120},{16,128},{24,136},{32,144},{40,152},{48,160},{56,1... | collective-permute-start | bytes 196616 | tf_op jit(solution)/shard_map/ppermute | solution.py:347
  68.0 53.5 %all-to-all-start.2 = ((bf16[8,128,256]{2,1,0:T(8,128)(2,1)}), bf16[8,128,256]{2,1,0:T(8,128)(2,1)S(1)}, u32[]{:S(2)}, u32[]{:S(2)}) async-start(bf16[8,128,256]{2,1,0:T(8,128)(2,1)} %bitcast.3), calls=%async_computation.2 | async-start | bytes 1048576 | tf_op jit(solution)/shard_map/all_to_all | solution.py:312
  76.9 10.3 %collective-permute-start.7 = (bf16[256,128]{1,0:T(8,128)(2,1)S(1)}, bf16[256,128]{1,0:T(8,128)(2,1)S(1)}, u32[]{:S(2)}, u32[]{:S(2)}) collective-permute-start(bf16[256,128]{1,0:T(8,128)(2,1)S(1)} %get-tuple-element.29.refs_3_), channel_id=1, source_target_pairs={{504,0},{496,504},{488,496},{480,488},{472,480},{464,472},{456,464... | collective-permute-start | bytes 196616 | tf_op jit(solution)/shard_map/ppermute | solution.py:347
  79.3 9.5 %collective-permute-start.6 = (bf16[256,128]{1,0:T(8,128)(2,1)S(1)}, bf16[256,128]{1,0:T(8,128)(2,1)S(1)}, u32[]{:S(2)}, u32[]{:S(2)}) collective-permute-start(bf16[256,128]{1,0:T(8,128)(2,1)S(1)} %get-tuple-element.29.refs_3_), channel_id=1, source_target_pairs={{504,496},{496,488},{488,480},{480,472},{472,464},{464,456},{456,4... | collective-permute-start | bytes 196616 | tf_op jit(solution)/shard_map/ppermute | solution.py:347
  89.4 13.6 %collective-permute-start.9 = (bf16[256,128]{1,0:T(8,128)(2,1)S(1)}, bf16[256,128]{1,0:T(8,128)(2,1)S(1)}, u32[]{:S(2)}, u32[]{:S(2)}) collective-permute-start(bf16[256,128]{1,0:T(8,128)(2,1)S(1)} %three_back.1.refs_5_.refs_3_), channel_id=1, source_target_pairs={{504,16},{496,8},{488,0},{480,504},{472,496},{464,488},{456,480},{... | collective-permute-start | bytes 196616 | tf_op jit(solution)/shard_map/ppermute | solution.py:347
  93.6 9.3 %collective-permute-start.8 = (bf16[256,128]{1,0:T(8,128)(2,1)S(1)}, bf16[256,128]{1,0:T(8,128)(2,1)S(1)}, u32[]{:S(2)}, u32[]{:S(2)}) collective-permute-start(bf16[256,128]{1,0:T(8,128)(2,1)S(1)} %three_back.1.refs_5_.refs_3_), channel_id=1, source_target_pairs={{504,480},{496,472},{488,464},{480,456},{472,448},{464,440},{456,4... | collective-permute-start | bytes 196616 | tf_op jit(solution)/shard_map/ppermute | solution.py:347
  103.6 15.9 %collective-permute-start.11 = (bf16[256,128]{1,0:T(8,128)(2,1)S(1)}, bf16[256,128]{1,0:T(8,128)(2,1)S(1)}, u32[]{:S(2)}, u32[]{:S(2)}) collective-permute-start(bf16[256,128]{1,0:T(8,128)(2,1)S(1)} %nine_back.1.refs_3_), channel_id=1, source_target_pairs={{504,464},{496,456},{488,448},{480,440},{472,432},{464,424},{456,4... | collective-permute-start | bytes 196616 | tf_op jit(solution)/shard_map/ppermute | solution.py:347
  108.9 10.5 %collective-permute-start.10 = (bf16[256,128]{1,0:T(8,128)(2,1)S(1)}, bf16[256,128]{1,0:T(8,128)(2,1)S(1)}, u32[]{:S(2)}, u32[]{:S(2)}) collective-permute-start(bf16[256,128]{1,0:T(8,128)(2,1)S(1)} %nine_back.1.refs_3_), channel_id=1, source_target_pairs={{504,392},{496,384},{488,376},{480,368},{472,360},{464,352},{456,3... | collective-permute-start | bytes 196616 | tf_op jit(solution)/shard_map/ppermute | solution.py:347
